TPU v7x, 512 devices: a whole 4x4x16 slice. The times are simulated.
512 devices in a mesh: grp: 16 (over z), ctx: 32 (over x, y, core).
Axes of the slice: x: 4, y: 4, z: 16, core: 2. Of those that a mesh axis runs over, the one named last changes fastest.
Arguments:
- query_vectors: bfloat16 [131072, 1536], P(('grp', 'ctx')), may hold values from -8 to 8
- key_vectors: bfloat16 [131072, 1536], P(('grp', 'ctx')), may hold values from -8 to 8
- value_vectors: bfloat16 [131072, 1536], P(('grp', 'ctx')), may hold values from -6 to 6
- chosen_groups: int32 [16, 8, 2], replicated, may hold values from -2 to 14, as said below
- chosen_count: int32 [16, 8], replicated, may hold values from 0 to 2, as said below
Outputs:
- attended: bfloat16 [131072, 1536], P(('grp', 'ctx'))
Inputs may be any that keep to these rules, and one draw needn't show every extreme that they name: For j < chosen_count[g, w] the entries chosen_groups[g, w, j] are distinct groups from g - 2 to g - 1, none below 0; later entries carry no meaning. chosen_count[g, w] is at most min(g, 2) and equals 2 for some window of the last group.
All inputs are finite; a program needn't handle non-finite values.
Results may differ from a plain program's by a relative error of at most 0.0041.
Values may be sent and summed in bfloat16 or wider, within the bound.
No kernel may reach another device: no remote copies, remote signals or barrier semaphores. Data moves between devices by JAX's collectives and lax.ppermute only.
A program may use at most 128 MiB of HBM per device.

v0:
```python
import jax
import jax.numpy as jnp
from jax import lax
from jax.sharding import PartitionSpec as P

HEADS = 12
HD = 128
POS = 256
SPAN = 4


NEG_FILL = -1e30


def partner_2(block, axis, apart):
    count = lax.axis_size(axis)
    route = []
    for low in range(count):
        high = low | 1 << apart
        if high != low and high < count:
            route += [(low, high), (high, low)]
    return lax.ppermute(block, axis, route)


def passed_along(value, axis, steps):
    count = lax.axis_size(axis)
    first, last = (max(0, -steps), min(count, count - steps))
    return lax.ppermute(value, axis, [(source, source + steps) for source in range(first, last)])


def tile_partial(query_heads, key_heads, value_heads, causal, frame_count):
    factor = query_heads.shape[-1] ** (-0.5)
    row_count = query_heads.shape[1]
    key_count = key_heads.shape[1]
    block_width = key_count // frame_count
    frame_query = jnp.arange(row_count) // block_width % frame_count
    frame_key = jnp.arange(key_count) // block_width
    visible = frame_query[:, None] >= frame_key[None, :]

    def one_head(operands):
        query_part, key_part, value_part = operands
        scores = (
            jnp.einsum("qd,kd->qk", query_part, key_part, preferred_element_type=jnp.float32)
            * factor
        )
        if causal:
            scores = jnp.where(visible, scores, NEG_FILL)
        highest = jnp.max(scores, axis=-1)
        weights = jnp.exp(scores - highest[:, None])
        summed = jnp.sum(weights, axis=-1)
        blended = jnp.dot(
            weights.astype(jnp.bfloat16), value_part, preferred_element_type=jnp.float32
        )
        return (highest, summed, blended)

    return lax.map(one_head, (query_heads, key_heads, value_heads))


def combine(left_part, right_part):
    ceiling = jnp.maximum(left_part[0], right_part[0])
    left_scale = jnp.exp(left_part[0] - ceiling)
    right_scale = jnp.exp(right_part[0] - ceiling)
    summed = left_part[1] * left_scale + right_part[1] * right_scale
    blended = left_part[2] * left_scale[..., None] + right_part[2] * right_scale[..., None]
    return (ceiling, summed, blended)


def entry_taken(picked, end_slot, source):
    slot_ids = jnp.arange(picked.shape[0], dtype=jnp.int32)
    return jnp.any((picked == source) & (slot_ids < end_slot)) & (source >= 0)


def position_of(entries, wanted_value):
    return [position for position, entry in enumerate(entries) if entry == wanted_value][0]


def gather_window(block, bit_order):
    column = lax.axis_index("ctx")
    stacked = block
    visited = []
    for which_bit in bit_order:
        partner = partner_2(stacked, "ctx", which_bit)
        upper_half = column >> which_bit & 1 == 1
        lower_part = jnp.where(upper_half, partner, stacked)
        upper_part = jnp.where(upper_half, stacked, partner)
        stacked = jnp.stack([lower_part, upper_part])
        visited = [which_bit] + visited
    wanted = sorted(visited, reverse=True)
    arrangement = [position_of(visited, which_bit) for which_bit in wanted] + list(
        range(len(visited), stacked.ndim)
    )
    return jnp.transpose(stacked, arrangement)


def settle(running, bit_order, span_bits):
    column = lax.axis_index("ctx")
    remaining = list(range(span_bits - 1, -1, -1))
    for which_bit in bit_order:
        axis_at = 1 + position_of(remaining, which_bit)
        own_half = column >> which_bit & 1
        kept = jax.tree.map(
            lambda array: lax.dynamic_index_in_dim(array, own_half, axis_at, keepdims=False),
            running,
        )
        sent = jax.tree.map(
            lambda array: lax.dynamic_index_in_dim(array, 1 - own_half, axis_at, keepdims=False),
            running,
        )
        partner = partner_2(sent, "ctx", which_bit)
        running = combine(kept, partner)
        remaining = [entry for entry in remaining if entry != which_bit]
    return running


def body(query_vectors, key_vectors, value_vectors, chosen_groups, chosen_count):
    column_devices = lax.axis_size("ctx")
    group_devices = lax.axis_size("grp")
    group_id = lax.axis_index("grp")
    window_id = lax.axis_index("ctx") // SPAN
    token_rows, channels = query_vectors.shape
    device_frames = token_rows // POS
    block_width = POS // column_devices
    frame_total = device_frames * column_devices
    lookback = min(2, group_devices - 1)
    span_bits = SPAN.bit_length() - 1
    bit_order = list(range(span_bits))

    def source_layout(matrix):
        return matrix.reshape(device_frames, column_devices, block_width, channels)

    query_window, key_window, value_window = (
        lax.all_to_all(
            source_layout(query_vectors), "ctx", split_axis=1, concat_axis=0, tiled=True
        ),
        lax.all_to_all(source_layout(key_vectors), "ctx", split_axis=1, concat_axis=0, tiled=True),
        lax.all_to_all(
            source_layout(value_vectors), "ctx", split_axis=1, concat_axis=0, tiled=True
        ),
    )

    def head_layout(matrix):
        return jnp.transpose(matrix.reshape(-1, HEADS, HD), (1, 0, 2))

    key_heads = head_layout(key_window)
    value_heads = head_layout(value_window)
    gathered = gather_window(query_window.reshape(frame_total, block_width, channels), bit_order)
    query_heads = head_layout(gathered)
    own_picked = lax.dynamic_index_in_dim(
        lax.dynamic_index_in_dim(chosen_groups, group_id, 0, keepdims=False),
        window_id,
        0,
        keepdims=False,
    )
    own_count = lax.dynamic_index_in_dim(
        lax.dynamic_index_in_dim(chosen_count, group_id, 0, keepdims=False),
        window_id,
        0,
        keepdims=False,
    )
    running = tile_partial(query_heads, key_heads, value_heads, True, frame_total)
    current_pair = (key_heads, value_heads)
    for distance in range(1, lookback + 1):
        current_pair = passed_along((current_pair[0], current_pair[1]), "grp", 1)
        source = group_id - distance

        def absorb_own(current, key_value=current_pair):
            return combine(
                current, tile_partial(query_heads, key_value[0], key_value[1], False, frame_total)
            )

        running = lax.cond(
            entry_taken(own_picked, own_count, source), absorb_own, lambda current: current, running
        )
    split_shape = (HEADS,) + (2,) * span_bits + (-1,)
    running = (
        running[0].reshape(split_shape),
        running[1].reshape(split_shape),
        running[2].reshape(split_shape + (HD,)),
    )
    running = settle(running, bit_order, span_bits)
    finished = running[2] / running[1][..., None]
    attended = jnp.transpose(finished, (1, 0, 2)).astype(jnp.bfloat16)
    attended = attended.reshape(frame_total, 1, block_width, channels)
    restored = lax.all_to_all(attended, "ctx", split_axis=0, concat_axis=1, tiled=True)
    return restored.reshape(token_rows, channels)


def solution(mesh):
    in_specs = (P(("grp", "ctx"), None), P(("grp", "ctx"), None), P(("grp", "ctx"), None), P(), P())
    out_specs = P(("grp", "ctx"), None)
    return jax.shard_map(body, mesh=mesh, in_specs=in_specs, out_specs=out_specs, check_vma=False)
```

profile of v0, /device:TPU:97, one launch (start us, length us, event | category | flops | bytes accessed | tf_op | source)
XLA Modules:
  0.0 358.7 jit_solution(10786476154508077978)
XLA Ops:
  0.0 22.0 %all_to_all.16 = bf16[1,32,8,1536]{3,2,0,1:T(8,128)(2,1)S(1)} all-to-all(bf16[1,32,8,1536]{3,2,0,1:T(8,128)(2,1)} %bitcast.193), channel_id=1, replica_groups=mesh['grp'=16,'ctx'=32] {'ctx'}, dimensions={1} | all-to-all | bytes 1572864 | tf_op jit(solution)/shard_map/all_to_all | solution.py:132
  22.0 1.9 collective-permute-start
  23.9 4.1 %all-to-all-start.1 = ((bf16[1,32,8,1536]{3,2,0,1:T(8,128)(2,1)}), bf16[1,32,8,1536]{3,2,0,1:T(8,128)(2,1)S(1)}, u32[]{:S(2)}, u32[]{:S(2)}) async-start(bf16[1,32,8,1536]{3,2,0,1:T(8,128)(2,1)} %bitcast.194), calls=%async_computation.1 | async-start | bytes 1572864 | tf_op jit(solution)/shard_map/all_to_all | solution.py:135
  28.0 1.2 select_bitcast_fusion.3
  29.2 1.3 pad_maximum_fusion.1
  30.5 3.3 collective-permute-start.1
  33.8 8.5 %all-to-all-done.1 = bf16[1,32,8,1536]{3,2,0,1:T(8,128)(2,1)S(1)} async-done(((bf16[1,32,8,1536]{3,2,0,1:T(8,128)(2,1)}), bf16[1,32,8,1536]{3,2,0,1:T(8,128)(2,1)S(1)}, u32[]{:S(2)}, u32[]{:S(2)}) %all-to-all-start.1) | async-done | bytes 786464 | tf_op jit(solution)/shard_map/all_to_all | solution.py:135
  42.3 4.4 %all-to-all-start.2 = ((bf16[1,32,8,1536]{3,2,0,1:T(8,128)(2,1)}), bf16[1,32,8,1536]{3,2,0,1:T(8,128)(2,1)}, u32[]{:S(2)}, u32[]{:S(2)}) async-start(bf16[1,32,8,1536]{3,2,0,1:T(8,128)(2,1)} %bitcast.195), calls=%async_computation.2 | async-start | bytes 1572864 | tf_op jit(solution)/shard_map/all_to_all | solution.py:136
  48.4 4.8 %collective-permute-start.2 = (bf16[12,256,128]{2,1,0:T(8,128)(2,1)}, bf16[12,256,128]{2,1,0:T(8,128)(2,1)}, u32[]{:S(2)}, u32[]{:S(2)}) collective-permute-start(bf16[12,256,128]{2,1,0:T(8,128)(2,1)} %copy.27), channel_id=1, source_target_pairs={{0,32},{32,64},{64,96},{96,128},{128,160},{160,192},{192,224},{224... | collective-permute-start | bytes 2359304 | tf_op jit(solution)/shard_map/ppermute | solution.py:28
  53.1 29.9 %all-to-all-done.2 = bf16[1,32,8,1536]{3,2,0,1:T(8,128)(2,1)} async-done(((bf16[1,32,8,1536]{3,2,0,1:T(8,128)(2,1)}), bf16[1,32,8,1536]{3,2,0,1:T(8,128)(2,1)}, u32[]{:S(2)}, u32[]{:S(2)}) %all-to-all-start.2) | async-done | bytes 786464 | tf_op jit(solution)/shard_map/all_to_all | solution.py:136
  83.1 1.6 reshape.133
  84.9 4.8 %collective-permute-start.3 = (bf16[12,256,128]{2,1,0:T(8,128)(2,1)S(1)}, bf16[12,256,128]{2,1,0:T(8,128)(2,1)}, u32[]{:S(2)}, u32[]{:S(2)}) collective-permute-start(bf16[12,256,128]{2,1,0:T(8,128)(2,1)S(1)} %copy.28), channel_id=1, source_target_pairs={{0,32},{32,64},{64,96},{96,128},{128,160},{160,192},{192,224},{224... | collective-permute-start | bytes 2359304 | tf_op jit(solution)/shard_map/ppermute | solution.py:28
  89.8 1.3 dynamic_slice.82
  91.9 1.3 and_reduce_fusion
  94.5 3.5 collective-permute-start.4
  98.0 8.2 %collective-permute-done.3 = bf16[12,256,128]{2,1,0:T(8,128)(2,1)} collective-permute-done((bf16[12,256,128]{2,1,0:T(8,128)(2,1)S(1)}, bf16[12,256,128]{2,1,0:T(8,128)(2,1)}, u32[]{:S(2)}, u32[]{:S(2)}) %collective-permute-start.3) | collective-permute-done | bytes 786464 | tf_op jit(solution)/shard_map/ppermute | solution.py:28
  106.2 5.4 %collective-permute-start.5 = (bf16[12,256,128]{2,1,0:T(8,128)(2,1)}, bf16[12,256,128]{2,1,0:T(8,128)(2,1)}, u32[]{:S(2)}, u32[]{:S(2)}) collective-permute-start(bf16[12,256,128]{2,1,0:T(8,128)(2,1)} %collective-permute-done.3), channel_id=1, source_target_pairs={{0,32},{32,64},{64,96},{96,128},{128,160},{160,192},{192,224},{224... | collective-permute-start | bytes 2359304 | tf_op jit(solution)/shard_map/ppermute | solution.py:28
  111.6 1.6 select_bitcast_fusion.1
  113.6 3.7 %reshape.129 = bf16[1024,12,128]{2,1,0:T(8,128)(2,1)} reshape(bf16[2,2,32,8,1536]{4,3,2,1,0:T(8,128)(2,1)S(1)} %pad_maximum_fusion) | data formatting | bytes 6291456 | tf_op jit(solution)/shard_map/reshape | solution.py:142
  117.3 3.0 copy.26
  120.3 43.1 %while.43 = (s32[]{:T(128)}, f32[12,1024]{1,0:T(8,128)S(1)}, f32[12,1024]{1,0:T(8,128)S(1)}, f32[12,1024,128]{2,1,0:T(8,128)}, bf16[12,1024,128]{2,1,0:T(8,128)(...) while((s32[]{:T(128)}, f32[12,1024]{1,0:T(8,128)S(1)}, ...), condition=%wide.region_5.6_spmd.clone, body=%wide.region_2.5_spmd.clone.sunk | while | flops 136312832 | bytes 4103285 | solution.py:56
  121.4 2.0 fusion.81
  125.0 2.0 fusion.81
  128.6 2.0 fusion.81
  131.0 1.2 fusion.79
  132.2 2.0 fusion.81
  135.8 2.0 fusion.81
  138.2 1.2 fusion.79
  139.4 2.0 fusion.81
  143.0 2.0 fusion.81
  146.6 2.0 fusion.81
  150.1 2.0 fusion.81
  153.7 2.0 fusion.81
  157.3 2.0 fusion.81
  161.0 2.0 fusion.81
  163.4 55.9 %conditional.2 = ((f32[12,1024]{1,0:T(8,128)S(1)}, f32[12,1024]{1,0:T(8,128)S(1)}, f32[12,1024,128]{2,1,0:T(8,128)})) conditional(s32[]{:T(128)} %convert_element_type.22, (f32[12,1024]{1,0:T(8,128)S(1)}, f32[12,1024]{1,0:T(8,128)S(1)}, f32[12,1024,128]{2,1,0:T(8,128)}) %tuple.49, (bf16[12,1024,128]{2,0,1:T(8,128)(2,1)}, ...), branch_computations={%region_6.7_spmd, %region_7.12_spmd} | conditional | flops 140580864 | bytes 29755604 | solution.py:171
  163.4 3.0 copy.31
  166.4 43.1 %while.41 = (s32[]{:T(128)}, f32[12,1024]{1,0:T(8,128)S(1)}, f32[12,1024]{1,0:T(8,128)S(1)}, f32[12,1024,128]{2,1,0:T(8,128)}, bf16[12,1024,128]{2,1,0:T(8,128)(...) while((s32[]{:T(128)}, f32[12,1024]{1,0:T(8,128)S(1)}, ...), condition=%wide.region_11.11_spmd, body=%wide.region_8.10_spmd.sunk | while | flops 135788544 | bytes 4098149 | solution.py:56
  167.6 2.0 fusion.91
  171.2 2.0 fusion.91
  174.8 2.0 fusion.91
  178.3 2.1 fusion.91
  182.0 2.0 fusion.91
  185.6 2.1 fusion.91
  189.2 2.0 fusion.91
  192.8 2.0 fusion.91
  196.4 2.0 fusion.91
  199.9 2.0 fusion.91
  203.5 2.0 fusion.91
  207.1 2.0 fusion.91
  209.6 9.7 %multiply_add_fusion = f32[12,1024,128]{2,1,0:T(8,128)} fusion(f32[12,1024,128]{2,1,0:T(8,128)} %get-tuple-element.172, f32[12,1024,128]{2,1,0:T(8,128)} %get-tuple-element.171, f32[12,1024]{1,0:T(8,128)S(1)} %get-tuple-element.331, f32[12,1024]{1,0:T(8,128)S(1)} %get-tuple-element.330), kind=kLoop, calls=%fused_computation.16 | loop fusion | flops 4718592 | bytes 18972672 | tf_op jit(solution)/shard_map/cond/branch_1_fun/add | solution.py:64
  219.5 3.3 constant_dynamic-slice_fusion.2
  222.8 1.9 copy.56
  224.6 4.2 %collective-permute-start.7 = (f32[12,2,256,128]{3,2,0,1:T(8,128)}, f32[12,2,256,128]{3,2,0,1:T(8,128)}, u32[]{:S(2)}, u32[]{:S(2)}) collective-permute-start(f32[12,2,256,128]{3,2,0,1:T(8,128)} %bitcast.141), channel_id=1, source_target_pairs={{0,1},{1,0},{2,3},{3,2},{4,5},{5,4},{6,7},{7,6},{8,9},{9,8},{10,11... | collective-permute-start | bytes 9437192 | tf_op jit(solution)/shard_map/ppermute | solution.py:22
  229.0 1.9 collective-permute-start.6
  231.0 2.4 collective-permute-start.10
  234.5 3.8 %fusion.42 = f32[12,2,256,128]{3,2,0,1:T(8,128)S(1)} fusion(f32[12,2,1,256,128]{4,3,2,1,0:T(8,128)S(1)} %get-tuple-element.350, f32[12,2,256,128]{3,2,0,1:T(8,128)} %collective-permute-done.7, f32[12,2,256]{2,0,1:T(8,128)S(1)} %get-tuple-element.341, f32[12,2,256]{2,0,1:T(8,128)S(1)} %get-tuple-element.342), kind=kLoop, calls=%fused_computation.57 | loop fusion | flops 2359296 | bytes 9486336 | tf_op jit(solution)/shard_map/add | solution.py:64
  238.3 1.6 copy-done
  240.0 2.0 collective-permute-start.9
  242.1 3.3 collective-permute-start.8
  245.4 2.0 collective-permute-start.11
  247.4 30.5 %collective-permute-done.8 = f32[12,256]{1,0:T(8,128)S(1)} collective-permute-done((f32[12,256]{1,0:T(8,128)S(1)}, f32[12,256]{1,0:T(8,128)S(1)}, u32[]{:S(2)}, u32[]{:S(2)}) %collective-permute-start.8) | collective-permute-done | bytes 12320 | tf_op jit(solution)/shard_map/ppermute | solution.py:22
  278.3 3.1 fusion.46
  282.4 75.4 %all_to_all.17 = bf16[32,1,8,1536]{3,2,1,0:T(8,128)(2,1)S(1)} all-to-all(bf16[32,1,8,1536]{3,2,1,0:T(8,128)(2,1)S(1)} %bitcast.187), channel_id=1, replica_groups=mesh['grp'=16,'ctx'=32] {'ctx'}, dimensions={0} | all-to-all | bytes 1572864 | tf_op jit(solution)/shard_map/all_to_all | solution.py:184
  (136 shorter events, 41.6 us)
Async XLA Ops:
  22.0 6.0 %collective-permute-start = (bf16[32,8,1536]{2,1,0:T(8,128)(2,1)S(1)}, bf16[32,8,1536]{2,1,0:T(8,128)(2,1)}, u32[]{:S(2)}, u32[]{:S(2)}) collective-permute-start(bf16[32,8,1536]{2,1,0:T(8,128)(2,1)S(1)} %bitcast.189), channel_id=1, source_target_pairs={{0,1},{1,0},{2,3},{3,2},{4,5},{5,4},{6,7},{7,6},{8,9},{9,8},{10,11... | collective-permute-start | bytes 2359304 | tf_op jit(solution)/shard_map/ppermute | solution.py:22
  23.9 18.4 %all-to-all-start.1 = ((bf16[1,32,8,1536]{3,2,0,1:T(8,128)(2,1)}), bf16[1,32,8,1536]{3,2,0,1:T(8,128)(2,1)S(1)}, u32[]{:S(2)}, u32[]{:S(2)}) async-start(bf16[1,32,8,1536]{3,2,0,1:T(8,128)(2,1)} %bitcast.194), calls=%async_computation.1 | async-start | bytes 1572864 | tf_op jit(solution)/shard_map/all_to_all | solution.py:135
  30.5 81.1 %collective-permute-start.1 = (bf16[2,32,8,1536]{3,2,1,0:T(8,128)(2,1)}, bf16[2,32,8,1536]{3,2,1,0:T(8,128)(2,1)}, u32[]{:S(2)}, u32[]{:S(2)}) collective-permute-start(bf16[2,32,8,1536]{3,2,1,0:T(8,128)(2,1)} %pad_maximum_fusion.1), channel_id=1, source_target_pairs={{0,2},{2,0},{1,3},{3,1},{4,6},{6,4},{5,7},{7,5},{8,10},{10,8},{9,1... | collective-permute-start | bytes 4718600 | tf_op jit(solution)/shard_map/ppermute | solution.py:22
  42.3 40.8 %all-to-all-start.2 = ((bf16[1,32,8,1536]{3,2,0,1:T(8,128)(2,1)}), bf16[1,32,8,1536]{3,2,0,1:T(8,128)(2,1)}, u32[]{:S(2)}, u32[]{:S(2)}) async-start(bf16[1,32,8,1536]{3,2,0,1:T(8,128)(2,1)} %bitcast.195), calls=%async_computation.2 | async-start | bytes 1572864 | tf_op jit(solution)/shard_map/all_to_all | solution.py:136
  48.4 46.1 %collective-permute-start.2 = (bf16[12,256,128]{2,1,0:T(8,128)(2,1)}, bf16[12,256,128]{2,1,0:T(8,128)(2,1)}, u32[]{:S(2)}, u32[]{:S(2)}) collective-permute-start(bf16[12,256,128]{2,1,0:T(8,128)(2,1)} %copy.27), channel_id=1, source_target_pairs={{0,32},{32,64},{64,96},{96,128},{128,160},{160,192},{192,224},{224... | collective-permute-start | bytes 2359304 | tf_op jit(solution)/shard_map/ppermute | solution.py:28
  84.9 28.3 %copy-start.1 = (bf16[12,256,128]{2,1,0:T(8,128)(2,1)}, bf16[12,256,128]{2,1,0:T(8,128)(2,1)S(1)}, u32[]{:S(2)}) copy-start(bf16[12,256,128]{2,1,0:T(8,128)(2,1)S(1)} %copy.28) | copy-start | bytes 2359300
  84.9 21.3 %collective-permute-start.3 = (bf16[12,256,128]{2,1,0:T(8,128)(2,1)S(1)}, bf16[12,256,128]{2,1,0:T(8,128)(2,1)}, u32[]{:S(2)}, u32[]{:S(2)}) collective-permute-start(bf16[12,256,128]{2,1,0:T(8,128)(2,1)S(1)} %copy.28), channel_id=1, source_target_pairs={{0,32},{32,64},{64,96},{96,128},{128,160},{160,192},{192,224},{224... | collective-permute-start | bytes 2359304 | tf_op jit(solution)/shard_map/ppermute | solution.py:28
  94.5 124.8 %collective-permute-start.4 = (bf16[12,256,128]{2,1,0:T(8,128)(2,1)}, bf16[12,256,128]{2,1,0:T(8,128)(2,1)}, u32[]{:S(2)}, u32[]{:S(2)}) collective-permute-start(bf16[12,256,128]{2,1,0:T(8,128)(2,1)} %collective-permute-done.2), channel_id=1, source_target_pairs={{0,32},{32,64},{64,96},{96,128},{128,160},{160,192},{192,224},{224... | collective-permute-start | bytes 2359304 | tf_op jit(solution)/shard_map/ppermute | solution.py:28
  106.2 113.1 %collective-permute-start.5 = (bf16[12,256,128]{2,1,0:T(8,128)(2,1)}, bf16[12,256,128]{2,1,0:T(8,128)(2,1)}, u32[]{:S(2)}, u32[]{:S(2)}) collective-permute-start(bf16[12,256,128]{2,1,0:T(8,128)(2,1)} %collective-permute-done.3), channel_id=1, source_target_pairs={{0,32},{32,64},{64,96},{96,128},{128,160},{160,192},{192,224},{224... | collective-permute-start | bytes 2359304 | tf_op jit(solution)/shard_map/ppermute | solution.py:28
  224.6 9.9 %collective-permute-start.7 = (f32[12,2,256,128]{3,2,0,1:T(8,128)}, f32[12,2,256,128]{3,2,0,1:T(8,128)}, u32[]{:S(2)}, u32[]{:S(2)}) collective-permute-start(f32[12,2,256,128]{3,2,0,1:T(8,128)} %bitcast.141), channel_id=1, source_target_pairs={{0,1},{1,0},{2,3},{3,2},{4,5},{5,4},{6,7},{7,6},{8,9},{9,8},{10,11... | collective-permute-start | bytes 9437192 | tf_op jit(solution)/shard_map/ppermute | solution.py:22
  229.0 5.2 %collective-permute-start.6 = (f32[12,2,256]{2,0,1:T(8,128)S(1)}, f32[12,2,256]{2,0,1:T(8,128)S(1)}, u32[]{:S(2)}, u32[]{:S(2)}) collective-permute-start(f32[12,2,256]{2,0,1:T(8,128)S(1)} %bitcast.199), channel_id=1, source_target_pairs={{0,1},{1,0},{2,3},{3,2},{4,5},{5,4},{6,7},{7,6},{8,9},{9,8},{10,11... | collective-permute-start | bytes 73736 | tf_op jit(solution)/shard_map/ppermute | solution.py:22
  231.0 3.3 collective-permute-start.10
  238.3 1.6 copy-start
  240.0 38.2 %collective-permute-start.9 = (f32[12,256,128]{2,1,0:T(8,128)S(1)}, f32[12,256,128]{2,1,0:T(8,128)S(1)}, u32[]{:S(2)}, u32[]{:S(2)}) collective-permute-start(f32[12,256,128]{2,1,0:T(8,128)S(1)} %dynamic-slice_bitcast_fusion), channel_id=1, source_target_pairs={{0,2},{2,0},{1,3},{3,1},{4,6},{6,4},{5,7},{7,5},{8,10},{10,8},{9,1... | collective-permute-start | bytes 4718600 | tf_op jit(solution)/shard_map/ppermute | solution.py:22
  242.1 35.8 %collective-permute-start.8 = (f32[12,256]{1,0:T(8,128)S(1)}, f32[12,256]{1,0:T(8,128)S(1)}, u32[]{:S(2)}, u32[]{:S(2)}) collective-permute-start(f32[12,256]{1,0:T(8,128)S(1)} %dynamic-slice_bitcast_fusion.2), channel_id=1, source_target_pairs={{0,2},{2,0},{1,3},{3,1},{4,6},{6,4},{5,7},{7,5},{8,10},{10,8},{9,1... | collective-permute-start | bytes 36872 | tf_op jit(solution)/shard_map/ppermute | solution.py:22
  245.4 32.9 %collective-permute-start.11 = (f32[12,256]{1,0:T(8,128)S(1)}, f32[12,256]{1,0:T(8,128)S(1)}, u32[]{:S(2)}, u32[]{:S(2)}) collective-permute-start(f32[12,256]{1,0:T(8,128)S(1)} %dynamic-slice_bitcast_fusion.1), channel_id=1, source_target_pairs={{0,2},{2,0},{1,3},{3,1},{4,6},{6,4},{5,7},{7,5},{8,10},{10,8},{9,1... | collective-permute-start | bytes 36872 | tf_op jit(solution)/shard_map/ppermute | solution.py:22
where the time goes:
time: 364 us; the launch traced here: 359 us
  blocking collectives  97.4 us (27%)
  waiting for transfers between devices  78.5 us (22%)
  matrix products  76 us (21%)
  starting transfers between devices  48 us (13%)
  local copies, waits for them, and re-layouts  28.6 us (8%)
  other arithmetic  27.4 us (8%)
    all_to_all x1, blocking collectives, body(): lax.all_to_all(attended, 'ctx', split_axis=0, concat_axis=1, tiled=True)  75.4 us
    dot_general x24, matrix products, one_head(): jnp.dot(weights.astype(jnp.bfloat16), value_part, preferred_element_type=...  48.3 us
    ppermute x8, waiting for transfers between devices, partner_2(): return lax.ppermute(block, axis, route)  31.9 us
    all_to_all x1, waiting for transfers between devices, body(): lax.all_to_all(source_layout(value_vectors), 'ctx', split_axis=1, concat_...  29.9 us
    dot_general x24, matrix products, one_head(): jnp.einsum('qd,kd->qk', query_part, key_part, preferred_element_type=jnp....  27.7 us
    all_to_all x1, blocking collectives, body(): lax.all_to_all(source_layout(query_vectors), 'ctx', split_axis=1, concat_...  22 us
    ppermute x8, starting transfers between devices, partner_2(): return lax.ppermute(block, axis, route)  21 us
    ppermute x4, starting transfers between devices, passed_along(): lax.ppermute(value, axis, [(source, source + steps) for source in range(f...  18.5 us
  transfers between devices with their start and end apart: 14, of which 8 were waited for; matrix products, arithmetic and copies ran while one was open for 32% of the time, Pallas kernels for 0%

commit v1 on v0

v1 whole, which is shorter than its diff:
```python
import functools
import math

import jax
import jax.numpy as jnp
from jax import lax
from jax.experimental import pallas as pl
from jax.experimental.pallas import tpu as pltpu
from jax.sharding import PartitionSpec as P

HEADS = 12
HD = 128
POS = 256
SPAN = 4
NWIN = 8
LOOK = 2
QB = 256
PARTS = HEADS // SPAN
POSITIONS = POS // NWIN
STAT_ROWS = 32
LOG2E = math.log2(math.e)
FACTOR = HD**-0.5 * LOG2E
NEG_FILL = -1e30
SMEM = pl.BlockSpec(memory_space=pltpu.SMEM)
VMEM = pl.BlockSpec(memory_space=pltpu.VMEM)
ANY = pl.BlockSpec(memory_space=pl.ANY)
PARAMS = pltpu.CompilerParams(vmem_limit_bytes=32 * 2**20)


def is_taken(groups_ref, count_ref, group, distance):
    groups = groups_ref.shape[0]
    window = lax.axis_index("ctx") // SPAN
    held = jnp.minimum(group, groups - 1)
    source = group - distance
    count = count_ref[held, window]
    taken = jnp.bool_(False)
    for slot in range(LOOK):
        taken = taken | ((groups_ref[held, window, slot] == source) & (slot < count))
    return taken & (source >= 0) & (group < groups)


def softmax_part(query, keys, values, diagonal):
    scores = lax.dot_general(
        query, keys, (((1,), (1,)), ((), ())), preferred_element_type=jnp.float32
    )
    if diagonal:
        rows, count = scores.shape
        tail = scores[:, count - rows :]
        frame_query = lax.broadcasted_iota(jnp.int32, (rows, rows), 0) // POSITIONS
        frame_key = lax.broadcasted_iota(jnp.int32, (rows, rows), 1) // POSITIONS
        tail = jnp.where(frame_query >= frame_key, tail, NEG_FILL)
        scores = jnp.concatenate([scores[:, : count - rows], tail], axis=1) if count > rows else tail
    highest = jnp.max(scores, axis=-1, keepdims=True)
    weights = jnp.exp2((scores - highest) * FACTOR)
    summed = jnp.sum(weights, axis=-1, keepdims=True)
    blended = jnp.dot(weights.astype(jnp.bfloat16), values, preferred_element_type=jnp.float32)
    return highest, summed, blended


def join(old, new):
    ceiling = jnp.maximum(old[0], new[0])
    old_scale = jnp.exp2((old[0] - ceiling) * FACTOR)
    new_scale = jnp.exp2((new[0] - ceiling) * FACTOR)
    return (
        ceiling,
        old[1] * old_scale + new[1] * new_scale,
        old[2] * old_scale + new[2] * new_scale,
    )


def rows_of(ref, slab, start, size):
    first, count = start // POSITIONS, size // POSITIONS
    return ref[pl.ds(first, count), slab].reshape(size, HD)


def eye_mask():
    return lax.broadcasted_iota(jnp.int32, (HD, HD), 0) == lax.broadcasted_iota(
        jnp.int32, (HD, HD), 1
    )


def log_rows(part):
    log_sum = part[0] * FACTOR + jnp.log(part[1]) * LOG2E
    return [
        jnp.sum(jnp.where(eye_mask(), log_sum[at : at + HD], 0.0), axis=0, keepdims=True)
        for at in range(0, log_sum.shape[0], HD)
    ]


def ahead_kernel(groups_ref, count_ref, q_ref, kv_ref, out_ref):
    rows = q_ref.shape[0] * POSITIONS
    taken = is_taken(groups_ref, count_ref, lax.axis_index("grp") + 1, 2)

    @pl.when(taken)
    def _():
        for head in range(q_ref.shape[1]):
            keys = rows_of(kv_ref, 2 * head, 0, rows)
            values = rows_of(kv_ref, 2 * head + 1, 0, rows)
            logs = []
            for start in range(0, rows, QB):
                query = rows_of(q_ref, head, start, QB)
                part = softmax_part(query, keys, values, False)
                out_ref[head, pl.ds(start, QB), :] = (part[2] / part[1]).astype(jnp.bfloat16)
                logs += log_rows(part)
            left = jnp.concatenate(logs, axis=0)
            pieces = []
            for _ in range(3):
                pieces.append(left.astype(jnp.bfloat16).astype(jnp.float32))
                left = left - pieces[-1]
            pieces.append(jnp.zeros((STAT_ROWS - 3 * len(logs), HD), jnp.float32))
            packed = jnp.concatenate(pieces, axis=0).astype(jnp.bfloat16)
            out_ref[head, pl.ds(rows, STAT_ROWS), :] = packed

    @pl.when(jnp.logical_not(taken))
    def _():
        out_ref[...] = jnp.zeros_like(out_ref)


def near_kernel(
    groups_ref, count_ref, first_ref, second_ref, first_up_ref, second_up_ref, out_ref, log_ref
):
    rows = first_ref.shape[0] * POSITIONS
    taken = is_taken(groups_ref, count_ref, lax.axis_index("grp"), 1)

    def pair_of(first, second, head, size):
        ref, slab = (first, 2 * head) if head < 2 else (second, 0)
        return rows_of(ref, slab, 0, size), rows_of(ref, slab + 1, 0, size)

    def put(head, start, part):
        out_ref[head, pl.ds(start, QB), :] = part[2] / part[1]
        for at, row in enumerate(log_rows(part)):
            log_ref[head, pl.ds(start // HD + at, 1), :] = row

    def own(head, start):
        query = rows_of(second_ref, 2 + head, start, QB)
        return softmax_part(query, *pair_of(first_ref, second_ref, head, start + QB), True)

    @pl.when(taken)
    def _():
        for head in range(PARTS):
            for start in range(0, rows, QB):
                query = rows_of(second_ref, 2 + head, start, QB)
                earlier = softmax_part(
                    query, *pair_of(first_up_ref, second_up_ref, head, rows), False
                )
                put(head, start, join(own(head, start), earlier))

    @pl.when(jnp.logical_not(taken))
    def _():
        for head in range(PARTS):
            for start in range(0, rows, QB):
                put(head, start, own(head, start))


def merge_kernel(
    groups_ref, count_ref, near_ref, log_ref, first_far_ref, second_far_ref, out_ref
):
    rows = near_ref.shape[1]
    blocks = rows // HD
    taken = is_taken(groups_ref, count_ref, lax.axis_index("grp"), 2)

    def put(head, start, value):
        out_ref[pl.ds(start // POSITIONS, HD // POSITIONS), head] = value.astype(
            jnp.bfloat16
        ).reshape(HD // POSITIONS, POSITIONS, HD)

    @pl.when(taken)
    def _():
        for head in range(PARTS):
            far_ref = first_far_ref.at[head] if head < 2 else second_far_ref.at[0]
            pieces = far_ref[pl.ds(rows, STAT_ROWS), :].astype(jnp.float32)
            far_log = pieces[:blocks] + pieces[blocks : 2 * blocks] + pieces[2 * blocks : 3 * blocks]
            shares = 1.0 / (1.0 + jnp.exp2(log_ref[head] - far_log))
            for block in range(blocks):
                share = jnp.sum(
                    jnp.where(eye_mask(), shares[block : block + 1], 0.0), axis=1, keepdims=True
                )
                part = pl.ds(block * HD, HD)
                near = near_ref[head, part, :]
                far = far_ref[part, :].astype(jnp.float32)
                put(head, block * HD, near + (far - near) * share)

    @pl.when(jnp.logical_not(taken))
    def _():
        for head in range(PARTS):
            for start in range(0, rows, HD):
                put(head, start, near_ref[head, pl.ds(start, HD), :])


def cost(passes, rows, heads, moved):
    return pl.CostEstimate(
        flops=int(4 * passes * rows * rows * heads * HD),
        bytes_accessed=moved,
        transcendentals=int(passes * rows * rows * heads),
    )


def attend_ahead(groups, count, query, pair):
    rows, heads = query.shape[0] * POSITIONS, query.shape[1]
    return pl.pallas_call(
        ahead_kernel,
        in_specs=[SMEM] * 2 + [VMEM] * 2,
        out_specs=VMEM,
        out_shape=jax.ShapeDtypeStruct((heads, rows + STAT_ROWS, HD), jnp.bfloat16),
        compiler_params=PARAMS,
        cost_estimate=cost(1, rows, heads, rows * heads * HD * 8),
        name="ahead",
    )(groups, count, query, pair)


def attend_near(groups, count, first, second, first_up, second_up):
    rows = first.shape[0] * POSITIONS
    return pl.pallas_call(
        near_kernel,
        in_specs=[SMEM] * 2 + [VMEM] * 4,
        out_specs=[VMEM] * 2,
        out_shape=[
            jax.ShapeDtypeStruct((PARTS, rows, HD), jnp.float32),
            jax.ShapeDtypeStruct((PARTS, rows // HD, HD), jnp.float32),
        ],
        compiler_params=PARAMS,
        cost_estimate=cost(1.6, rows, PARTS, rows * PARTS * HD * 14),
        name="near",
    )(groups, count, first, second, first_up, second_up)


def merge(groups, count, near, logs, first_far, second_far):
    frames = near.shape[1] // POSITIONS
    return pl.pallas_call(
        merge_kernel,
        in_specs=[SMEM] * 2 + [VMEM] * 4,
        out_specs=VMEM,
        out_shape=jax.ShapeDtypeStruct((frames, PARTS, POSITIONS, HD), jnp.bfloat16),
        compiler_params=PARAMS,
        cost_estimate=cost(0, frames * POSITIONS, PARTS, frames * POSITIONS * PARTS * HD * 8),
        name="merge",
    )(groups, count, near, logs, first_far, second_far)


def cut_kernel(slabs, *refs):
    sources, out_ref = refs[:-1], refs[-1]
    for window in range(NWIN):
        rows = pl.ds(window * POSITIONS, POSITIONS)
        for part in range(SPAN):
            for slab, (source, head) in enumerate(slabs):
                lanes = pl.ds((part * PARTS + head) * HD, HD)
                out_ref[window * SPAN + part, slab] = sources[source][rows, lanes]


def cut(sources, slabs):
    return pl.pallas_call(
        functools.partial(cut_kernel, slabs),
        in_specs=[VMEM] * len(sources),
        out_specs=VMEM,
        out_shape=jax.ShapeDtypeStruct((NWIN * SPAN, len(slabs), POSITIONS, HD), jnp.bfloat16),
        compiler_params=PARAMS,
        name="cut",
    )(*sources)


def paste_kernel(in_ref, out_ref, held_ref, sems):
    copies = []
    for window in range(NWIN):
        rows = pl.ds(window * POSITIONS, POSITIONS)
        for part in range(SPAN):
            for head in range(PARTS):
                lanes = pl.ds((part * PARTS + head) * HD, HD)
                held_ref[rows, lanes] = in_ref[window * SPAN + part, head]
        copies.append(
            pltpu.make_async_copy(held_ref.at[rows], out_ref.at[rows], sems.at[window])
        )
        copies[-1].start()
    for copy in copies:
        copy.wait()


def paste(pieces):
    return pl.pallas_call(
        paste_kernel,
        in_specs=[VMEM],
        out_specs=ANY,
        out_shape=jax.ShapeDtypeStruct((POS, HEADS * HD), jnp.bfloat16),
        scratch_shapes=[
            pltpu.VMEM((POS, HEADS * HD), jnp.bfloat16),
            pltpu.SemaphoreType.DMA((NWIN,)),
        ],
        compiler_params=PARAMS,
        name="paste",
    )(pieces)


def body(query_vectors, key_vectors, value_vectors, chosen_groups, chosen_count):
    group_devices = lax.axis_size("grp")

    def to_peers(block):
        return lax.all_to_all(block, "ctx", split_axis=0, concat_axis=0, tiled=True)

    def up(block):
        return lax.ppermute(block, "grp", [(at, at + 1) for at in range(group_devices - 1)])

    def down(block):
        return lax.ppermute(block, "grp", [(at + 1, at) for at in range(group_devices - 1)])

    first = to_peers(cut((key_vectors, value_vectors), ((0, 0), (1, 0), (0, 1), (1, 1))))
    second = cut(
        (key_vectors, value_vectors, query_vectors), ((0, 2), (1, 2), (2, 0), (2, 1), (2, 2))
    )
    first, second = lax.optimization_barrier((first, second))
    first_up = up(first)
    second = to_peers(second)
    first_query = down(second[:, 2:4])
    second_up = up(second[:, 0:2])
    second_query = down(second[:, 4:5])
    first_far = up(attend_ahead(chosen_groups, chosen_count, first_query, first_up))
    second_far = up(attend_ahead(chosen_groups, chosen_count, second_query, second_up))
    near, logs = attend_near(chosen_groups, chosen_count, first, second, first_up, second_up)
    return paste(to_peers(merge(chosen_groups, chosen_count, near, logs, first_far, second_far)))


def solution(mesh):
    in_specs = (P(("grp", "ctx"), None), P(("grp", "ctx"), None), P(("grp", "ctx"), None), P(), P())
    out_specs = P(("grp", "ctx"), None)
    return jax.shard_map(body, mesh=mesh, in_specs=in_specs, out_specs=out_specs, check_vma=False)
```

time: 364 us -> 123 us (0.34)
  the two profiles are of different devices: /device:TPU:97 before, /device:TPU:33 now
where the time goes in v1:
time: 123 us; the launch traced here: 122 us
  starting transfers between devices  38.8 us (32%)
  waiting for transfers between devices  38.2 us (31%)
  blocking collectives  25.4 us (21%)
  Pallas kernels  16 us (13%)
  local copies, waits for them, and re-layouts  3.64 us (3%)
    all_to_all x2, waiting for transfers between devices, to_peers(): return lax.all_to_all(block, 'ctx', split_axis=0, concat_axis=0, tiled=True)  31.8 us
    all_to_all x1, blocking collectives, to_peers(): return lax.all_to_all(block, 'ctx', split_axis=0, concat_axis=0, tiled=True)  25.4 us
    ppermute x4, starting transfers between devices, up(): lax.ppermute(block, 'grp', [(at, at + 1) for at in range(group_devices -...  19.9 us
    all_to_all x2, starting transfers between devices, to_peers(): return lax.all_to_all(block, 'ctx', split_axis=0, concat_axis=0, tiled=True)  11.8 us
    pallas_call x1, Pallas kernels, attend_near(): pl.pallas_call(near_kernel, in_specs=[SMEM] * 2 + [VMEM] * 4, out_specs=[...  7.13 us
    ppermute x2, starting transfers between devices, down(): lax.ppermute(block, 'grp', [(at + 1, at) for at in range(group_devices -...  7.06 us
    ppermute x2, waiting for transfers between devices, down(): lax.ppermute(block, 'grp', [(at + 1, at) for at in range(group_devices -...  6.45 us
    pallas_call x2, Pallas kernels, attend_ahead(): pl.pallas_call(ahead_kernel, in_specs=[SMEM] * 2 + [VMEM] * 2, out_specs=...  3.65 us
  transfers between devices with their start and end apart: 8, of which 3 were waited for; matrix products, arithmetic and copies ran while one was open for 1% of the time, Pallas kernels for 10%

profile of v1, /device:TPU:33, one launch (start us, length us, event | category | flops | bytes accessed | tf_op | source)
XLA Modules:
  0.0 122.5 jit_solution(16541300381805464987)
XLA Ops:
  0.0 0.0 copy-start
  0.0 1.1 copy-done
  1.1 0.0 copy-start.2
  1.1 1.1 copy-done.2
  2.3 0.0 copy-start.4
  2.3 1.1 cut.2
  3.4 0.0 copy-start.1
  3.4 0.0 copy-start.3
  3.4 7.9 %all-to-all-start = ((bf16[32,4,32,128]{3,2,1,0:T(8,128)(2,1)}), bf16[32,4,32,128]{3,2,1,0:T(8,128)(2,1)S(1)}, u32[]{:S(2)}, u32[]{:S(2)}) async-start(bf16[32,4,32,128]{3,2,1,0:T(8,128)(2,1)} %cut.2), calls=%async_computation | async-start | bytes 2097152 | tf_op jit(solution)/shard_map/all_to_all | solution.py:296
  11.3 0.0 copy-done.4
  11.3 0.0 copy-done.1
  11.3 0.0 copy-done.3
  11.4 1.3 %cut.3 = bf16[32,5,32,128]{3,2,1,0:T(8,128)(2,1)} custom-call(bf16[256,1536]{1,0:T(8,128)(2,1)S(1)} %copy-done.1, bf16[256,1536]{1,0:T(8,128)(2,1)S(1)} %copy-done.3, bf16[256,1536]{1,0:T(8,128)(2,1)S(1)} %copy-done.4), custom_call_target="tpu_custom_call" | custom-call | tf_op jit(solution)/shard_map/cut/pallas_call | solution.py:251
  12.7 15.6 %all-to-all-done.first_ref = bf16[32,4,32,128]{3,2,1,0:T(8,128)(2,1)S(1)} async-done(((bf16[32,4,32,128]{3,2,1,0:T(8,128)(2,1)}), bf16[32,4,32,128]{3,2,1,0:T(8,128)(2,1)S(1)}, u32[]{:S(2)}, u32[]{:S(2)}) %all-to-all-start) | async-done | bytes 1048608 | tf_op jit(solution)/shard_map/all_to_all | solution.py:296
  28.2 4.0 %all-to-all-start.1 = ((bf16[32,5,32,128]{3,2,1,0:T(8,128)(2,1)}), bf16[32,5,32,128]{3,2,1,0:T(8,128)(2,1)S(1)}, u32[]{:S(2)}, u32[]{:S(2)}) async-start(bf16[32,5,32,128]{3,2,1,0:T(8,128)(2,1)} %cut.3), calls=%async_computation.1 | async-start | bytes 2621440 | tf_op jit(solution)/shard_map/all_to_all | solution.py:296
  32.2 0.0 copy-start.5
  32.2 0.0 copy-start.6
  32.2 3.5 %collective-permute-start = (bf16[32,4,32,128]{3,2,1,0:T(8,128)(2,1)S(1)}, bf16[32,4,32,128]{3,2,1,0:T(8,128)(2,1)}, u32[]{:S(2)}, u32[]{:S(2)}) collective-permute-start(bf16[32,4,32,128]{3,2,1,0:T(8,128)(2,1)S(1)} %all-to-all-done.first_ref), channel_id=1, source_target_pairs={{0,32},{32,64},{64,96},{96,128},{128,160},{160,192},{192,224},{224... | collective-permute-start | bytes 3145736 | tf_op jit(solution)/shard_map/ppermute | solution.py:299
  35.8 16.2 %all-to-all-done.1.second_ref = bf16[32,5,32,128]{3,2,1,0:T(8,128)(2,1)S(1)} async-done(((bf16[32,5,32,128]{3,2,1,0:T(8,128)(2,1)}), bf16[32,5,32,128]{3,2,1,0:T(8,128)(2,1)S(1)}, u32[]{:S(2)}, u32[]{:S(2)}) %all-to-all-start.1) | async-done | bytes 1310752 | tf_op jit(solution)/shard_map/all_to_all | solution.py:296
  52.0 1.1 fusion
  53.1 3.7 %collective-permute-start.2 = (bf16[32,2,32,128]{3,2,1,0:T(8,128)(2,1)}, bf16[32,2,32,128]{3,2,1,0:T(8,128)(2,1)}, u32[]{:S(2)}, u32[]{:S(2)}) collective-permute-start(bf16[32,2,32,128]{3,2,1,0:T(8,128)(2,1)} %get-tuple-element.13), channel_id=1, source_target_pairs={{32,0},{64,32},{96,64},{128,96},{160,128},{192,160},{224,192},{256... | collective-permute-start | bytes 1572872 | tf_op jit(solution)/shard_map/ppermute | solution.py:302
  56.8 1.9 %collective-permute-start.1 = (bf16[32,2,32,128]{3,2,1,0:T(8,128)(2,1)}, bf16[32,2,32,128]{3,2,1,0:T(8,128)(2,1)S(1)}, u32[]{:S(2)}, u32[]{:S(2)}) collective-permute-start(bf16[32,2,32,128]{3,2,1,0:T(8,128)(2,1)} %get-tuple-element.14), channel_id=1, source_target_pairs={{0,32},{32,64},{64,96},{96,128},{128,160},{160,192},{192,224},{224... | collective-permute-start | bytes 1572872 | tf_op jit(solution)/shard_map/ppermute | solution.py:299
  58.7 0.0 copy-done.5
  58.7 0.1 copy.12.groups_ref
  58.9 0.0 copy-done.6
  58.9 0.1 copy.13.count_ref
  59.0 3.4 %collective-permute-start.4 = (bf16[32,1,32,128]{3,2,1,0:T(8,128)(2,1)S(1)}, bf16[32,1,32,128]{3,2,1,0:T(8,128)(2,1)S(1)}, u32[]{:S(2)}, u32[]{:S(2)}) collective-permute-start(bf16[32,1,32,128]{3,2,1,0:T(8,128)(2,1)S(1)} %slice.14), channel_id=1, source_target_pairs={{32,0},{64,32},{96,64},{128,96},{160,128},{192,160},{224,192},{256... | collective-permute-start | bytes 786440 | tf_op jit(solution)/shard_map/ppermute | solution.py:302
  62.4 0.0 collective-permute-done.first_up_ref.kv_ref
  62.4 6.5 %collective-permute-done.2.q_ref = bf16[32,2,32,128]{3,2,1,0:T(8,128)(2,1)} collective-permute-done((bf16[32,2,32,128]{3,2,1,0:T(8,128)(2,1)}, bf16[32,2,32,128]{3,2,1,0:T(8,128)(2,1)}, u32[]{:S(2)}, u32[]{:S(2)}) %collective-permute-start.2) | collective-permute-done | bytes 524320 | tf_op jit(solution)/shard_map/ppermute | solution.py:302
  68.8 1.8 %ahead.2 = bf16[2,1056,128]{2,1,0:T(8,128)(2,1)S(1)} custom-call(s32[16,8,2]{2,1,0:T(8,128)S(1)} %copy.12.groups_ref, s32[16,8]{1,0:T(8,128)S(1)} %copy.13.count_ref, bf16[32,2,32,128]{3,2,1,0:T(8,128)(2,1)} %collective-permute-done.2.q_ref, bf16[32,4,32,128]{3,2,1,0:T(8,128)(2,1)} %collective-permute-done.first_up_ref.kv_ref), custom_call_target="tpu_custom_call" | custom-call | flops 1073741824 | bytes 2097152 | tf_op jit(solution)/shard_map/ahead/pallas_call | solution.py:200
  70.7 7.6 %collective-permute-start.3 = (bf16[2,1056,128]{2,1,0:T(8,128)(2,1)S(1)}, bf16[2,1056,128]{2,1,0:T(8,128)(2,1)S(1)}, u32[]{:S(2)}, u32[]{:S(2)}) collective-permute-start(bf16[2,1056,128]{2,1,0:T(8,128)(2,1)S(1)} %ahead.2), channel_id=1, source_target_pairs={{0,32},{32,64},{64,96},{96,128},{128,160},{160,192},{192,224},{224... | collective-permute-start | bytes 1622024 | tf_op jit(solution)/shard_map/ppermute | solution.py:299
  78.3 0.0 collective-permute-done.4.q_ref
  78.3 0.0 collective-permute-done.1.second_up_ref.kv_ref
  78.3 1.8 %ahead.3 = bf16[1,1056,128]{2,1,0:T(8,128)(2,1)S(1)} custom-call(s32[16,8,2]{2,1,0:T(8,128)S(1)} %copy.12.groups_ref, s32[16,8]{1,0:T(8,128)S(1)} %copy.13.count_ref, bf16[32,1,32,128]{3,2,1,0:T(8,128)(2,1)S(1)} %collective-permute-done.4.q_ref, bf16[32,2,32,128]{3,2,1,0:T(8,128)(2,1)S(1)} %collective-permute-done.1.second_up_ref.kv_ref), custom_call_target="tpu_custom_call" | custom-call | flops 536870912 | bytes 1048576 | tf_op jit(solution)/shard_map/ahead/pallas_call | solution.py:200
  80.1 6.8 %collective-permute-start.5 = (bf16[1,1056,128]{2,1,0:T(8,128)(2,1)S(1)}, bf16[1,1056,128]{2,1,0:T(8,128)(2,1)S(1)}, u32[]{:S(2)}, u32[]{:S(2)}) collective-permute-start(bf16[1,1056,128]{2,1,0:T(8,128)(2,1)S(1)} %ahead.3), channel_id=1, source_target_pairs={{0,32},{32,64},{64,96},{96,128},{128,160},{160,192},{192,224},{224... | collective-permute-start | bytes 811016 | tf_op jit(solution)/shard_map/ppermute | solution.py:299
  87.0 7.1 %near.1 = (f32[3,1024,128]{2,1,0:T(8,128)S(1)}, f32[3,8,128]{2,1,0:T(8,128)S(1)}) custom-call(s32[16,8,2]{2,1,0:T(8,128)S(1)} %copy.12.groups_ref, s32[16,8]{1,0:T(8,128)S(1)} %copy.13.count_ref, bf16[32,4,32,128]{3,2,1,0:T(8,128)(2,1)S(1)} %all-to-all-done.first_ref, bf16[32,5,32,128]{3,2,1,0:T(8,128)(2,1)S(1)} %all-to-all-done.1.second_ref, ...), custom_call_target="tpu_custom_call" | custom-call | flops 2576980480 | bytes 5505024 | tf_op jit(solution)/shard_map/near/pallas_call | solution.py:213
  94.1 0.0 collective-permute-done.5.second_far_ref
  94.1 0.0 collective-permute-done.3.first_far_ref
  94.1 1.8 %merge.1 = bf16[32,3,32,128]{3,2,1,0:T(8,128)(2,1)S(1)} custom-call(s32[16,8,2]{2,1,0:T(8,128)S(1)} %copy.12.groups_ref, s32[16,8]{1,0:T(8,128)S(1)} %copy.13.count_ref, f32[3,1024,128]{2,1,0:T(8,128)S(1)} %get-tuple-element.11.near_ref, f32[3,8,128]{2,1,0:T(8,128)S(1)} %get-tuple-element.12.log_ref, ...), custom_call_target="tpu_custom_call" | custom-call | bytes 3145728 | tf_op jit(solution)/shard_map/merge/pallas_call | solution.py:229
  96.0 25.4 %all_to_all.15.in_ref = bf16[32,3,32,128]{3,2,1,0:T(8,128)(2,1)S(1)} all-to-all(bf16[32,3,32,128]{3,2,1,0:T(8,128)(2,1)S(1)} %merge.1), channel_id=1, replica_groups=mesh['grp'=16,'ctx'=32] {'ctx'}, dimensions={0} | all-to-all | bytes 1572864 | tf_op jit(solution)/shard_map/all_to_all | solution.py:296
  121.3 1.0 paste.1
  (1 shorter events, 0.0 us)
Async XLA Ops:
  0.0 1.1 copy-start
  1.1 1.1 copy-start.2
  2.3 9.1 %copy-start.4 = (bf16[256,1536]{1,0:T(8,128)(2,1)S(1)}, bf16[256,1536]{1,0:T(8,128)(2,1)}, u32[]{:S(2)}) copy-start(bf16[256,1536]{1,0:T(8,128)(2,1)} %refs_2_.1) | copy-start | bytes 2359300
  3.4 7.9 %copy-start.1 = (bf16[256,1536]{1,0:T(8,128)(2,1)S(1)}, bf16[256,1536]{1,0:T(8,128)(2,1)}, u32[]{:S(2)}) copy-start(bf16[256,1536]{1,0:T(8,128)(2,1)} %refs_0_.3) | copy-start | bytes 2359300
  3.4 7.9 %copy-start.3 = (bf16[256,1536]{1,0:T(8,128)(2,1)S(1)}, bf16[256,1536]{1,0:T(8,128)(2,1)}, u32[]{:S(2)}) copy-start(bf16[256,1536]{1,0:T(8,128)(2,1)} %refs_1_.3) | copy-start | bytes 2359300
  3.4 24.8 %all-to-all-start = ((bf16[32,4,32,128]{3,2,1,0:T(8,128)(2,1)}), bf16[32,4,32,128]{3,2,1,0:T(8,128)(2,1)S(1)}, u32[]{:S(2)}, u32[]{:S(2)}) async-start(bf16[32,4,32,128]{3,2,1,0:T(8,128)(2,1)} %cut.2), calls=%async_computation | async-start | bytes 2097152 | tf_op jit(solution)/shard_map/all_to_all | solution.py:296
  28.2 23.8 %all-to-all-start.1 = ((bf16[32,5,32,128]{3,2,1,0:T(8,128)(2,1)}), bf16[32,5,32,128]{3,2,1,0:T(8,128)(2,1)S(1)}, u32[]{:S(2)}, u32[]{:S(2)}) async-start(bf16[32,5,32,128]{3,2,1,0:T(8,128)(2,1)} %cut.3), calls=%async_computation.1 | async-start | bytes 2621440 | tf_op jit(solution)/shard_map/all_to_all | solution.py:296
  32.2 26.5 %copy-start.5 = (s32[16,8,2]{0,2,1:T(2,128)S(1)}, s32[16,8,2]{0,2,1:T(2,128)}, u32[]{:S(2)}) copy-start(s32[16,8,2]{0,2,1:T(2,128)} %param.8) | copy-start | bytes 3076
  32.2 26.7 %copy-start.6 = (s32[16,8]{0,1:T(8,128)S(1)}, s32[16,8]{0,1:T(8,128)}, u32[]{:S(2)}) copy-start(s32[16,8]{0,1:T(8,128)} %param.9) | copy-start | bytes 1540
  32.2 30.1 %collective-permute-start = (bf16[32,4,32,128]{3,2,1,0:T(8,128)(2,1)S(1)}, bf16[32,4,32,128]{3,2,1,0:T(8,128)(2,1)}, u32[]{:S(2)}, u32[]{:S(2)}) collective-permute-start(bf16[32,4,32,128]{3,2,1,0:T(8,128)(2,1)S(1)} %all-to-all-done.first_ref), channel_id=1, source_target_pairs={{0,32},{32,64},{64,96},{96,128},{128,160},{160,192},{192,224},{224... | collective-permute-start | bytes 3145736 | tf_op jit(solution)/shard_map/ppermute | solution.py:299
  53.1 15.7 %collective-permute-start.2 = (bf16[32,2,32,128]{3,2,1,0:T(8,128)(2,1)}, bf16[32,2,32,128]{3,2,1,0:T(8,128)(2,1)}, u32[]{:S(2)}, u32[]{:S(2)}) collective-permute-start(bf16[32,2,32,128]{3,2,1,0:T(8,128)(2,1)} %get-tuple-element.13), channel_id=1, source_target_pairs={{32,0},{64,32},{96,64},{128,96},{160,128},{192,160},{224,192},{256... | collective-permute-start | bytes 1572872 | tf_op jit(solution)/shard_map/ppermute | solution.py:302
  56.8 21.5 %collective-permute-start.1 = (bf16[32,2,32,128]{3,2,1,0:T(8,128)(2,1)}, bf16[32,2,32,128]{3,2,1,0:T(8,128)(2,1)S(1)}, u32[]{:S(2)}, u32[]{:S(2)}) collective-permute-start(bf16[32,2,32,128]{3,2,1,0:T(8,128)(2,1)} %get-tuple-element.14), channel_id=1, source_target_pairs={{0,32},{32,64},{64,96},{96,128},{128,160},{160,192},{192,224},{224... | collective-permute-start | bytes 1572872 | tf_op jit(solution)/shard_map/ppermute | solution.py:299
  59.0 19.3 %collective-permute-start.4 = (bf16[32,1,32,128]{3,2,1,0:T(8,128)(2,1)S(1)}, bf16[32,1,32,128]{3,2,1,0:T(8,128)(2,1)S(1)}, u32[]{:S(2)}, u32[]{:S(2)}) collective-permute-start(bf16[32,1,32,128]{3,2,1,0:T(8,128)(2,1)S(1)} %slice.14), channel_id=1, source_target_pairs={{32,0},{64,32},{96,64},{128,96},{160,128},{192,160},{224,192},{256... | collective-permute-start | bytes 786440 | tf_op jit(solution)/shard_map/ppermute | solution.py:302
  70.7 23.4 %collective-permute-start.3 = (bf16[2,1056,128]{2,1,0:T(8,128)(2,1)S(1)}, bf16[2,1056,128]{2,1,0:T(8,128)(2,1)S(1)}, u32[]{:S(2)}, u32[]{:S(2)}) collective-permute-start(bf16[2,1056,128]{2,1,0:T(8,128)(2,1)S(1)} %ahead.2), channel_id=1, source_target_pairs={{0,32},{32,64},{64,96},{96,128},{128,160},{160,192},{192,224},{224... | collective-permute-start | bytes 1622024 | tf_op jit(solution)/shard_map/ppermute | solution.py:299
  80.1 14.0 %collective-permute-start.5 = (bf16[1,1056,128]{2,1,0:T(8,128)(2,1)S(1)}, bf16[1,1056,128]{2,1,0:T(8,128)(2,1)S(1)}, u32[]{:S(2)}, u32[]{:S(2)}) collective-permute-start(bf16[1,1056,128]{2,1,0:T(8,128)(2,1)S(1)} %ahead.3), channel_id=1, source_target_pairs={{0,32},{32,64},{64,96},{96,128},{128,160},{160,192},{192,224},{224... | collective-permute-start | bytes 811016 | tf_op jit(solution)/shard_map/ppermute | solution.py:299

commit v2 on v1

v2 whole, which is shorter than its diff:
```python
import functools
import math

import jax
import jax.numpy as jnp
from jax import lax
from jax.experimental import pallas as pl
from jax.experimental.pallas import tpu as pltpu
from jax.sharding import PartitionSpec as P

HEADS = 12
HD = 128
POS = 256
SPAN = 4
NWIN = 8
LOOK = 2
QB = 256
PARTS = HEADS // SPAN
POSITIONS = POS // NWIN
STAT_ROWS = 32
LOG2E = math.log2(math.e)
FACTOR = HD**-0.5 * LOG2E
NEG_FILL = -1e30
SMEM = pl.BlockSpec(memory_space=pltpu.SMEM)
VMEM = pl.BlockSpec(memory_space=pltpu.VMEM)
ANY = pl.BlockSpec(memory_space=pl.ANY)
HBM = pl.BlockSpec(memory_space=pltpu.HBM)
SMALL = pltpu.CompilerParams(vmem_limit_bytes=2**20)
PARAMS = pltpu.CompilerParams(vmem_limit_bytes=8 * 2**20)


def is_taken(groups_ref, count_ref, group, distance):
    groups = groups_ref.shape[0]
    window = lax.axis_index("ctx") // SPAN
    held = jnp.minimum(group, groups - 1)
    source = group - distance
    count = count_ref[held, window]
    taken = jnp.bool_(False)
    for slot in range(LOOK):
        taken = taken | ((groups_ref[held, window, slot] == source) & (slot < count))
    return taken & (source >= 0) & (group < groups)


def flags_kernel(groups_ref, count_ref, out_ref):
    group = lax.axis_index("grp")
    for at, (owner, distance) in enumerate(((group, 1), (group, 2), (group + 1, 2))):
        out_ref[at] = is_taken(groups_ref, count_ref, owner, distance).astype(jnp.int32)
    out_ref[3] = jnp.int32(0)


def make_flags(groups, count):
    return pl.pallas_call(
        flags_kernel,
        in_specs=[SMEM] * 2,
        out_specs=SMEM,
        out_shape=jax.ShapeDtypeStruct((4,), jnp.int32),
        compiler_params=SMALL,
        name="flags",
    )(groups, count)


def score(query, keys):
    return lax.dot_general(
        query, keys, (((1,), (1,)), ((), ())), preferred_element_type=jnp.float32
    )


def soften(scores, values, diagonal=False):
    if diagonal:
        rows, count = scores.shape
        tail = scores[:, count - rows :]
        frame_query = lax.broadcasted_iota(jnp.int32, (rows, rows), 0) // POSITIONS
        frame_key = lax.broadcasted_iota(jnp.int32, (rows, rows), 1) // POSITIONS
        tail = jnp.where(frame_query >= frame_key, tail, NEG_FILL)
        scores = jnp.concatenate([scores[:, : count - rows], tail], axis=1) if count > rows else tail
    highest = jnp.max(scores, axis=-1, keepdims=True)
    weights = jnp.exp2((scores - highest) * FACTOR)
    summed = jnp.sum(weights, axis=-1, keepdims=True)
    blended = jnp.dot(weights.astype(jnp.bfloat16), values, preferred_element_type=jnp.float32)
    return highest, summed, blended


def in_turn(jobs, done):
    scores = jobs[0][0]()
    for at, (_, finish) in enumerate(jobs):
        following = jobs[at + 1][0]() if at + 1 < len(jobs) else None
        done(at, finish(scores))
        scores = following


def join(old, new):
    ceiling = jnp.maximum(old[0], new[0])
    old_scale = jnp.exp2((old[0] - ceiling) * FACTOR)
    new_scale = jnp.exp2((new[0] - ceiling) * FACTOR)
    return (
        ceiling,
        old[1] * old_scale + new[1] * new_scale,
        old[2] * old_scale + new[2] * new_scale,
    )


def rows_of(ref, slab, start, size):
    first, count = start // POSITIONS, size // POSITIONS
    return ref[pl.ds(first, count), slab].reshape(size, HD)


def eye_mask():
    return lax.broadcasted_iota(jnp.int32, (HD, HD), 0) == lax.broadcasted_iota(
        jnp.int32, (HD, HD), 1
    )


def log_rows(part):
    log_sum = part[0] * FACTOR + jnp.log(part[1]) * LOG2E
    return [
        jnp.sum(jnp.where(eye_mask(), log_sum[at : at + HD], 0.0), axis=0, keepdims=True)
        for at in range(0, log_sum.shape[0], HD)
    ]


def ahead_kernel(flags_ref, q_ref, kv_ref, out_ref):
    rows = q_ref.shape[0] * POSITIONS
    heads = out_ref.shape[0]
    taken = flags_ref[2] > 0

    @pl.when(taken)
    def _():
        @pl.loop(0, heads)
        def _(head):
            keys = kv_ref[:, 2 * head].reshape(rows, HD)
            values = kv_ref[:, 2 * head + 1].reshape(rows, HD)

            def job(start):
                return (
                    lambda: score(rows_of(q_ref, head, start, QB), keys),
                    lambda scores: soften(scores, values),
                )

            logs = []

            def done(at, part):
                out_ref[head, pl.ds(at * QB, QB), :] = (part[2] / part[1]).astype(jnp.bfloat16)
                logs.extend(log_rows(part))

            in_turn([job(start) for start in range(0, rows, QB)], done)
            left = jnp.concatenate(logs, axis=0)
            pieces = []
            for _ in range(3):
                pieces.append(left.astype(jnp.bfloat16).astype(jnp.float32))
                left = left - pieces[-1]
            pieces.append(jnp.zeros((STAT_ROWS - 3 * left.shape[0], HD), jnp.float32))
            packed = jnp.concatenate(pieces, axis=0).astype(jnp.bfloat16)
            out_ref[head, pl.ds(rows, STAT_ROWS), :] = packed

    @pl.when(jnp.logical_not(taken))
    def _():
        out_ref[:, pl.ds(rows, STAT_ROWS), :] = jnp.zeros((heads, STAT_ROWS, HD), jnp.bfloat16)


def near_kernel(query_slab, flags_ref, q_ref, own_ref, up_ref, out_ref, log_ref):
    rows = q_ref.shape[0] * POSITIONS
    heads = out_ref.shape[0]
    taken = flags_ref[0] > 0

    def run(with_earlier):
        @pl.loop(0, heads)
        def _(head):
            def own(start):
                def begin():
                    query = rows_of(q_ref, query_slab + head, start, QB)
                    return score(query, rows_of(own_ref, 2 * head, 0, start + QB))

                def finish(scores):
                    return soften(scores, rows_of(own_ref, 2 * head + 1, 0, start + QB), True)

                return begin, finish

            def earlier(start):
                def begin():
                    query = rows_of(q_ref, query_slab + head, start, QB)
                    return score(query, rows_of(up_ref, 2 * head, 0, rows))

                def finish(scores):
                    return soften(scores, rows_of(up_ref, 2 * head + 1, 0, rows))

                return begin, finish

            logs = []
            held = []

            def done(at, part):
                if with_earlier:
                    held.append(part)
                    if at % 2 == 0:
                        return
                    part = join(held[-2], held[-1])
                    at = at // 2
                out_ref[head, pl.ds(at * QB, QB), :] = part[2] / part[1]
                logs.extend(log_rows(part))

            jobs = []
            for start in range(0, rows, QB):
                jobs.append(own(start))
                if with_earlier:
                    jobs.append(earlier(start))
            in_turn(jobs, done)
            log_ref[head] = jnp.concatenate(logs, axis=0)

    @pl.when(taken)
    def _():
        run(True)

    @pl.when(jnp.logical_not(taken))
    def _():
        run(False)


def merge_kernel(flags_ref, near_a, near_b, log_a, log_b, far_a, far_b, out_ref):
    rows = near_a.shape[1]
    blocks = rows // HD
    taken = flags_ref[1] > 0

    def put(head, block, value):
        count = HD // POSITIONS
        frames = pl.ds(block * count, count)
        out_ref[frames, head] = value.astype(jnp.bfloat16).reshape(count, POSITIONS, HD)

    def each_head():
        count = near_a.shape[0]
        for head in range(PARTS):
            refs = (near_a, log_a, far_a) if head < count else (near_b, log_b, far_b)
            yield (head,) + tuple(ref.at[head if head < count else head - count] for ref in refs)

    @pl.when(taken)
    def _():
        for head, near_ref, log_ref, far_ref in each_head():
            pieces = far_ref[pl.ds(rows, STAT_ROWS), :].astype(jnp.float32)
            far_log = pieces[:blocks] + pieces[blocks : 2 * blocks] + pieces[2 * blocks : 3 * blocks]
            shares = jnp.transpose(1.0 / (1.0 + jnp.exp2(log_ref[...] - far_log)))
            for block in range(blocks):
                part = pl.ds(block * HD, HD)
                near = near_ref[part, :]
                far = far_ref[part, :].astype(jnp.float32)
                put(head, block, near + (far - near) * shares[:, block : block + 1])

    @pl.when(jnp.logical_not(taken))
    def _():
        for head, near_ref, _, _ in each_head():
            for block in range(blocks):
                put(head, block, near_ref[pl.ds(block * HD, HD), :])


def cost(passes, rows, heads, moved):
    return pl.CostEstimate(
        flops=int(4 * passes * rows * rows * heads * HD),
        bytes_accessed=moved,
        transcendentals=int(passes * rows * rows * heads),
    )


def attend_ahead(flags, query, pair):
    rows, heads = pair.shape[0] * POSITIONS, pair.shape[1] // 2
    return pl.pallas_call(
        ahead_kernel,
        in_specs=[SMEM] + [VMEM] * 2,
        out_specs=VMEM,
        out_shape=jax.ShapeDtypeStruct((heads, rows + STAT_ROWS, HD), jnp.bfloat16),
        compiler_params=PARAMS,
        cost_estimate=cost(1, rows, heads, rows * heads * HD * 8),
        name="ahead",
    )(flags, query, pair)


def attend_near(flags, query, query_slab, own, pair):
    rows, heads = pair.shape[0] * POSITIONS, pair.shape[1] // 2
    return pl.pallas_call(
        functools.partial(near_kernel, query_slab),
        in_specs=[SMEM] + [VMEM] * 3,
        out_specs=[VMEM] * 2,
        out_shape=[
            jax.ShapeDtypeStruct((heads, rows, HD), jnp.float32),
            jax.ShapeDtypeStruct((heads, rows // HD, HD), jnp.float32),
        ],
        compiler_params=PARAMS,
        cost_estimate=cost(1.6, rows, heads, rows * heads * HD * 14),
        name="near",
    )(flags, query, own, pair)


def merge(flags, near, logs, far):
    rows = near[0].shape[1]
    return pl.pallas_call(
        merge_kernel,
        in_specs=[SMEM] + [VMEM] * 6,
        out_specs=VMEM,
        out_shape=jax.ShapeDtypeStruct((rows // POSITIONS, PARTS, POSITIONS, HD), jnp.bfloat16),
        compiler_params=PARAMS,
        cost_estimate=cost(0, rows, PARTS, rows * PARTS * HD * 8),
        name="merge",
    )(flags, *near, *logs, *far)


def cut_first_kernel(k_ref, v_ref, out_ref, held_ref, piece_ref, in_sems, out_sems):
    def fetch(which, window):
        rows = pl.ds(window * POSITIONS, POSITIONS)
        ref = (k_ref, v_ref)[which]
        return pltpu.make_async_copy(
            ref.at[rows], held_ref.at[which, rows], in_sems.at[which, window]
        )

    def store(window):
        peers = pl.ds(window * SPAN, SPAN)
        return pltpu.make_async_copy(piece_ref.at[peers], out_ref.at[peers], out_sems.at[window])

    for window in range(NWIN):
        for which in range(2):
            fetch(which, window).start()
    for window in range(NWIN):
        rows = pl.ds(window * POSITIONS, POSITIONS)
        for which in range(2):
            fetch(which, window).wait()
            for part in range(SPAN):
                for head in range(2):
                    lanes = pl.ds((part * PARTS + head) * HD, HD)
                    piece_ref[window * SPAN + part, 2 * head + which] = held_ref[which, rows, lanes]
        store(window).start()
    for window in range(NWIN):
        store(window).wait()


def cut_first(key, value):
    shape = (NWIN * SPAN, 4, POSITIONS, HD)
    return pl.pallas_call(
        cut_first_kernel,
        in_specs=[HBM] * 2,
        out_specs=HBM,
        out_shape=jax.ShapeDtypeStruct(shape, jnp.bfloat16),
        scratch_shapes=[
            pltpu.VMEM((2,) + key.shape, jnp.bfloat16),
            pltpu.VMEM(shape, jnp.bfloat16),
            pltpu.SemaphoreType.DMA((2, NWIN)),
            pltpu.SemaphoreType.DMA((NWIN,)),
        ],
        compiler_params=pltpu.CompilerParams(vmem_limit_bytes=60 * 2**20),
        name="cut_first",
    )(key, value)


def gate_kernel(*refs):
    del refs


def gate(passed, *waited):
    return pl.pallas_call(
        gate_kernel,
        in_specs=[ANY] * (1 + len(waited)),
        out_specs=ANY,
        out_shape=jax.ShapeDtypeStruct(passed.shape, passed.dtype),
        input_output_aliases={0: 0},
        compiler_params=SMALL,
        name="gate",
    )(passed, *waited)


def cut_kernel(slabs, *refs):
    sources, out_ref = refs[:-1], refs[-1]
    for window in range(NWIN):
        rows = pl.ds(window * POSITIONS, POSITIONS)
        for part in range(SPAN):
            for slab, (source, head) in enumerate(slabs):
                lanes = pl.ds((part * PARTS + head) * HD, HD)
                out_ref[window * SPAN + part, slab] = sources[source][rows, lanes]


def cut(sources, slabs):
    return pl.pallas_call(
        functools.partial(cut_kernel, slabs),
        in_specs=[VMEM] * len(sources),
        out_specs=VMEM,
        out_shape=jax.ShapeDtypeStruct((NWIN * SPAN, len(slabs), POSITIONS, HD), jnp.bfloat16),
        compiler_params=PARAMS,
        cost_estimate=pl.CostEstimate(flops=10**11, bytes_accessed=2**22, transcendentals=0),
        name="cut",
    )(*sources)


def paste_kernel(in_ref, out_ref, held_ref, sems):
    copies = []
    for window in range(NWIN):
        rows = pl.ds(window * POSITIONS, POSITIONS)
        for part in range(SPAN):
            for head in range(PARTS):
                lanes = pl.ds((part * PARTS + head) * HD, HD)
                held_ref[rows, lanes] = in_ref[window * SPAN + part, head]
        copies.append(
            pltpu.make_async_copy(held_ref.at[rows], out_ref.at[rows], sems.at[window])
        )
        copies[-1].start()
    for copy in copies:
        copy.wait()


def paste(pieces):
    return pl.pallas_call(
        paste_kernel,
        in_specs=[VMEM],
        out_specs=ANY,
        out_shape=jax.ShapeDtypeStruct((POS, HEADS * HD), jnp.bfloat16),
        scratch_shapes=[
            pltpu.VMEM((POS, HEADS * HD), jnp.bfloat16),
            pltpu.SemaphoreType.DMA((NWIN,)),
        ],
        compiler_params=PARAMS,
        name="paste",
    )(pieces)


def body(query_vectors, key_vectors, value_vectors, chosen_groups, chosen_count):
    group_devices = lax.axis_size("grp")

    def to_peers(block):
        return lax.all_to_all(block, "ctx", split_axis=0, concat_axis=0, tiled=True)

    def up(block):
        return lax.ppermute(block, "grp", [(at, at + 1) for at in range(group_devices - 1)])

    def down(block):
        return lax.ppermute(block, "grp", [(at + 1, at) for at in range(group_devices - 1)])

    later_query = down(query_vectors)
    first = to_peers(cut_first(key_vectors, value_vectors))
    first_up = up(first)
    flags = make_flags(chosen_groups, chosen_count)
    second = cut(
        (key_vectors, value_vectors, later_query), ((0, 2), (1, 2), (2, 0), (2, 1), (2, 2))
    )
    second = to_peers(gate(second, first, flags))
    second_pair = second[:, 0:2]
    second_up = up(second_pair)
    query = to_peers(gate(cut((query_vectors,), ((0, 0), (0, 1), (0, 2))), second_pair))
    first_far = up(attend_ahead(flags, second[:, 2:4], first_up))
    second_far = up(attend_ahead(flags, second[:, 4:5], second_up))
    near_a, log_a = attend_near(flags, query, 0, first, first_up)
    near_b, log_b = attend_near(flags, query, 2, second_pair, second_up)
    merged = merge(flags, (near_a, near_b), (log_a, log_b), (first_far, second_far))
    return paste(to_peers(merged))


def solution(mesh):
    in_specs = (P(("grp", "ctx"), None), P(("grp", "ctx"), None), P(("grp", "ctx"), None), P(), P())
    out_specs = P(("grp", "ctx"), None)
    return jax.shard_map(body, mesh=mesh, in_specs=in_specs, out_specs=out_specs, check_vma=False)
```

time: 123 us -> 120 us (0.976)
  the two profiles are of different devices: /device:TPU:33 before, /device:TPU:385 now
where the time goes in v2:
time: 120 us; the launch traced here: 119 us
  waiting for transfers between devices  42.9 us (36%)
  starting transfers between devices  31.7 us (26%)
  blocking collectives  22.7 us (19%)
  Pallas kernels  17.8 us (15%)
  local copies, waits for them, and re-layouts  3.75 us (3%)
    all_to_all x3, waiting for transfers between devices, to_peers(): return lax.all_to_all(block, 'ctx', split_axis=0, concat_axis=0, tiled=True)  25.2 us
    all_to_all x1, blocking collectives, to_peers(): return lax.all_to_all(block, 'ctx', split_axis=0, concat_axis=0, tiled=True)  22.7 us
    all_to_all x3, starting transfers between devices, to_peers(): return lax.all_to_all(block, 'ctx', split_axis=0, concat_axis=0, tiled=True)  16.7 us
    ppermute x4, waiting for transfers between devices, up(): lax.ppermute(block, 'grp', [(at, at + 1) for at in range(group_devices -...  14 us
    ppermute x4, starting transfers between devices, up(): lax.ppermute(block, 'grp', [(at, at + 1) for at in range(group_devices -...  11.1 us
    pallas_call x2, Pallas kernels, attend_near(): pl.pallas_call(functools.partial(near_kernel, query_slab), in_specs=[SMEM...  5.52 us
    ppermute x1, starting transfers between devices, down(): lax.ppermute(block, 'grp', [(at + 1, at) for at in range(group_devices -...  3.84 us
    ppermute x1, waiting for transfers between devices, down(): lax.ppermute(block, 'grp', [(at + 1, at) for at in range(group_devices -...  3.6 us
  transfers between devices with their start and end apart: 8, of which 7 were waited for; matrix products, arithmetic and copies ran while one was open for 2% of the time, Pallas kernels for 14%

profile of v2, /device:TPU:385, one launch (start us, length us, event | category | flops | bytes accessed | tf_op | source)
XLA Modules:
  0.0 119.1 jit_solution(1392119143293630460)
XLA Ops:
  0.0 3.8 %collective-permute-start = (bf16[256,1536]{1,0:T(8,128)(2,1)}, bf16[256,1536]{1,0:T(8,128)(2,1)}, u32[]{:S(2)}, u32[]{:S(2)}) collective-permute-start(bf16[256,1536]{1,0:T(8,128)(2,1)} %refs_0_.2), channel_id=1, source_target_pairs={{32,0},{64,32},{96,64},{128,96},{160,128},{192,160},{224,192},{256... | collective-permute-start | bytes 2359304 | tf_op jit(solution)/shard_map/ppermute | solution.py:428
  3.8 2.3 %cut_first.1 = bf16[32,4,32,128]{3,2,1,0:T(8,128)(2,1)} custom-call(bf16[256,1536]{1,0:T(8,128)(2,1)} %k_ref.1, bf16[256,1536]{1,0:T(8,128)(2,1)} %v_ref.1), custom_call_target="tpu_custom_call" | custom-call | tf_op jit(solution)/shard_map/cut_first/pallas_call | solution.py:333
  6.2 0.0 copy-start.6
  6.2 0.0 copy-start.5
  6.2 0.0 copy-start
  6.2 0.0 copy-start.1
  6.2 8.2 %all-to-all-start = ((bf16[32,4,32,128]{3,2,1,0:T(8,128)(2,1)}), bf16[32,4,32,128]{3,2,1,0:T(8,128)(2,1)S(1)}, u32[]{:S(2)}, u32[]{:S(2)}) async-start(bf16[32,4,32,128]{3,2,1,0:T(8,128)(2,1)} %cut_first.1), calls=%async_computation | async-start | bytes 2097152 | tf_op jit(solution)/shard_map/all_to_all | solution.py:422
  14.4 0.0 copy-done.6
  14.4 0.1 copy.9.count_ref
  14.5 0.0 copy-done.5
  14.5 0.1 copy.8.groups_ref
  14.6 2.4 %flags.1.refs_2_.flags_ref = s32[4]{0:T(128)S(1)} custom-call(s32[16,8,2]{2,1,0:T(8,128)S(1)} %copy.8.groups_ref, s32[16,8]{1,0:T(8,128)S(1)} %copy.9.count_ref), custom_call_target="tpu_custom_call" | custom-call | tf_op jit(solution)/shard_map/flags/pallas_call | solution.py:52
  17.0 3.6 %collective-permute-done.refs_2_ = bf16[256,1536]{1,0:T(8,128)(2,1)} collective-permute-done((bf16[256,1536]{1,0:T(8,128)(2,1)}, bf16[256,1536]{1,0:T(8,128)(2,1)}, u32[]{:S(2)}, u32[]{:S(2)}) %collective-permute-start) | collective-permute-done | bytes 786464 | tf_op jit(solution)/shard_map/ppermute | solution.py:428
  20.6 0.0 copy-done
  20.6 0.0 copy-done.1
  20.6 2.4 %cut.3.refs_0_ = bf16[32,5,32,128]{3,2,1,0:T(8,128)(2,1)} custom-call(bf16[256,1536]{1,0:T(8,128)(2,1)S(1)} %copy-done, bf16[256,1536]{1,0:T(8,128)(2,1)S(1)} %copy-done.1, bf16[256,1536]{1,0:T(8,128)(2,1)} %collective-permute-done.refs_2_), custom_call_target="tpu_custom_call" | custom-call | flops 99999997952 | bytes 4194304 | tf_op jit(solution)/shard_map/cut/pallas_call | solution.py:376
  23.0 8.3 %all-to-all-done.refs_1_.own_ref = bf16[32,4,32,128]{3,2,1,0:T(8,128)(2,1)S(1)} async-done(((bf16[32,4,32,128]{3,2,1,0:T(8,128)(2,1)}), bf16[32,4,32,128]{3,2,1,0:T(8,128)(2,1)S(1)}, u32[]{:S(2)}, u32[]{:S(2)}) %all-to-all-start) | async-done | bytes 1048608 | tf_op jit(solution)/shard_map/all_to_all | solution.py:422
  31.3 0.0 copy-start.2
  31.3 4.6 %all-to-all-start.1 = ((bf16[32,5,32,128]{3,2,1,0:T(8,128)(2,1)}), bf16[32,5,32,128]{3,2,1,0:T(8,128)(2,1)}, u32[]{:S(2)}, u32[]{:S(2)}) async-start(bf16[32,5,32,128]{3,2,1,0:T(8,128)(2,1)} %gate.2), calls=%async_computation.1 | async-start | bytes 2621440 | tf_op jit(solution)/shard_map/all_to_all | solution.py:422
  35.9 1.9 %collective-permute-start.1 = (bf16[32,4,32,128]{3,2,1,0:T(8,128)(2,1)S(1)}, bf16[32,4,32,128]{3,2,1,0:T(8,128)(2,1)}, u32[]{:S(2)}, u32[]{:S(2)}) collective-permute-start(bf16[32,4,32,128]{3,2,1,0:T(8,128)(2,1)S(1)} %all-to-all-done.refs_1_.own_ref), channel_id=1, source_target_pairs={{0,32},{32,64},{64,96},{96,128},{128,160},{160,192},{192,224},{224... | collective-permute-start | bytes 3145736 | tf_op jit(solution)/shard_map/ppermute | solution.py:425
  37.9 0.0 copy-done.2
  37.9 1.0 cut.2.refs_0_
  38.9 16.9 %all-to-all-done.1 = bf16[32,5,32,128]{3,2,1,0:T(8,128)(2,1)} async-done(((bf16[32,5,32,128]{3,2,1,0:T(8,128)(2,1)}), bf16[32,5,32,128]{3,2,1,0:T(8,128)(2,1)}, u32[]{:S(2)}, u32[]{:S(2)}) %all-to-all-start.1) | async-done | bytes 1310752 | tf_op jit(solution)/shard_map/all_to_all | solution.py:422
  55.8 1.3 %fusion = (bf16[32,2,32,128]{3,2,1,0:T(8,128)(2,1)S(1)}, bf16[32,2,32,128]{3,2,1,0:T(8,128)(2,1)S(1)}) fusion(bf16[32,5,32,128]{3,2,1,0:T(8,128)(2,1)} %all-to-all-done.1), kind=kLoop, calls=%fused_computation | loop fusion | bytes 2097152 | tf_op jit(solution)/shard_map/slice | solution.py:441
  57.1 4.0 %all-to-all-start.2 = ((bf16[32,3,32,128]{3,2,1,0:T(8,128)(2,1)}), bf16[32,3,32,128]{3,2,1,0:T(8,128)(2,1)S(1)}, u32[]{:S(2)}, u32[]{:S(2)}) async-start(bf16[32,3,32,128]{3,2,1,0:T(8,128)(2,1)} %gate.3), calls=%async_computation.2 | async-start | bytes 1572864 | tf_op jit(solution)/shard_map/all_to_all | solution.py:422
  61.1 1.9 %collective-permute-start.2 = (bf16[32,2,32,128]{3,2,1,0:T(8,128)(2,1)S(1)}, bf16[32,2,32,128]{3,2,1,0:T(8,128)(2,1)S(1)}, u32[]{:S(2)}, u32[]{:S(2)}) collective-permute-start(bf16[32,2,32,128]{3,2,1,0:T(8,128)(2,1)S(1)} %get-tuple-element.14.refs_1_.own_ref), channel_id=1, source_target_pairs={{0,32},{32,64},{64,96},{96,128},{128,160},{160,192},{192,224},{224... | collective-permute-start | bytes 1572872 | tf_op jit(solution)/shard_map/ppermute | solution.py:425
  63.0 0.5 collective-permute-done.1.up_ref.kv_ref
  63.5 2.0 %ahead.2 = bf16[2,1056,128]{2,1,0:T(8,128)(2,1)} custom-call(s32[4]{0:T(128)S(1)} %flags.1.refs_2_.flags_ref, bf16[32,2,32,128]{3,2,1,0:T(8,128)(2,1)S(1)} %get-tuple-element.13.q_ref, bf16[32,4,32,128]{3,2,1,0:T(8,128)(2,1)} %collective-permute-done.1.up_ref.kv_ref), custom_call_target="tpu_custom_call" | custom-call | flops 1073741824 | bytes 2097152 | tf_op jit(solution)/shard_map/ahead/pallas_call | solution.py:263
  65.6 4.9 %collective-permute-start.3 = (bf16[2,1056,128]{2,1,0:T(8,128)(2,1)}, bf16[2,1056,128]{2,1,0:T(8,128)(2,1)S(1)}, u32[]{:S(2)}, u32[]{:S(2)}) collective-permute-start(bf16[2,1056,128]{2,1,0:T(8,128)(2,1)} %ahead.2), channel_id=1, source_target_pairs={{0,32},{32,64},{64,96},{96,128},{128,160},{160,192},{192,224},{224... | collective-permute-start | bytes 1622024 | tf_op jit(solution)/shard_map/ppermute | solution.py:425
  70.4 1.0 slice.14.q_ref
  71.4 5.9 %collective-permute-done.2.up_ref.kv_ref = bf16[32,2,32,128]{3,2,1,0:T(8,128)(2,1)S(1)} collective-permute-done((bf16[32,2,32,128]{3,2,1,0:T(8,128)(2,1)S(1)}, bf16[32,2,32,128]{3,2,1,0:T(8,128)(2,1)S(1)}, u32[]{:S(2)}, u32[]{:S(2)}) %collective-permute-start.2) | collective-permute-done | bytes 524320 | tf_op jit(solution)/shard_map/ppermute | solution.py:425
  77.3 0.0 copy-start.3
  77.3 0.6 ahead.3
  77.9 0.2 copy-done.3
  78.1 2.4 %collective-permute-start.4 = (bf16[1,1056,128]{2,1,0:T(8,128)(2,1)S(1)}, bf16[1,1056,128]{2,1,0:T(8,128)(2,1)S(1)}, u32[]{:S(2)}, u32[]{:S(2)}) collective-permute-start(bf16[1,1056,128]{2,1,0:T(8,128)(2,1)S(1)} %ahead.3), channel_id=1, source_target_pairs={{0,32},{32,64},{64,96},{96,128},{128,160},{160,192},{192,224},{224... | collective-permute-start | bytes 811016 | tf_op jit(solution)/shard_map/ppermute | solution.py:425
  80.5 0.0 all-to-all-done.2.q_ref
  80.6 0.0 copy-start.4
  80.6 1.0 copy-done.4
  81.6 1.7 %near.3 = (f32[1,1024,128]{2,1,0:T(8,128)S(1)}, f32[1,8,128]{2,1,0:T(8,128)S(1)}) custom-call(s32[4]{0:T(128)S(1)} %flags.1.refs_2_.flags_ref, bf16[32,3,32,128]{3,2,1,0:T(8,128)(2,1)S(1)} %all-to-all-done.2.q_ref, bf16[32,2,32,128]{3,2,1,0:T(8,128)(2,1)S(1)} %get-tuple-element.14.refs_1_.own_ref, bf16[32,2,32,128]{3,2,1,0:T(8,128)(2,1)S(1)} %copy-done.4), custom_call_target="tpu_custom_call" | custom-call | flops 858993472 | bytes 1835008 | tf_op jit(solution)/shard_map/near/pallas_call | solution.py:276
  83.3 3.8 %near.2 = (f32[2,1024,128]{2,1,0:T(8,128)S(1)}, f32[2,8,128]{2,1,0:T(8,128)S(1)}) custom-call(s32[4]{0:T(128)S(1)} %flags.1.refs_2_.flags_ref, bf16[32,3,32,128]{3,2,1,0:T(8,128)(2,1)S(1)} %all-to-all-done.2.q_ref, bf16[32,4,32,128]{3,2,1,0:T(8,128)(2,1)S(1)} %all-to-all-done.refs_1_.own_ref, bf16[32,4,32,128]{3,2,1,0:T(8,128)(2,1)} %collective-permute-done.1.up_ref.kv_ref), custom_call_target="tpu_custom_call" | custom-call | flops 1717986944 | bytes 3670016 | tf_op jit(solution)/shard_map/near/pallas_call | solution.py:276
  87.1 1.8 %collective-permute-done.3.far_a = bf16[2,1056,128]{2,1,0:T(8,128)(2,1)S(1)} collective-permute-done((bf16[2,1056,128]{2,1,0:T(8,128)(2,1)}, bf16[2,1056,128]{2,1,0:T(8,128)(2,1)S(1)}, u32[]{:S(2)}, u32[]{:S(2)}) %collective-permute-start.3) | collective-permute-done | bytes 540704 | tf_op jit(solution)/shard_map/ppermute | solution.py:425
  88.9 5.8 %collective-permute-done.4.far_b = bf16[1,1056,128]{2,1,0:T(8,128)(2,1)S(1)} collective-permute-done((bf16[1,1056,128]{2,1,0:T(8,128)(2,1)S(1)}, bf16[1,1056,128]{2,1,0:T(8,128)(2,1)S(1)}, u32[]{:S(2)}, u32[]{:S(2)}) %collective-permute-start.4) | collective-permute-done | bytes 270368 | tf_op jit(solution)/shard_map/ppermute | solution.py:425
  94.7 0.6 merge.1
  95.3 22.7 %all_to_all.20.in_ref = bf16[32,3,32,128]{3,2,1,0:T(8,128)(2,1)S(1)} all-to-all(bf16[32,3,32,128]{3,2,1,0:T(8,128)(2,1)S(1)} %merge.1), channel_id=1, replica_groups=mesh['grp'=16,'ctx'=32] {'ctx'}, dimensions={0} | all-to-all | bytes 1572864 | tf_op jit(solution)/shard_map/all_to_all | solution.py:422
  118.0 1.0 paste.1
  (2 shorter events, 0.0 us)
Async XLA Ops:
  0.0 20.6 %collective-permute-start = (bf16[256,1536]{1,0:T(8,128)(2,1)}, bf16[256,1536]{1,0:T(8,128)(2,1)}, u32[]{:S(2)}, u32[]{:S(2)}) collective-permute-start(bf16[256,1536]{1,0:T(8,128)(2,1)} %refs_0_.2), channel_id=1, source_target_pairs={{32,0},{64,32},{96,64},{128,96},{160,128},{192,160},{224,192},{256... | collective-permute-start | bytes 2359304 | tf_op jit(solution)/shard_map/ppermute | solution.py:428
  6.2 8.2 %copy-start.6 = (s32[16,8]{0,1:T(8,128)S(1)}, s32[16,8]{0,1:T(8,128)}, u32[]{:S(2)}) copy-start(s32[16,8]{0,1:T(8,128)} %param.9) | copy-start | bytes 1540
  6.2 8.3 %copy-start.5 = (s32[16,8,2]{0,2,1:T(2,128)S(1)}, s32[16,8,2]{0,2,1:T(2,128)}, u32[]{:S(2)}) copy-start(s32[16,8,2]{0,2,1:T(2,128)} %param.8) | copy-start | bytes 3076
  6.2 14.4 %copy-start = (bf16[256,1536]{1,0:T(8,128)(2,1)S(1)}, bf16[256,1536]{1,0:T(8,128)(2,1)}, u32[]{:S(2)}) copy-start(bf16[256,1536]{1,0:T(8,128)(2,1)} %k_ref.1) | copy-start | bytes 2359300
  6.2 14.4 %copy-start.1 = (bf16[256,1536]{1,0:T(8,128)(2,1)S(1)}, bf16[256,1536]{1,0:T(8,128)(2,1)}, u32[]{:S(2)}) copy-start(bf16[256,1536]{1,0:T(8,128)(2,1)} %v_ref.1) | copy-start | bytes 2359300
  6.2 25.1 %all-to-all-start = ((bf16[32,4,32,128]{3,2,1,0:T(8,128)(2,1)}), bf16[32,4,32,128]{3,2,1,0:T(8,128)(2,1)S(1)}, u32[]{:S(2)}, u32[]{:S(2)}) async-start(bf16[32,4,32,128]{3,2,1,0:T(8,128)(2,1)} %cut_first.1), calls=%async_computation | async-start | bytes 2097152 | tf_op jit(solution)/shard_map/all_to_all | solution.py:422
  31.3 6.5 %copy-start.2 = (bf16[256,1536]{1,0:T(8,128)(2,1)S(1)}, bf16[256,1536]{1,0:T(8,128)(2,1)}, u32[]{:S(2)}) copy-start(bf16[256,1536]{1,0:T(8,128)(2,1)} %refs_0_.2) | copy-start | bytes 2359300
  31.3 24.5 %all-to-all-start.1 = ((bf16[32,5,32,128]{3,2,1,0:T(8,128)(2,1)}), bf16[32,5,32,128]{3,2,1,0:T(8,128)(2,1)}, u32[]{:S(2)}, u32[]{:S(2)}) async-start(bf16[32,5,32,128]{3,2,1,0:T(8,128)(2,1)} %gate.2), calls=%async_computation.1 | async-start | bytes 2621440 | tf_op jit(solution)/shard_map/all_to_all | solution.py:422
  35.9 27.6 %collective-permute-start.1 = (bf16[32,4,32,128]{3,2,1,0:T(8,128)(2,1)S(1)}, bf16[32,4,32,128]{3,2,1,0:T(8,128)(2,1)}, u32[]{:S(2)}, u32[]{:S(2)}) collective-permute-start(bf16[32,4,32,128]{3,2,1,0:T(8,128)(2,1)S(1)} %all-to-all-done.refs_1_.own_ref), channel_id=1, source_target_pairs={{0,32},{32,64},{64,96},{96,128},{128,160},{160,192},{192,224},{224... | collective-permute-start | bytes 3145736 | tf_op jit(solution)/shard_map/ppermute | solution.py:425
  57.1 23.4 %all-to-all-start.2 = ((bf16[32,3,32,128]{3,2,1,0:T(8,128)(2,1)}), bf16[32,3,32,128]{3,2,1,0:T(8,128)(2,1)S(1)}, u32[]{:S(2)}, u32[]{:S(2)}) async-start(bf16[32,3,32,128]{3,2,1,0:T(8,128)(2,1)} %gate.3), calls=%async_computation.2 | async-start | bytes 1572864 | tf_op jit(solution)/shard_map/all_to_all | solution.py:422
  61.1 16.3 %collective-permute-start.2 = (bf16[32,2,32,128]{3,2,1,0:T(8,128)(2,1)S(1)}, bf16[32,2,32,128]{3,2,1,0:T(8,128)(2,1)S(1)}, u32[]{:S(2)}, u32[]{:S(2)}) collective-permute-start(bf16[32,2,32,128]{3,2,1,0:T(8,128)(2,1)S(1)} %get-tuple-element.14.refs_1_.own_ref), channel_id=1, source_target_pairs={{0,32},{32,64},{64,96},{96,128},{128,160},{160,192},{192,224},{224... | collective-permute-start | bytes 1572872 | tf_op jit(solution)/shard_map/ppermute | solution.py:425
  65.6 23.4 %collective-permute-start.3 = (bf16[2,1056,128]{2,1,0:T(8,128)(2,1)}, bf16[2,1056,128]{2,1,0:T(8,128)(2,1)S(1)}, u32[]{:S(2)}, u32[]{:S(2)}) collective-permute-start(bf16[2,1056,128]{2,1,0:T(8,128)(2,1)} %ahead.2), channel_id=1, source_target_pairs={{0,32},{32,64},{64,96},{96,128},{128,160},{160,192},{192,224},{224... | collective-permute-start | bytes 1622024 | tf_op jit(solution)/shard_map/ppermute | solution.py:425
  77.3 0.8 copy-start.3
  78.1 16.6 %collective-permute-start.4 = (bf16[1,1056,128]{2,1,0:T(8,128)(2,1)S(1)}, bf16[1,1056,128]{2,1,0:T(8,128)(2,1)S(1)}, u32[]{:S(2)}, u32[]{:S(2)}) collective-permute-start(bf16[1,1056,128]{2,1,0:T(8,128)(2,1)S(1)} %ahead.3), channel_id=1, source_target_pairs={{0,32},{32,64},{64,96},{96,128},{128,160},{160,192},{192,224},{224... | collective-permute-start | bytes 811016 | tf_op jit(solution)/shard_map/ppermute | solution.py:425
  80.6 1.0 copy-start.4

commit v3 on v2

--- a/solution.py
+++ b/solution.py
@@ -258,7 +258,7 @@
     )
 
 
-def attend_ahead(flags, query, pair):
+def attend_ahead(flags, query, pair, flops):
     rows, heads = pair.shape[0] * POSITIONS, pair.shape[1] // 2
     return pl.pallas_call(
         ahead_kernel,
@@ -266,7 +266,7 @@
         out_specs=VMEM,
         out_shape=jax.ShapeDtypeStruct((heads, rows + STAT_ROWS, HD), jnp.bfloat16),
         compiler_params=PARAMS,
-        cost_estimate=cost(1, rows, heads, rows * heads * HD * 8),
+        cost_estimate=pl.CostEstimate(flops=flops, bytes_accessed=2**20, transcendentals=0),
         name="ahead",
     )(flags, query, pair)
 
@@ -372,14 +372,14 @@
                 out_ref[window * SPAN + part, slab] = sources[source][rows, lanes]
 
 
-def cut(sources, slabs):
+def cut(sources, slabs, flops):
     return pl.pallas_call(
         functools.partial(cut_kernel, slabs),
         in_specs=[VMEM] * len(sources),
         out_specs=VMEM,
         out_shape=jax.ShapeDtypeStruct((NWIN * SPAN, len(slabs), POSITIONS, HD), jnp.bfloat16),
         compiler_params=PARAMS,
-        cost_estimate=pl.CostEstimate(flops=10**11, bytes_accessed=2**22, transcendentals=0),
+        cost_estimate=pl.CostEstimate(flops=flops, bytes_accessed=2**21, transcendentals=0),
         name="cut",
     )(*sources)
 
@@ -432,16 +432,17 @@
     first_up = up(first)
     flags = make_flags(chosen_groups, chosen_count)
     second = cut(
-        (key_vectors, value_vectors, later_query), ((0, 2), (1, 2), (2, 0), (2, 1), (2, 2))
+        (key_vectors, value_vectors, later_query), ((0, 2), (1, 2), (2, 0), (2, 1)), 10**11
     )
+    third = cut((query_vectors, later_query), ((0, 0), (0, 1), (0, 2), (1, 2)), 10**6)
     second = to_peers(gate(second, first, flags))
     second_pair = second[:, 0:2]
     second_up = up(second_pair)
-    query = to_peers(gate(cut((query_vectors,), ((0, 0), (0, 1), (0, 2))), second_pair))
-    first_far = up(attend_ahead(flags, second[:, 2:4], first_up))
-    second_far = up(attend_ahead(flags, second[:, 4:5], second_up))
-    near_a, log_a = attend_near(flags, query, 0, first, first_up)
-    near_b, log_b = attend_near(flags, query, 2, second_pair, second_up)
+    third = to_peers(gate(third, second_pair))
+    first_far = up(attend_ahead(flags, second[:, 2:4], first_up, 10**6))
+    second_far = up(attend_ahead(flags, third[:, 3:4], second_up, 10**11))
+    near_a, log_a = attend_near(flags, third, 0, first, first_up)
+    near_b, log_b = attend_near(flags, third, 2, second_pair, second_up)
     merged = merge(flags, (near_a, near_b), (log_a, log_b), (first_far, second_far))
     return paste(to_peers(merged))
 

time: 120 us -> 119 us (level)
  Pallas kernels: 17.8 us -> 23.2 us
  waiting for transfers between devices: 42.9 us -> 39.2 us
  local copies, waits for them, and re-layouts: 3.75 us -> 2.07 us
    ppermute x4, waiting for transfers between devices: 14 us -> 8.73 us  [up(): lax.ppermute(block, 'grp', [(at, at + 1) for at in range(group_devices -...]
    pallas_call x2, Pallas kernels: 5.52 us -> 10.4 us  [attend_near(): pl.pallas_call(functools.partial(near_kernel, query_slab), in_specs=[SMEM...]
    all_to_all x3, waiting for transfers between devices: 25.2 us -> 27.5 us  [to_peers(): return lax.all_to_all(block, 'ctx', split_axis=0, concat_axis=0, tiled=True)]
  transfers between devices with their start and end apart: 8 -> 8, of which waited for: 7 -> 7; matrix products, arithmetic and copies ran while one was open for 2% -> 1% of each run, Pallas kernels for 14% -> 17%
where the time goes in v3:
time: 119 us; the launch traced here: 118 us
  waiting for transfers between devices  39.2 us (33%)
  starting transfers between devices  31.2 us (26%)
  Pallas kernels  23.2 us (19%)
  blocking collectives  21.7 us (18%)
  local copies, waits for them, and re-layouts  2.07 us (2%)
    all_to_all x3, waiting for transfers between devices, to_peers(): return lax.all_to_all(block, 'ctx', split_axis=0, concat_axis=0, tiled=True)  27.5 us
    all_to_all x1, blocking collectives, to_peers(): return lax.all_to_all(block, 'ctx', split_axis=0, concat_axis=0, tiled=True)  21.7 us
    all_to_all x3, starting transfers between devices, to_peers(): return lax.all_to_all(block, 'ctx', split_axis=0, concat_axis=0, tiled=True)  16.7 us
    ppermute x4, starting transfers between devices, up(): lax.ppermute(block, 'grp', [(at, at + 1) for at in range(group_devices -...  10.6 us
    pallas_call x2, Pallas kernels, attend_near(): pl.pallas_call(functools.partial(near_kernel, query_slab), in_specs=[SMEM...  10.4 us
    ppermute x4, waiting for transfers between devices, up(): lax.ppermute(block, 'grp', [(at, at + 1) for at in range(group_devices -...  8.73 us
    ppermute x1, starting transfers between devices, down(): lax.ppermute(block, 'grp', [(at + 1, at) for at in range(group_devices -...  3.84 us
    pallas_call x2, Pallas kernels, attend_ahead(): pl.pallas_call(ahead_kernel, in_specs=[SMEM] + [VMEM] * 2, out_specs=VMEM...  3.11 us
  transfers between devices with their start and end apart: 8, of which 7 were waited for; matrix products, arithmetic and copies ran while one was open for 1% of the time, Pallas kernels for 17%

profile of v3, /device:TPU:385, one launch (start us, length us, event | category | flops | bytes accessed | tf_op | source)
XLA Modules:
  0.0 117.7 jit_solution(3761285407551776388)
XLA Ops:
  0.0 3.8 %collective-permute-start = (bf16[256,1536]{1,0:T(8,128)(2,1)}, bf16[256,1536]{1,0:T(8,128)(2,1)S(1)}, u32[]{:S(2)}, u32[]{:S(2)}) collective-permute-start(bf16[256,1536]{1,0:T(8,128)(2,1)} %refs_0_.2), channel_id=1, source_target_pairs={{32,0},{64,32},{96,64},{128,96},{160,128},{192,160},{224,192},{256... | collective-permute-start | bytes 2359304 | tf_op jit(solution)/shard_map/ppermute | solution.py:428
  3.8 2.3 %cut_first.1 = bf16[32,4,32,128]{3,2,1,0:T(8,128)(2,1)} custom-call(bf16[256,1536]{1,0:T(8,128)(2,1)} %k_ref.1, bf16[256,1536]{1,0:T(8,128)(2,1)} %v_ref.1), custom_call_target="tpu_custom_call" | custom-call | tf_op jit(solution)/shard_map/cut_first/pallas_call | solution.py:333
  6.2 0.0 copy-start.3
  6.2 0.0 copy-start
  6.2 0.0 copy-start.1
  6.2 8.2 %all-to-all-start = ((bf16[32,4,32,128]{3,2,1,0:T(8,128)(2,1)}), bf16[32,4,32,128]{3,2,1,0:T(8,128)(2,1)S(1)}, u32[]{:S(2)}, u32[]{:S(2)}) async-start(bf16[32,4,32,128]{3,2,1,0:T(8,128)(2,1)} %cut_first.1), calls=%async_computation | async-start | bytes 2097152 | tf_op jit(solution)/shard_map/all_to_all | solution.py:422
  14.4 0.0 copy-done.3
  14.4 0.0 copy-start.4
  14.4 0.1 copy.8.groups_ref
  14.6 0.5 copy-done.4
  15.1 0.1 copy.9.count_ref
  15.2 2.4 %flags.1.refs_2_.flags_ref = s32[4]{0:T(128)S(1)} custom-call(s32[16,8,2]{2,1,0:T(8,128)S(1)} %copy.8.groups_ref, s32[16,8]{1,0:T(8,128)S(1)} %copy.9.count_ref), custom_call_target="tpu_custom_call" | custom-call | tf_op jit(solution)/shard_map/flags/pallas_call | solution.py:52
  17.6 2.9 %collective-permute-done.refs_1_.refs_2_ = bf16[256,1536]{1,0:T(8,128)(2,1)S(1)} collective-permute-done((bf16[256,1536]{1,0:T(8,128)(2,1)}, bf16[256,1536]{1,0:T(8,128)(2,1)S(1)}, u32[]{:S(2)}, u32[]{:S(2)}) %collective-permute-start) | collective-permute-done | bytes 786464 | tf_op jit(solution)/shard_map/ppermute | solution.py:428
  20.5 0.0 copy-done
  20.5 0.0 copy-done.1
  20.5 1.2 %cut.3.refs_0_ = bf16[32,4,32,128]{3,2,1,0:T(8,128)(2,1)} custom-call(bf16[256,1536]{1,0:T(8,128)(2,1)S(1)} %copy-done, bf16[256,1536]{1,0:T(8,128)(2,1)S(1)} %copy-done.1, bf16[256,1536]{1,0:T(8,128)(2,1)S(1)} %collective-permute-done.refs_1_.refs_2_), custom_call_target="tpu_custom_call" | custom-call | flops 99999997952 | bytes 2097152 | tf_op jit(solution)/shard_map/cut/pallas_call | solution.py:376
  21.7 9.6 %all-to-all-done.refs_1_.own_ref = bf16[32,4,32,128]{3,2,1,0:T(8,128)(2,1)S(1)} async-done(((bf16[32,4,32,128]{3,2,1,0:T(8,128)(2,1)}), bf16[32,4,32,128]{3,2,1,0:T(8,128)(2,1)S(1)}, u32[]{:S(2)}, u32[]{:S(2)}) %all-to-all-start) | async-done | bytes 1048608 | tf_op jit(solution)/shard_map/all_to_all | solution.py:422
  31.3 0.0 copy-start.2
  31.3 4.6 %all-to-all-start.1 = ((bf16[32,4,32,128]{3,2,1,0:T(8,128)(2,1)}), bf16[32,4,32,128]{3,2,1,0:T(8,128)(2,1)}, u32[]{:S(2)}, u32[]{:S(2)}) async-start(bf16[32,4,32,128]{3,2,1,0:T(8,128)(2,1)} %gate.2), calls=%async_computation.1 | async-start | bytes 2097152 | tf_op jit(solution)/shard_map/all_to_all | solution.py:422
  35.9 0.0 copy-done.2
  35.9 1.2 %cut.2.refs_0_ = bf16[32,4,32,128]{3,2,1,0:T(8,128)(2,1)} custom-call(bf16[256,1536]{1,0:T(8,128)(2,1)S(1)} %copy-done.2, bf16[256,1536]{1,0:T(8,128)(2,1)S(1)} %collective-permute-done.refs_1_.refs_2_), custom_call_target="tpu_custom_call" | custom-call | flops 1000000 | bytes 2097152 | tf_op jit(solution)/shard_map/cut/pallas_call | solution.py:376
  37.1 1.9 %collective-permute-start.1 = (bf16[32,4,32,128]{3,2,1,0:T(8,128)(2,1)S(1)}, bf16[32,4,32,128]{3,2,1,0:T(8,128)(2,1)}, u32[]{:S(2)}, u32[]{:S(2)}) collective-permute-start(bf16[32,4,32,128]{3,2,1,0:T(8,128)(2,1)S(1)} %all-to-all-done.refs_1_.own_ref), channel_id=1, source_target_pairs={{0,32},{32,64},{64,96},{96,128},{128,160},{160,192},{192,224},{224... | collective-permute-start | bytes 3145736 | tf_op jit(solution)/shard_map/ppermute | solution.py:425
  39.0 13.9 %all-to-all-done.1 = bf16[32,4,32,128]{3,2,1,0:T(8,128)(2,1)} async-done(((bf16[32,4,32,128]{3,2,1,0:T(8,128)(2,1)}), bf16[32,4,32,128]{3,2,1,0:T(8,128)(2,1)}, u32[]{:S(2)}, u32[]{:S(2)}) %all-to-all-start.1) | async-done | bytes 1048608 | tf_op jit(solution)/shard_map/all_to_all | solution.py:422
  52.9 1.3 %fusion = (bf16[32,2,32,128]{3,2,1,0:T(8,128)(2,1)S(1)}, bf16[32,2,32,128]{3,2,1,0:T(8,128)(2,1)S(1)}) fusion(bf16[32,4,32,128]{3,2,1,0:T(8,128)(2,1)} %all-to-all-done.1), kind=kLoop, calls=%fused_computation | loop fusion | bytes 2097152 | tf_op jit(solution)/shard_map/slice | solution.py:442
  54.2 3.9 %all-to-all-start.2 = ((bf16[32,4,32,128]{3,2,1,0:T(8,128)(2,1)}), bf16[32,4,32,128]{3,2,1,0:T(8,128)(2,1)S(1)}, u32[]{:S(2)}, u32[]{:S(2)}) async-start(bf16[32,4,32,128]{3,2,1,0:T(8,128)(2,1)} %gate.3), calls=%async_computation.2 | async-start | bytes 2097152 | tf_op jit(solution)/shard_map/all_to_all | solution.py:422
  58.1 1.9 %collective-permute-start.2 = (bf16[32,2,32,128]{3,2,1,0:T(8,128)(2,1)S(1)}, bf16[32,2,32,128]{3,2,1,0:T(8,128)(2,1)}, u32[]{:S(2)}, u32[]{:S(2)}) collective-permute-start(bf16[32,2,32,128]{3,2,1,0:T(8,128)(2,1)S(1)} %get-tuple-element.14.refs_1_.own_ref), channel_id=1, source_target_pairs={{0,32},{32,64},{64,96},{96,128},{128,160},{160,192},{192,224},{224... | collective-permute-start | bytes 1572872 | tf_op jit(solution)/shard_map/ppermute | solution.py:425
  60.1 4.6 %collective-permute-done.1.up_ref.kv_ref = bf16[32,4,32,128]{3,2,1,0:T(8,128)(2,1)} collective-permute-done((bf16[32,4,32,128]{3,2,1,0:T(8,128)(2,1)S(1)}, bf16[32,4,32,128]{3,2,1,0:T(8,128)(2,1)}, u32[]{:S(2)}, u32[]{:S(2)}) %collective-permute-start.1) | collective-permute-done | bytes 1048608 | tf_op jit(solution)/shard_map/ppermute | solution.py:425
  64.7 2.0 %ahead.2 = bf16[2,1056,128]{2,1,0:T(8,128)(2,1)} custom-call(s32[4]{0:T(128)S(1)} %flags.1.refs_2_.flags_ref, bf16[32,2,32,128]{3,2,1,0:T(8,128)(2,1)S(1)} %get-tuple-element.13.q_ref, bf16[32,4,32,128]{3,2,1,0:T(8,128)(2,1)} %collective-permute-done.1.up_ref.kv_ref), custom_call_target="tpu_custom_call" | custom-call | flops 1000000 | bytes 1048576 | tf_op jit(solution)/shard_map/ahead/pallas_call | solution.py:263
  66.8 4.2 %collective-permute-start.3 = (bf16[2,1056,128]{2,1,0:T(8,128)(2,1)}, bf16[2,1056,128]{2,1,0:T(8,128)(2,1)}, u32[]{:S(2)}, u32[]{:S(2)}) collective-permute-start(bf16[2,1056,128]{2,1,0:T(8,128)(2,1)} %ahead.2), channel_id=1, source_target_pairs={{0,32},{32,64},{64,96},{96,128},{128,160},{160,192},{192,224},{224... | collective-permute-start | bytes 1622024 | tf_op jit(solution)/shard_map/ppermute | solution.py:425
  71.0 4.0 %all-to-all-done.2.q_ref = bf16[32,4,32,128]{3,2,1,0:T(8,128)(2,1)S(1)} async-done(((bf16[32,4,32,128]{3,2,1,0:T(8,128)(2,1)}), bf16[32,4,32,128]{3,2,1,0:T(8,128)(2,1)S(1)}, u32[]{:S(2)}, u32[]{:S(2)}) %all-to-all-start.2) | async-done | bytes 1048608 | tf_op jit(solution)/shard_map/all_to_all | solution.py:422
  75.1 0.9 collective-permute-done.2.up_ref.kv_ref
  75.9 1.1 ahead.3
  77.0 2.6 %collective-permute-start.4 = (bf16[1,1056,128]{2,1,0:T(8,128)(2,1)S(1)}, bf16[1,1056,128]{2,1,0:T(8,128)(2,1)S(1)}, u32[]{:S(2)}, u32[]{:S(2)}) collective-permute-start(bf16[1,1056,128]{2,1,0:T(8,128)(2,1)S(1)} %ahead.3), channel_id=1, source_target_pairs={{0,32},{32,64},{64,96},{96,128},{128,160},{160,192},{192,224},{224... | collective-permute-start | bytes 811016 | tf_op jit(solution)/shard_map/ppermute | solution.py:425
  79.6 3.7 %near.3 = (f32[1,1024,128]{2,1,0:T(8,128)S(1)}, f32[1,8,128]{2,1,0:T(8,128)S(1)}) custom-call(s32[4]{0:T(128)S(1)} %flags.1.refs_2_.flags_ref, bf16[32,4,32,128]{3,2,1,0:T(8,128)(2,1)S(1)} %all-to-all-done.2.q_ref, bf16[32,2,32,128]{3,2,1,0:T(8,128)(2,1)S(1)} %get-tuple-element.14.refs_1_.own_ref, bf16[32,2,32,128]{3,2,1,0:T(8,128)(2,1)} %collective-permute-done.2.up_ref.kv_ref), custom_call_target="tpu_custom_call" | custom-call | flops 858993472 | bytes 1835008 | tf_op jit(solution)/shard_map/near/pallas_call | solution.py:276
  83.3 6.7 %near.2 = (f32[2,1024,128]{2,1,0:T(8,128)S(1)}, f32[2,8,128]{2,1,0:T(8,128)S(1)}) custom-call(s32[4]{0:T(128)S(1)} %flags.1.refs_2_.flags_ref, bf16[32,4,32,128]{3,2,1,0:T(8,128)(2,1)S(1)} %all-to-all-done.2.q_ref, bf16[32,4,32,128]{3,2,1,0:T(8,128)(2,1)S(1)} %all-to-all-done.refs_1_.own_ref, bf16[32,4,32,128]{3,2,1,0:T(8,128)(2,1)} %collective-permute-done.1.up_ref.kv_ref), custom_call_target="tpu_custom_call" | custom-call | flops 1717986944 | bytes 3670016 | tf_op jit(solution)/shard_map/near/pallas_call | solution.py:276
  90.0 0.0 collective-permute-done.3.far_a
  90.0 3.2 %collective-permute-done.4.far_b = bf16[1,1056,128]{2,1,0:T(8,128)(2,1)S(1)} collective-permute-done((bf16[1,1056,128]{2,1,0:T(8,128)(2,1)S(1)}, bf16[1,1056,128]{2,1,0:T(8,128)(2,1)S(1)}, u32[]{:S(2)}, u32[]{:S(2)}) %collective-permute-start.4) | collective-permute-done | bytes 270368 | tf_op jit(solution)/shard_map/ppermute | solution.py:425
  93.2 1.7 %merge.1 = bf16[32,3,32,128]{3,2,1,0:T(8,128)(2,1)S(1)} custom-call(s32[4]{0:T(128)S(1)} %flags.1.refs_2_.flags_ref, f32[2,1024,128]{2,1,0:T(8,128)S(1)} %get-tuple-element.9.near_a, f32[1,1024,128]{2,1,0:T(8,128)S(1)} %get-tuple-element.10.near_b, f32[2,8,128]{2,1,0:T(8,128)S(1)} %get-tuple-element.11.log_a, f32[1,8,128]{2,1,0:T(8,128)S(1)} %get-tuple-element.12.log_b, ...), custom_call_target="tpu_custom_call" | custom-call | bytes 3145728 | tf_op jit(solution)/shard_map/merge/pallas_call | solution.py:292
  94.9 21.7 %all_to_all.20.in_ref = bf16[32,3,32,128]{3,2,1,0:T(8,128)(2,1)S(1)} all-to-all(bf16[32,3,32,128]{3,2,1,0:T(8,128)(2,1)S(1)} %merge.1), channel_id=1, replica_groups=mesh['grp'=16,'ctx'=32] {'ctx'}, dimensions={0} | all-to-all | bytes 1572864 | tf_op jit(solution)/shard_map/all_to_all | solution.py:422
  116.6 1.0 paste.1
  (3 shorter events, 0.0 us)
Async XLA Ops:
  0.0 20.5 %collective-permute-start = (bf16[256,1536]{1,0:T(8,128)(2,1)}, bf16[256,1536]{1,0:T(8,128)(2,1)S(1)}, u32[]{:S(2)}, u32[]{:S(2)}) collective-permute-start(bf16[256,1536]{1,0:T(8,128)(2,1)} %refs_0_.2), channel_id=1, source_target_pairs={{32,0},{64,32},{96,64},{128,96},{160,128},{192,160},{224,192},{256... | collective-permute-start | bytes 2359304 | tf_op jit(solution)/shard_map/ppermute | solution.py:428
  6.2 8.2 %copy-start.3 = (s32[16,8,2]{0,2,1:T(2,128)S(1)}, s32[16,8,2]{0,2,1:T(2,128)}, u32[]{:S(2)}) copy-start(s32[16,8,2]{0,2,1:T(2,128)} %param.8) | copy-start | bytes 3076
  6.2 14.3 %copy-start = (bf16[256,1536]{1,0:T(8,128)(2,1)S(1)}, bf16[256,1536]{1,0:T(8,128)(2,1)}, u32[]{:S(2)}) copy-start(bf16[256,1536]{1,0:T(8,128)(2,1)} %k_ref.1) | copy-start | bytes 2359300
  6.2 14.3 %copy-start.1 = (bf16[256,1536]{1,0:T(8,128)(2,1)S(1)}, bf16[256,1536]{1,0:T(8,128)(2,1)}, u32[]{:S(2)}) copy-start(bf16[256,1536]{1,0:T(8,128)(2,1)} %v_ref.1) | copy-start | bytes 2359300
  6.2 25.1 %all-to-all-start = ((bf16[32,4,32,128]{3,2,1,0:T(8,128)(2,1)}), bf16[32,4,32,128]{3,2,1,0:T(8,128)(2,1)S(1)}, u32[]{:S(2)}, u32[]{:S(2)}) async-start(bf16[32,4,32,128]{3,2,1,0:T(8,128)(2,1)} %cut_first.1), calls=%async_computation | async-start | bytes 2097152 | tf_op jit(solution)/shard_map/all_to_all | solution.py:422
  14.4 0.7 copy-start.4
  31.3 4.6 %copy-start.2 = (bf16[256,1536]{1,0:T(8,128)(2,1)S(1)}, bf16[256,1536]{1,0:T(8,128)(2,1)}, u32[]{:S(2)}) copy-start(bf16[256,1536]{1,0:T(8,128)(2,1)} %refs_0_.2) | copy-start | bytes 2359300
  31.3 21.6 %all-to-all-start.1 = ((bf16[32,4,32,128]{3,2,1,0:T(8,128)(2,1)}), bf16[32,4,32,128]{3,2,1,0:T(8,128)(2,1)}, u32[]{:S(2)}, u32[]{:S(2)}) async-start(bf16[32,4,32,128]{3,2,1,0:T(8,128)(2,1)} %gate.2), calls=%async_computation.1 | async-start | bytes 2097152 | tf_op jit(solution)/shard_map/all_to_all | solution.py:422
  37.1 27.6 %collective-permute-start.1 = (bf16[32,4,32,128]{3,2,1,0:T(8,128)(2,1)S(1)}, bf16[32,4,32,128]{3,2,1,0:T(8,128)(2,1)}, u32[]{:S(2)}, u32[]{:S(2)}) collective-permute-start(bf16[32,4,32,128]{3,2,1,0:T(8,128)(2,1)S(1)} %all-to-all-done.refs_1_.own_ref), channel_id=1, source_target_pairs={{0,32},{32,64},{64,96},{96,128},{128,160},{160,192},{192,224},{224... | collective-permute-start | bytes 3145736 | tf_op jit(solution)/shard_map/ppermute | solution.py:425
  54.2 20.9 %all-to-all-start.2 = ((bf16[32,4,32,128]{3,2,1,0:T(8,128)(2,1)}), bf16[32,4,32,128]{3,2,1,0:T(8,128)(2,1)S(1)}, u32[]{:S(2)}, u32[]{:S(2)}) async-start(bf16[32,4,32,128]{3,2,1,0:T(8,128)(2,1)} %gate.3), calls=%async_computation.2 | async-start | bytes 2097152 | tf_op jit(solution)/shard_map/all_to_all | solution.py:422
  58.1 17.8 %collective-permute-start.2 = (bf16[32,2,32,128]{3,2,1,0:T(8,128)(2,1)S(1)}, bf16[32,2,32,128]{3,2,1,0:T(8,128)(2,1)}, u32[]{:S(2)}, u32[]{:S(2)}) collective-permute-start(bf16[32,2,32,128]{3,2,1,0:T(8,128)(2,1)S(1)} %get-tuple-element.14.refs_1_.own_ref), channel_id=1, source_target_pairs={{0,32},{32,64},{64,96},{96,128},{128,160},{160,192},{192,224},{224... | collective-permute-start | bytes 1572872 | tf_op jit(solution)/shard_map/ppermute | solution.py:425
  66.8 23.2 %collective-permute-start.3 = (bf16[2,1056,128]{2,1,0:T(8,128)(2,1)}, bf16[2,1056,128]{2,1,0:T(8,128)(2,1)}, u32[]{:S(2)}, u32[]{:S(2)}) collective-permute-start(bf16[2,1056,128]{2,1,0:T(8,128)(2,1)} %ahead.2), channel_id=1, source_target_pairs={{0,32},{32,64},{64,96},{96,128},{128,160},{160,192},{192,224},{224... | collective-permute-start | bytes 1622024 | tf_op jit(solution)/shard_map/ppermute | solution.py:425
  77.0 16.2 %collective-permute-start.4 = (bf16[1,1056,128]{2,1,0:T(8,128)(2,1)S(1)}, bf16[1,1056,128]{2,1,0:T(8,128)(2,1)S(1)}, u32[]{:S(2)}, u32[]{:S(2)}) collective-permute-start(bf16[1,1056,128]{2,1,0:T(8,128)(2,1)S(1)} %ahead.3), channel_id=1, source_target_pairs={{0,32},{32,64},{64,96},{96,128},{128,160},{160,192},{192,224},{224... | collective-permute-start | bytes 811016 | tf_op jit(solution)/shard_map/ppermute | solution.py:425

commit v4 on v2

--- a/solution.py
+++ b/solution.py
@@ -75,9 +75,9 @@
         scores = jnp.concatenate([scores[:, : count - rows], tail], axis=1) if count > rows else tail
     highest = jnp.max(scores, axis=-1, keepdims=True)
     weights = jnp.exp2((scores - highest) * FACTOR)
-    summed = jnp.sum(weights, axis=-1, keepdims=True)
-    blended = jnp.dot(weights.astype(jnp.bfloat16), values, preferred_element_type=jnp.float32)
-    return highest, summed, blended
+    beside = jnp.concatenate([values, jnp.ones_like(values)], axis=1)
+    product = jnp.dot(weights.astype(jnp.bfloat16), beside, preferred_element_type=jnp.float32)
+    return highest, product[:, HD:], product[:, :HD]
 
 
 def in_turn(jobs, done):
@@ -118,7 +118,8 @@
     ]
 
 
-def ahead_kernel(flags_ref, q_ref, kv_ref, out_ref):
+def ahead_kernel(query_slab, pair_slab, flags_ref, q_ref, kv_ref, *rest):
+    out_ref = rest[-1]
     rows = q_ref.shape[0] * POSITIONS
     heads = out_ref.shape[0]
     taken = flags_ref[2] > 0
@@ -127,12 +128,12 @@
     def _():
         @pl.loop(0, heads)
         def _(head):
-            keys = kv_ref[:, 2 * head].reshape(rows, HD)
-            values = kv_ref[:, 2 * head + 1].reshape(rows, HD)
+            keys = kv_ref[:, pair_slab + 2 * head].reshape(rows, HD)
+            values = kv_ref[:, pair_slab + 2 * head + 1].reshape(rows, HD)
 
             def job(start):
                 return (
-                    lambda: score(rows_of(q_ref, head, start, QB), keys),
+                    lambda: score(rows_of(q_ref, query_slab + head, start, QB), keys),
                     lambda scores: soften(scores, values),
                 )
 
@@ -157,7 +158,7 @@
         out_ref[:, pl.ds(rows, STAT_ROWS), :] = jnp.zeros((heads, STAT_ROWS, HD), jnp.bfloat16)
 
 
-def near_kernel(query_slab, flags_ref, q_ref, own_ref, up_ref, out_ref, log_ref):
+def near_kernel(query_slab, own_slab, up_slab, flags_ref, q_ref, own_ref, up_ref, out_ref, log_ref):
     rows = q_ref.shape[0] * POSITIONS
     heads = out_ref.shape[0]
     taken = flags_ref[0] > 0
@@ -168,20 +169,20 @@
             def own(start):
                 def begin():
                     query = rows_of(q_ref, query_slab + head, start, QB)
-                    return score(query, rows_of(own_ref, 2 * head, 0, start + QB))
+                    return score(query, rows_of(own_ref, own_slab + 2 * head, 0, start + QB))
 
                 def finish(scores):
-                    return soften(scores, rows_of(own_ref, 2 * head + 1, 0, start + QB), True)
+                    return soften(scores, rows_of(own_ref, own_slab + 2 * head + 1, 0, start + QB), True)
 
                 return begin, finish
 
             def earlier(start):
                 def begin():
                     query = rows_of(q_ref, query_slab + head, start, QB)
-                    return score(query, rows_of(up_ref, 2 * head, 0, rows))
+                    return score(query, rows_of(up_ref, up_slab + 2 * head, 0, rows))
 
                 def finish(scores):
-                    return soften(scores, rows_of(up_ref, 2 * head + 1, 0, rows))
+                    return soften(scores, rows_of(up_ref, up_slab + 2 * head + 1, 0, rows))
 
                 return begin, finish
 
@@ -258,23 +259,23 @@
     )
 
 
-def attend_ahead(flags, query, pair):
-    rows, heads = pair.shape[0] * POSITIONS, pair.shape[1] // 2
-    return pl.pallas_call(
-        ahead_kernel,
-        in_specs=[SMEM] + [VMEM] * 2,
+def attend_ahead(flags, heads, query, query_slab, pair, pair_slab, *waited):
+    rows = pair.shape[0] * POSITIONS
+    return pl.pallas_call(
+        functools.partial(ahead_kernel, query_slab, pair_slab),
+        in_specs=[SMEM] + [VMEM] * 2 + [ANY] * len(waited),
         out_specs=VMEM,
         out_shape=jax.ShapeDtypeStruct((heads, rows + STAT_ROWS, HD), jnp.bfloat16),
         compiler_params=PARAMS,
         cost_estimate=cost(1, rows, heads, rows * heads * HD * 8),
         name="ahead",
-    )(flags, query, pair)
-
-
-def attend_near(flags, query, query_slab, own, pair):
-    rows, heads = pair.shape[0] * POSITIONS, pair.shape[1] // 2
-    return pl.pallas_call(
-        functools.partial(near_kernel, query_slab),
+    )(flags, query, pair, *waited)
+
+
+def attend_near(flags, heads, query, query_slab, own, own_slab, up, up_slab):
+    rows = query.shape[0] * POSITIONS
+    return pl.pallas_call(
+        functools.partial(near_kernel, query_slab, own_slab, up_slab),
         in_specs=[SMEM] + [VMEM] * 3,
         out_specs=[VMEM] * 2,
         out_shape=[
@@ -284,7 +285,7 @@
         compiler_params=PARAMS,
         cost_estimate=cost(1.6, rows, heads, rows * heads * HD * 14),
         name="near",
-    )(flags, query, own, pair)
+    )(flags, query, own, up)
 
 
 def merge(flags, near, logs, far):
@@ -300,7 +301,9 @@
     )(flags, *near, *logs, *far)
 
 
-def cut_first_kernel(k_ref, v_ref, out_ref, held_ref, piece_ref, in_sems, out_sems):
+def cut_first_kernel(k_ref, v_ref, first_ref, last_ref, held_ref, first_piece, last_piece, *sems):
+    in_sems, first_sems, last_sems = sems
+
     def fetch(which, window):
         rows = pl.ds(window * POSITIONS, POSITIONS)
         ref = (k_ref, v_ref)[which]
@@ -308,9 +311,12 @@
             ref.at[rows], held_ref.at[which, rows], in_sems.at[which, window]
         )
 
-    def store(window):
+    def stores(window):
         peers = pl.ds(window * SPAN, SPAN)
-        return pltpu.make_async_copy(piece_ref.at[peers], out_ref.at[peers], out_sems.at[window])
+        return (
+            pltpu.make_async_copy(first_piece.at[peers], first_ref.at[peers], first_sems.at[window]),
+            pltpu.make_async_copy(last_piece.at[peers], last_ref.at[peers], last_sems.at[window]),
+        )
 
     for window in range(NWIN):
         for which in range(2):
@@ -320,25 +326,34 @@
         for which in range(2):
             fetch(which, window).wait()
             for part in range(SPAN):
-                for head in range(2):
+                for head in range(PARTS):
                     lanes = pl.ds((part * PARTS + head) * HD, HD)
-                    piece_ref[window * SPAN + part, 2 * head + which] = held_ref[which, rows, lanes]
-        store(window).start()
+                    value = held_ref[which, rows, lanes]
+                    if head < 2:
+                        first_piece[window * SPAN + part, 2 * head + which] = value
+                    else:
+                        last_piece[window * SPAN + part, which] = value
+        for copy in stores(window):
+            copy.start()
     for window in range(NWIN):
-        store(window).wait()
+        for copy in stores(window):
+            copy.wait()
 
 
 def cut_first(key, value):
-    shape = (NWIN * SPAN, 4, POSITIONS, HD)
+    first = (NWIN * SPAN, 4, POSITIONS, HD)
+    last = (NWIN * SPAN, 2, POSITIONS, HD)
     return pl.pallas_call(
         cut_first_kernel,
         in_specs=[HBM] * 2,
-        out_specs=HBM,
-        out_shape=jax.ShapeDtypeStruct(shape, jnp.bfloat16),
+        out_specs=[HBM] * 2,
+        out_shape=[jax.ShapeDtypeStruct(shape, jnp.bfloat16) for shape in (first, last)],
         scratch_shapes=[
             pltpu.VMEM((2,) + key.shape, jnp.bfloat16),
-            pltpu.VMEM(shape, jnp.bfloat16),
+            pltpu.VMEM(first, jnp.bfloat16),
+            pltpu.VMEM(last, jnp.bfloat16),
             pltpu.SemaphoreType.DMA((2, NWIN)),
+            pltpu.SemaphoreType.DMA((NWIN,)),
             pltpu.SemaphoreType.DMA((NWIN,)),
         ],
         compiler_params=pltpu.CompilerParams(vmem_limit_bytes=60 * 2**20),
@@ -362,26 +377,28 @@
     )(passed, *waited)
 
 
-def cut_kernel(slabs, *refs):
-    sources, out_ref = refs[:-1], refs[-1]
+def cut_kernel(whole_ref, piece_ref, out_ref):
+    heads = out_ref.shape[1] - piece_ref.shape[1]
     for window in range(NWIN):
         rows = pl.ds(window * POSITIONS, POSITIONS)
         for part in range(SPAN):
-            for slab, (source, head) in enumerate(slabs):
+            for head in range(heads):
                 lanes = pl.ds((part * PARTS + head) * HD, HD)
-                out_ref[window * SPAN + part, slab] = sources[source][rows, lanes]
-
-
-def cut(sources, slabs):
-    return pl.pallas_call(
-        functools.partial(cut_kernel, slabs),
-        in_specs=[VMEM] * len(sources),
+                out_ref[window * SPAN + part, head] = whole_ref[rows, lanes]
+    out_ref[:, heads:] = piece_ref[...]
+
+
+def cut(whole, piece, flops):
+    slabs = PARTS + piece.shape[1]
+    return pl.pallas_call(
+        cut_kernel,
+        in_specs=[VMEM] * 2,
         out_specs=VMEM,
-        out_shape=jax.ShapeDtypeStruct((NWIN * SPAN, len(slabs), POSITIONS, HD), jnp.bfloat16),
+        out_shape=jax.ShapeDtypeStruct((NWIN * SPAN, slabs, POSITIONS, HD), jnp.bfloat16),
         compiler_params=PARAMS,
-        cost_estimate=pl.CostEstimate(flops=10**11, bytes_accessed=2**22, transcendentals=0),
+        cost_estimate=pl.CostEstimate(flops=flops, bytes_accessed=2**21, transcendentals=0),
         name="cut",
-    )(*sources)
+    )(whole, piece)
 
 
 def paste_kernel(in_ref, out_ref, held_ref, sems):
@@ -428,21 +445,19 @@
         return lax.ppermute(block, "grp", [(at + 1, at) for at in range(group_devices - 1)])
 
     later_query = down(query_vectors)
-    first = to_peers(cut_first(key_vectors, value_vectors))
+    first, last = cut_first(key_vectors, value_vectors)
+    last_up = up(last)
+    first = to_peers(first)
     first_up = up(first)
     flags = make_flags(chosen_groups, chosen_count)
-    second = cut(
-        (key_vectors, value_vectors, later_query), ((0, 2), (1, 2), (2, 0), (2, 1), (2, 2))
-    )
-    second = to_peers(gate(second, first, flags))
-    second_pair = second[:, 0:2]
-    second_up = up(second_pair)
-    query = to_peers(gate(cut((query_vectors,), ((0, 0), (0, 1), (0, 2))), second_pair))
-    first_far = up(attend_ahead(flags, second[:, 2:4], first_up))
-    second_far = up(attend_ahead(flags, second[:, 4:5], second_up))
-    near_a, log_a = attend_near(flags, query, 0, first, first_up)
-    near_b, log_b = attend_near(flags, query, 2, second_pair, second_up)
-    merged = merge(flags, (near_a, near_b), (log_a, log_b), (first_far, second_far))
+    second = to_peers(gate(cut(later_query, last_up, 10**11), first, flags))
+    third = to_peers(gate(cut(query_vectors, last, 10**6), second))
+    ahead_b = attend_ahead(flags, 1, second, 2, second, 3)
+    far_b = up(ahead_b)
+    far_a = up(attend_ahead(flags, 2, second, 0, first_up, 0, ahead_b))
+    near_b, log_b = attend_near(flags, 1, third, 2, third, 3, second, 3)
+    near_a, log_a = attend_near(flags, 2, third, 0, first, 0, first_up, 0)
+    merged = merge(flags, (near_a, near_b), (log_a, log_b), (far_a, far_b))
     return paste(to_peers(merged))
 
 

time: 120 us -> 119 us (level)
  Pallas kernels: 17.8 us -> 21.6 us
  starting transfers between devices: 31.7 us -> 28.2 us
  local copies, waits for them, and re-layouts: 3.75 us -> 2.35 us
    all_to_all x3, waiting for transfers between devices: 25.2 us -> 33 us  [to_peers(): return lax.all_to_all(block, 'ctx', split_axis=0, concat_axis=0, tiled=True)]
    ppermute x4, waiting for transfers between devices: 14 us -> 10.2 us  [up(): lax.ppermute(block, 'grp', [(at, at + 1) for at in range(group_devices -...]
    ppermute x1, waiting for transfers between devices: 3.6 us -> 0.01 us  [down(): lax.ppermute(block, 'grp', [(at + 1, at) for at in range(group_devices -...]
    pallas_call x7, Pallas kernels: 13.9 us -> 17.2 us  [the longest x2 7.49 us: attend_ahead(): pl.pallas_call(functools.partial(ahead_kernel, query_slab, pair_slab), in...]
    ppermute x4, starting transfers between devices: 11.1 us -> 8.19 us  [up(): lax.ppermute(block, 'grp', [(at, at + 1) for at in range(group_devices -...]
    slice x2 -> x0, local copies, waits for them, and re-layouts: 2.25 us -> none  [the longest x1 1.27 us: body(): first_far = up(attend_ahead(flags, second[:, 2:4], first_up))]
  transfers between devices with their start and end apart: 8 -> 8, of which waited for: 7 -> 6; matrix products, arithmetic and copies ran while one was open for 2% -> 0% of each run, Pallas kernels for 14% -> 17%
where the time goes in v4:
time: 119 us
  waiting for transfers between devices  43.3 us (36%)
  starting transfers between devices  28.2 us (24%)
  blocking collectives  23.1 us (19%)
  Pallas kernels  21.6 us (18%)
  local copies, waits for them, and re-layouts  2.35 us (2%)
    all_to_all x3, waiting for transfers between devices, to_peers(): return lax.all_to_all(block, 'ctx', split_axis=0, concat_axis=0, tiled=True)  33 us
    all_to_all x1, blocking collectives, to_peers(): return lax.all_to_all(block, 'ctx', split_axis=0, concat_axis=0, tiled=True)  23.1 us
    all_to_all x3, starting transfers between devices, to_peers(): return lax.all_to_all(block, 'ctx', split_axis=0, concat_axis=0, tiled=True)  16.2 us
    ppermute x4, waiting for transfers between devices, up(): lax.ppermute(block, 'grp', [(at, at + 1) for at in range(group_devices -...  10.2 us
    ppermute x4, starting transfers between devices, up(): lax.ppermute(block, 'grp', [(at, at + 1) for at in range(group_devices -...  8.19 us
    pallas_call x2, Pallas kernels, attend_ahead(): pl.pallas_call(functools.partial(ahead_kernel, query_slab, pair_slab), in...  7.49 us
    pallas_call x2, Pallas kernels, attend_near(): pl.pallas_call(functools.partial(near_kernel, query_slab, own_slab, up_sl...  5.87 us
    ppermute x1, starting transfers between devices, down(): lax.ppermute(block, 'grp', [(at + 1, at) for at in range(group_devices -...  3.84 us
  transfers between devices with their start and end apart: 8, of which 6 were waited for; matrix products, arithmetic and copies ran while one was open for 0% of the time, Pallas kernels for 17%

profile of v4, /device:TPU:385, one launch (start us, length us, event | category | flops | bytes accessed | tf_op | source)
XLA Modules:
  0.0 118.6 jit_solution(15359772510452719670)
XLA Ops:
  0.0 3.8 %collective-permute-start = (bf16[256,1536]{1,0:T(8,128)(2,1)}, bf16[256,1536]{1,0:T(8,128)(2,1)S(1)}, u32[]{:S(2)}, u32[]{:S(2)}) collective-permute-start(bf16[256,1536]{1,0:T(8,128)(2,1)} %whole_ref.1), channel_id=1, source_target_pairs={{32,0},{64,32},{96,64},{128,96},{160,128},{192,160},{224,192},{256... | collective-permute-start | bytes 2359304 | tf_op jit(solution)/shard_map/ppermute | solution.py:445
  3.8 2.4 %cut_first.1 = (bf16[32,4,32,128]{3,2,1,0:T(8,128)(2,1)}, bf16[32,2,32,128]{3,2,1,0:T(8,128)(2,1)}) custom-call(bf16[256,1536]{1,0:T(8,128)(2,1)} %k_ref.1, bf16[256,1536]{1,0:T(8,128)(2,1)} %v_ref.1), custom_call_target="tpu_custom_call" | custom-call | tf_op jit(solution)/shard_map/cut_first/pallas_call | solution.py:346
  6.3 0.0 copy-start.3
  6.3 0.0 copy-start.4
  6.3 1.9 %collective-permute-start.1 = (bf16[32,2,32,128]{3,2,1,0:T(8,128)(2,1)}, bf16[32,2,32,128]{3,2,1,0:T(8,128)(2,1)S(1)}, u32[]{:S(2)}, u32[]{:S(2)}) collective-permute-start(bf16[32,2,32,128]{3,2,1,0:T(8,128)(2,1)} %get-tuple-element.11.piece_ref), channel_id=1, source_target_pairs={{0,32},{32,64},{64,96},{96,128},{128,160},{160,192},{192,224},{224... | collective-permute-start | bytes 1572872 | tf_op jit(solution)/shard_map/ppermute | solution.py:442
  8.2 8.1 %all-to-all-start = ((bf16[32,4,32,128]{3,2,1,0:T(8,128)(2,1)}), bf16[32,4,32,128]{3,2,1,0:T(8,128)(2,1)}, u32[]{:S(2)}, u32[]{:S(2)}) async-start(bf16[32,4,32,128]{3,2,1,0:T(8,128)(2,1)} %get-tuple-element.12), calls=%async_computation | async-start | bytes 2097152 | tf_op jit(solution)/shard_map/all_to_all | solution.py:439
  16.4 0.0 copy-done.3
  16.4 0.1 copy.8.groups_ref
  16.5 0.0 copy-done.4
  16.5 0.1 copy.9.count_ref
  16.6 2.4 %flags.1.refs_2_.flags_ref = s32[4]{0:T(128)S(1)} custom-call(s32[16,8,2]{2,1,0:T(8,128)S(1)} %copy.8.groups_ref, s32[16,8]{1,0:T(8,128)S(1)} %copy.9.count_ref), custom_call_target="tpu_custom_call" | custom-call | tf_op jit(solution)/shard_map/flags/pallas_call | solution.py:52
  18.9 3.3 %collective-permute-done.1.piece_ref = bf16[32,2,32,128]{3,2,1,0:T(8,128)(2,1)S(1)} collective-permute-done((bf16[32,2,32,128]{3,2,1,0:T(8,128)(2,1)}, bf16[32,2,32,128]{3,2,1,0:T(8,128)(2,1)S(1)}, u32[]{:S(2)}, u32[]{:S(2)}) %collective-permute-start.1) | collective-permute-done | bytes 524320 | tf_op jit(solution)/shard_map/ppermute | solution.py:442
  22.2 0.0 collective-permute-done.whole_ref
  22.2 1.3 %cut.3.refs_0_ = bf16[32,5,32,128]{3,2,1,0:T(8,128)(2,1)} custom-call(bf16[256,1536]{1,0:T(8,128)(2,1)S(1)} %collective-permute-done.whole_ref, bf16[32,2,32,128]{3,2,1,0:T(8,128)(2,1)S(1)} %collective-permute-done.1.piece_ref), custom_call_target="tpu_custom_call" | custom-call | flops 99999997952 | bytes 2097152 | tf_op jit(solution)/shard_map/cut/pallas_call | solution.py:393
  23.5 9.8 %all-to-all-done.refs_1_.own_ref = bf16[32,4,32,128]{3,2,1,0:T(8,128)(2,1)} async-done(((bf16[32,4,32,128]{3,2,1,0:T(8,128)(2,1)}), bf16[32,4,32,128]{3,2,1,0:T(8,128)(2,1)}, u32[]{:S(2)}, u32[]{:S(2)}) %all-to-all-start) | async-done | bytes 1048608 | tf_op jit(solution)/shard_map/all_to_all | solution.py:439
  33.3 0.0 copy-start.1
  33.3 4.1 %all-to-all-start.1 = ((bf16[32,5,32,128]{3,2,1,0:T(8,128)(2,1)}), bf16[32,5,32,128]{3,2,1,0:T(8,128)(2,1)S(1)}, u32[]{:S(2)}, u32[]{:S(2)}) async-start(bf16[32,5,32,128]{3,2,1,0:T(8,128)(2,1)} %gate.2), calls=%async_computation.1 | async-start | bytes 2621440 | tf_op jit(solution)/shard_map/all_to_all | solution.py:439
  37.4 2.4 %collective-permute-start.2 = (bf16[32,4,32,128]{3,2,1,0:T(8,128)(2,1)}, bf16[32,4,32,128]{3,2,1,0:T(8,128)(2,1)}, u32[]{:S(2)}, u32[]{:S(2)}) collective-permute-start(bf16[32,4,32,128]{3,2,1,0:T(8,128)(2,1)} %all-to-all-done.refs_1_.own_ref), channel_id=1, source_target_pairs={{0,32},{32,64},{64,96},{96,128},{128,160},{160,192},{192,224},{224... | collective-permute-start | bytes 3145736 | tf_op jit(solution)/shard_map/ppermute | solution.py:442
  39.9 0.0 copy-done.1
  39.9 0.0 copy-start.2
  39.9 1.0 copy-done.2
  40.9 0.2 cut.2.refs_0_
  41.1 16.1 %all-to-all-done.1.refs_1_.up_ref.q_ref.kv_ref = bf16[32,5,32,128]{3,2,1,0:T(8,128)(2,1)S(1)} async-done(((bf16[32,5,32,128]{3,2,1,0:T(8,128)(2,1)}), bf16[32,5,32,128]{3,2,1,0:T(8,128)(2,1)S(1)}, u32[]{:S(2)}, u32[]{:S(2)}) %all-to-all-start.1) | async-done | bytes 1310752 | tf_op jit(solution)/shard_map/all_to_all | solution.py:439
  57.2 0.0 copy-start
  57.2 1.1 copy-done
  58.3 4.0 %all-to-all-start.2 = ((bf16[32,5,32,128]{3,2,1,0:T(8,128)(2,1)}), bf16[32,5,32,128]{3,2,1,0:T(8,128)(2,1)S(1)}, u32[]{:S(2)}, u32[]{:S(2)}) async-start(bf16[32,5,32,128]{3,2,1,0:T(8,128)(2,1)} %copy-done), calls=%async_computation.2 | async-start | bytes 2621440 | tf_op jit(solution)/shard_map/all_to_all | solution.py:439
  62.3 2.2 %ahead.2.rest_0_ = bf16[1,1056,128]{2,1,0:T(8,128)(2,1)S(1)} custom-call(s32[4]{0:T(128)S(1)} %flags.1.refs_2_.flags_ref, bf16[32,5,32,128]{3,2,1,0:T(8,128)(2,1)S(1)} %all-to-all-done.1.refs_1_.up_ref.q_ref.kv_ref, bf16[32,5,32,128]{3,2,1,0:T(8,128)(2,1)S(1)} %all-to-all-done.1.refs_1_.up_ref.q_ref.kv_ref), custom_call_target="tpu_custom_call" | custom-call | flops 536870912 | bytes 1048576 | tf_op jit(solution)/shard_map/ahead/pallas_call | solution.py:264
  64.5 1.5 %collective-permute-done.2.up_ref.kv_ref = bf16[32,4,32,128]{3,2,1,0:T(8,128)(2,1)} collective-permute-done((bf16[32,4,32,128]{3,2,1,0:T(8,128)(2,1)}, bf16[32,4,32,128]{3,2,1,0:T(8,128)(2,1)}, u32[]{:S(2)}, u32[]{:S(2)}) %collective-permute-start.2) | collective-permute-done | bytes 1048608 | tf_op jit(solution)/shard_map/ppermute | solution.py:442
  66.0 5.3 %ahead.3 = bf16[2,1056,128]{2,1,0:T(8,128)(2,1)} custom-call(s32[4]{0:T(128)S(1)} %flags.1.refs_2_.flags_ref, bf16[32,5,32,128]{3,2,1,0:T(8,128)(2,1)S(1)} %all-to-all-done.1.refs_1_.up_ref.q_ref.kv_ref, bf16[32,4,32,128]{3,2,1,0:T(8,128)(2,1)} %collective-permute-done.2.up_ref.kv_ref, bf16[1,1056,128]{2,1,0:T(8,128)(2,1)S(1)} %ahead.2.rest_0_), custom_call_target="tpu_custom_call" | custom-call | flops 1073741824 | bytes 2097152 | tf_op jit(solution)/shard_map/ahead/pallas_call | solution.py:264
  71.3 1.9 %collective-permute-start.3 = (bf16[2,1056,128]{2,1,0:T(8,128)(2,1)}, bf16[2,1056,128]{2,1,0:T(8,128)(2,1)S(1)}, u32[]{:S(2)}, u32[]{:S(2)}) collective-permute-start(bf16[2,1056,128]{2,1,0:T(8,128)(2,1)} %ahead.3), channel_id=1, source_target_pairs={{0,32},{32,64},{64,96},{96,128},{128,160},{160,192},{192,224},{224... | collective-permute-start | bytes 1622024 | tf_op jit(solution)/shard_map/ppermute | solution.py:442
  73.2 1.9 %collective-permute-start.4 = (bf16[1,1056,128]{2,1,0:T(8,128)(2,1)S(1)}, bf16[1,1056,128]{2,1,0:T(8,128)(2,1)}, u32[]{:S(2)}, u32[]{:S(2)}) collective-permute-start(bf16[1,1056,128]{2,1,0:T(8,128)(2,1)S(1)} %ahead.2.rest_0_), channel_id=1, source_target_pairs={{0,32},{32,64},{64,96},{96,128},{128,160},{160,192},{192,224},{224... | collective-permute-start | bytes 811016 | tf_op jit(solution)/shard_map/ppermute | solution.py:442
  75.1 7.1 %all-to-all-done.2.q_ref.own_ref = bf16[32,5,32,128]{3,2,1,0:T(8,128)(2,1)S(1)} async-done(((bf16[32,5,32,128]{3,2,1,0:T(8,128)(2,1)}), bf16[32,5,32,128]{3,2,1,0:T(8,128)(2,1)S(1)}, u32[]{:S(2)}, u32[]{:S(2)}) %all-to-all-start.2) | async-done | bytes 1310752 | tf_op jit(solution)/shard_map/all_to_all | solution.py:439
  82.2 1.8 %near.3 = (f32[1,1024,128]{2,1,0:T(8,128)S(1)}, f32[1,8,128]{2,1,0:T(8,128)S(1)}) custom-call(s32[4]{0:T(128)S(1)} %flags.1.refs_2_.flags_ref, bf16[32,5,32,128]{3,2,1,0:T(8,128)(2,1)S(1)} %all-to-all-done.2.q_ref.own_ref, bf16[32,5,32,128]{3,2,1,0:T(8,128)(2,1)S(1)} %all-to-all-done.2.q_ref.own_ref, ...), custom_call_target="tpu_custom_call" | custom-call | flops 858993472 | bytes 1835008 | tf_op jit(solution)/shard_map/near/pallas_call | solution.py:277
  84.0 4.1 %near.2 = (f32[2,1024,128]{2,1,0:T(8,128)S(1)}, f32[2,8,128]{2,1,0:T(8,128)S(1)}) custom-call(s32[4]{0:T(128)S(1)} %flags.1.refs_2_.flags_ref, bf16[32,5,32,128]{3,2,1,0:T(8,128)(2,1)S(1)} %all-to-all-done.2.q_ref.own_ref, bf16[32,4,32,128]{3,2,1,0:T(8,128)(2,1)} %all-to-all-done.refs_1_.own_ref, bf16[32,4,32,128]{3,2,1,0:T(8,128)(2,1)} %collective-permute-done.2.up_ref.kv_ref), custom_call_target="tpu_custom_call" | custom-call | flops 1717986944 | bytes 3670016 | tf_op jit(solution)/shard_map/near/pallas_call | solution.py:277
  88.1 5.5 %collective-permute-done.4.far_b = bf16[1,1056,128]{2,1,0:T(8,128)(2,1)} collective-permute-done((bf16[1,1056,128]{2,1,0:T(8,128)(2,1)S(1)}, bf16[1,1056,128]{2,1,0:T(8,128)(2,1)}, u32[]{:S(2)}, u32[]{:S(2)}) %collective-permute-start.4) | collective-permute-done | bytes 270368 | tf_op jit(solution)/shard_map/ppermute | solution.py:442
  93.6 0.0 collective-permute-done.3.far_a
  93.6 1.0 merge.1
  94.6 23.1 %all_to_all.20.in_ref = bf16[32,3,32,128]{3,2,1,0:T(8,128)(2,1)S(1)} all-to-all(bf16[32,3,32,128]{3,2,1,0:T(8,128)(2,1)S(1)} %merge.1), channel_id=1, replica_groups=mesh['grp'=16,'ctx'=32] {'ctx'}, dimensions={0} | all-to-all | bytes 1572864 | tf_op jit(solution)/shard_map/all_to_all | solution.py:439
  117.7 1.0 paste.1
  (2 shorter events, 0.0 us)
Async XLA Ops:
  0.0 22.2 %collective-permute-start = (bf16[256,1536]{1,0:T(8,128)(2,1)}, bf16[256,1536]{1,0:T(8,128)(2,1)S(1)}, u32[]{:S(2)}, u32[]{:S(2)}) collective-permute-start(bf16[256,1536]{1,0:T(8,128)(2,1)} %whole_ref.1), channel_id=1, source_target_pairs={{32,0},{64,32},{96,64},{128,96},{160,128},{192,160},{224,192},{256... | collective-permute-start | bytes 2359304 | tf_op jit(solution)/shard_map/ppermute | solution.py:445
  6.3 10.1 %copy-start.3 = (s32[16,8,2]{0,2,1:T(2,128)S(1)}, s32[16,8,2]{0,2,1:T(2,128)}, u32[]{:S(2)}) copy-start(s32[16,8,2]{0,2,1:T(2,128)} %param.8) | copy-start | bytes 3076
  6.3 10.2 %copy-start.4 = (s32[16,8]{0,1:T(8,128)S(1)}, s32[16,8]{0,1:T(8,128)}, u32[]{:S(2)}) copy-start(s32[16,8]{0,1:T(8,128)} %param.9) | copy-start | bytes 1540
  6.3 15.9 %collective-permute-start.1 = (bf16[32,2,32,128]{3,2,1,0:T(8,128)(2,1)}, bf16[32,2,32,128]{3,2,1,0:T(8,128)(2,1)S(1)}, u32[]{:S(2)}, u32[]{:S(2)}) collective-permute-start(bf16[32,2,32,128]{3,2,1,0:T(8,128)(2,1)} %get-tuple-element.11.piece_ref), channel_id=1, source_target_pairs={{0,32},{32,64},{64,96},{96,128},{128,160},{160,192},{192,224},{224... | collective-permute-start | bytes 1572872 | tf_op jit(solution)/shard_map/ppermute | solution.py:442
  8.2 25.1 %all-to-all-start = ((bf16[32,4,32,128]{3,2,1,0:T(8,128)(2,1)}), bf16[32,4,32,128]{3,2,1,0:T(8,128)(2,1)}, u32[]{:S(2)}, u32[]{:S(2)}) async-start(bf16[32,4,32,128]{3,2,1,0:T(8,128)(2,1)} %get-tuple-element.12), calls=%async_computation | async-start | bytes 2097152 | tf_op jit(solution)/shard_map/all_to_all | solution.py:439
  33.3 6.5 %copy-start.1 = (bf16[256,1536]{1,0:T(8,128)(2,1)S(1)}, bf16[256,1536]{1,0:T(8,128)(2,1)}, u32[]{:S(2)}) copy-start(bf16[256,1536]{1,0:T(8,128)(2,1)} %whole_ref.1) | copy-start | bytes 2359300
  33.3 23.9 %all-to-all-start.1 = ((bf16[32,5,32,128]{3,2,1,0:T(8,128)(2,1)}), bf16[32,5,32,128]{3,2,1,0:T(8,128)(2,1)S(1)}, u32[]{:S(2)}, u32[]{:S(2)}) async-start(bf16[32,5,32,128]{3,2,1,0:T(8,128)(2,1)} %gate.2), calls=%async_computation.1 | async-start | bytes 2621440 | tf_op jit(solution)/shard_map/all_to_all | solution.py:439
  37.4 28.5 %collective-permute-start.2 = (bf16[32,4,32,128]{3,2,1,0:T(8,128)(2,1)}, bf16[32,4,32,128]{3,2,1,0:T(8,128)(2,1)}, u32[]{:S(2)}, u32[]{:S(2)}) collective-permute-start(bf16[32,4,32,128]{3,2,1,0:T(8,128)(2,1)} %all-to-all-done.refs_1_.own_ref), channel_id=1, source_target_pairs={{0,32},{32,64},{64,96},{96,128},{128,160},{160,192},{192,224},{224... | collective-permute-start | bytes 3145736 | tf_op jit(solution)/shard_map/ppermute | solution.py:442
  39.9 1.0 copy-start.2
  57.2 1.1 copy-start
  58.3 23.9 %all-to-all-start.2 = ((bf16[32,5,32,128]{3,2,1,0:T(8,128)(2,1)}), bf16[32,5,32,128]{3,2,1,0:T(8,128)(2,1)S(1)}, u32[]{:S(2)}, u32[]{:S(2)}) async-start(bf16[32,5,32,128]{3,2,1,0:T(8,128)(2,1)} %copy-done), calls=%async_computation.2 | async-start | bytes 2621440 | tf_op jit(solution)/shard_map/all_to_all | solution.py:439
  71.3 22.3 %collective-permute-start.3 = (bf16[2,1056,128]{2,1,0:T(8,128)(2,1)}, bf16[2,1056,128]{2,1,0:T(8,128)(2,1)S(1)}, u32[]{:S(2)}, u32[]{:S(2)}) collective-permute-start(bf16[2,1056,128]{2,1,0:T(8,128)(2,1)} %ahead.3), channel_id=1, source_target_pairs={{0,32},{32,64},{64,96},{96,128},{128,160},{160,192},{192,224},{224... | collective-permute-start | bytes 1622024 | tf_op jit(solution)/shard_map/ppermute | solution.py:442
  73.2 20.4 %collective-permute-start.4 = (bf16[1,1056,128]{2,1,0:T(8,128)(2,1)S(1)}, bf16[1,1056,128]{2,1,0:T(8,128)(2,1)}, u32[]{:S(2)}, u32[]{:S(2)}) collective-permute-start(bf16[1,1056,128]{2,1,0:T(8,128)(2,1)S(1)} %ahead.2.rest_0_), channel_id=1, source_target_pairs={{0,32},{32,64},{64,96},{96,128},{128,160},{160,192},{192,224},{224... | collective-permute-start | bytes 811016 | tf_op jit(solution)/shard_map/ppermute | solution.py:442

commit v5 on v4

--- a/solution.py
+++ b/solution.py
@@ -26,7 +26,7 @@
 ANY = pl.BlockSpec(memory_space=pl.ANY)
 HBM = pl.BlockSpec(memory_space=pltpu.HBM)
 SMALL = pltpu.CompilerParams(vmem_limit_bytes=2**20)
-PARAMS = pltpu.CompilerParams(vmem_limit_bytes=8 * 2**20)
+PARAMS = pltpu.CompilerParams(vmem_limit_bytes=14 * 2**20)
 
 
 def is_taken(groups_ref, count_ref, group, distance):
@@ -61,31 +61,45 @@
 
 def score(query, keys):
     return lax.dot_general(
-        query, keys, (((1,), (1,)), ((), ())), preferred_element_type=jnp.float32
+        keys, query, (((1,), (1,)), ((), ())), preferred_element_type=jnp.float32
     )
 
 
-def soften(scores, values, diagonal=False):
+def soften(score_ref, values, diagonal=False):
+    count = values.shape[0]
+    scores = score_ref[:count, :]
     if diagonal:
-        rows, count = scores.shape
-        tail = scores[:, count - rows :]
-        frame_query = lax.broadcasted_iota(jnp.int32, (rows, rows), 0) // POSITIONS
-        frame_key = lax.broadcasted_iota(jnp.int32, (rows, rows), 1) // POSITIONS
+        tail = scores[count - QB :]
+        frame_key = lax.broadcasted_iota(jnp.int32, (QB, QB), 0) // POSITIONS
+        frame_query = lax.broadcasted_iota(jnp.int32, (QB, QB), 1) // POSITIONS
         tail = jnp.where(frame_query >= frame_key, tail, NEG_FILL)
-        scores = jnp.concatenate([scores[:, : count - rows], tail], axis=1) if count > rows else tail
-    highest = jnp.max(scores, axis=-1, keepdims=True)
+        scores = jnp.concatenate([scores[: count - QB], tail], axis=0) if count > QB else tail
+    highest = jnp.max(scores, axis=0, keepdims=True)
     weights = jnp.exp2((scores - highest) * FACTOR)
-    beside = jnp.concatenate([values, jnp.ones_like(values)], axis=1)
-    product = jnp.dot(weights.astype(jnp.bfloat16), beside, preferred_element_type=jnp.float32)
-    return highest, product[:, HD:], product[:, :HD]
-
-
-def in_turn(jobs, done):
-    scores = jobs[0][0]()
+    summed = jnp.sum(weights, axis=0, keepdims=True)
+    blended = lax.dot_general(
+        values,
+        weights.astype(jnp.bfloat16),
+        (((0,), (0,)), ((), ())),
+        preferred_element_type=jnp.float32,
+    )
+    return highest, summed, blended
+
+
+def in_turn(jobs, score_refs, done):
+    def begin(at):
+        scores = jobs[at][0]()
+        score_refs[at % 2][: scores.shape[0], :] = scores
+
+    begin(0)
     for at, (_, finish) in enumerate(jobs):
-        following = jobs[at + 1][0]() if at + 1 < len(jobs) else None
-        done(at, finish(scores))
-        scores = following
+        if at + 1 < len(jobs):
+            begin(at + 1)
+        done(at, finish(score_refs[at % 2]))
+
+
+def buffers(rows):
+    return [pltpu.VMEM((rows, QB), jnp.float32)] * 2
 
 
 def join(old, new):
@@ -99,27 +113,23 @@
     )
 
 
+def put_blocks(ref, head, start, value):
+    for at in range(0, QB, HD):
+        ref[head, pl.ds(start + at, HD), :] = value[:, at : at + HD].astype(ref.dtype)
+
+
 def rows_of(ref, slab, start, size):
     first, count = start // POSITIONS, size // POSITIONS
     return ref[pl.ds(first, count), slab].reshape(size, HD)
 
 
-def eye_mask():
-    return lax.broadcasted_iota(jnp.int32, (HD, HD), 0) == lax.broadcasted_iota(
-        jnp.int32, (HD, HD), 1
-    )
-
-
 def log_rows(part):
     log_sum = part[0] * FACTOR + jnp.log(part[1]) * LOG2E
-    return [
-        jnp.sum(jnp.where(eye_mask(), log_sum[at : at + HD], 0.0), axis=0, keepdims=True)
-        for at in range(0, log_sum.shape[0], HD)
-    ]
+    return [log_sum[:, at : at + HD] for at in range(0, QB, HD)]
 
 
 def ahead_kernel(query_slab, pair_slab, flags_ref, q_ref, kv_ref, *rest):
-    out_ref = rest[-1]
+    out_ref, score_refs = rest[-3], rest[-2:]
     rows = q_ref.shape[0] * POSITIONS
     heads = out_ref.shape[0]
     taken = flags_ref[2] > 0
@@ -140,10 +150,10 @@
             logs = []
 
             def done(at, part):
-                out_ref[head, pl.ds(at * QB, QB), :] = (part[2] / part[1]).astype(jnp.bfloat16)
+                put_blocks(out_ref, head, at * QB, part[2] / part[1])
                 logs.extend(log_rows(part))
 
-            in_turn([job(start) for start in range(0, rows, QB)], done)
+            in_turn([job(start) for start in range(0, rows, QB)], score_refs, done)
             left = jnp.concatenate(logs, axis=0)
             pieces = []
             for _ in range(3):
@@ -158,7 +168,7 @@
         out_ref[:, pl.ds(rows, STAT_ROWS), :] = jnp.zeros((heads, STAT_ROWS, HD), jnp.bfloat16)
 
 
-def near_kernel(query_slab, own_slab, up_slab, flags_ref, q_ref, own_ref, up_ref, out_ref, log_ref):
+def near_kernel(query_slab, own_slab, up_slab, flags_ref, q_ref, own_ref, up_ref, out_ref, log_ref, *score_refs):
     rows = q_ref.shape[0] * POSITIONS
     heads = out_ref.shape[0]
     taken = flags_ref[0] > 0
@@ -196,7 +206,7 @@
                         return
                     part = join(held[-2], held[-1])
                     at = at // 2
-                out_ref[head, pl.ds(at * QB, QB), :] = part[2] / part[1]
+                put_blocks(out_ref, head, at * QB, part[2] / part[1])
                 logs.extend(log_rows(part))
 
             jobs = []
@@ -204,7 +214,7 @@
                 jobs.append(own(start))
                 if with_earlier:
                     jobs.append(earlier(start))
-            in_turn(jobs, done)
+            in_turn(jobs, score_refs, done)
             log_ref[head] = jnp.concatenate(logs, axis=0)
 
     @pl.when(taken)
@@ -224,7 +234,8 @@
     def put(head, block, value):
         count = HD // POSITIONS
         frames = pl.ds(block * count, count)
-        out_ref[frames, head] = value.astype(jnp.bfloat16).reshape(count, POSITIONS, HD)
+        turned = jnp.transpose(value).astype(jnp.bfloat16)
+        out_ref[frames, head] = turned.reshape(count, POSITIONS, HD)
 
     def each_head():
         count = near_a.shape[0]
@@ -237,12 +248,12 @@
         for head, near_ref, log_ref, far_ref in each_head():
             pieces = far_ref[pl.ds(rows, STAT_ROWS), :].astype(jnp.float32)
             far_log = pieces[:blocks] + pieces[blocks : 2 * blocks] + pieces[2 * blocks : 3 * blocks]
-            shares = jnp.transpose(1.0 / (1.0 + jnp.exp2(log_ref[...] - far_log)))
+            shares = 1.0 / (1.0 + jnp.exp2(log_ref[...] - far_log))
             for block in range(blocks):
                 part = pl.ds(block * HD, HD)
                 near = near_ref[part, :]
                 far = far_ref[part, :].astype(jnp.float32)
-                put(head, block, near + (far - near) * shares[:, block : block + 1])
+                put(head, block, near + (far - near) * shares[block : block + 1])
 
     @pl.when(jnp.logical_not(taken))
     def _():
@@ -266,6 +277,7 @@
         in_specs=[SMEM] + [VMEM] * 2 + [ANY] * len(waited),
         out_specs=VMEM,
         out_shape=jax.ShapeDtypeStruct((heads, rows + STAT_ROWS, HD), jnp.bfloat16),
+        scratch_shapes=buffers(rows),
         compiler_params=PARAMS,
         cost_estimate=cost(1, rows, heads, rows * heads * HD * 8),
         name="ahead",
@@ -282,6 +294,7 @@
             jax.ShapeDtypeStruct((heads, rows, HD), jnp.float32),
             jax.ShapeDtypeStruct((heads, rows // HD, HD), jnp.float32),
         ],
+        scratch_shapes=buffers(rows),
         compiler_params=PARAMS,
         cost_estimate=cost(1.6, rows, heads, rows * heads * HD * 14),
         name="near",

time: 119 us -> 120 us (level)
  Pallas kernels: 21.6 us -> 23 us
where the time goes in v5:
time: 120 us; the launch traced here: 119 us
  waiting for transfers between devices  42.5 us (35%)
  starting transfers between devices  28.2 us (24%)
  Pallas kernels  23 us (19%)
  blocking collectives  22.5 us (19%)
  local copies, waits for them, and re-layouts  2.35 us (2%)
    all_to_all x3, waiting for transfers between devices, to_peers(): return lax.all_to_all(block, 'ctx', split_axis=0, concat_axis=0, tiled=True)  32.6 us
    all_to_all x1, blocking collectives, to_peers(): return lax.all_to_all(block, 'ctx', split_axis=0, concat_axis=0, tiled=True)  22.5 us
    all_to_all x3, starting transfers between devices, to_peers(): return lax.all_to_all(block, 'ctx', split_axis=0, concat_axis=0, tiled=True)  16.2 us
    ppermute x4, waiting for transfers between devices, up(): lax.ppermute(block, 'grp', [(at, at + 1) for at in range(group_devices -...  9.86 us
    ppermute x4, starting transfers between devices, up(): lax.ppermute(block, 'grp', [(at, at + 1) for at in range(group_devices -...  8.19 us
    pallas_call x2, Pallas kernels, attend_ahead(): pl.pallas_call(functools.partial(ahead_kernel, query_slab, pair_slab), in...  8.14 us
    pallas_call x2, Pallas kernels, attend_near(): pl.pallas_call(functools.partial(near_kernel, query_slab, own_slab, up_sl...  6.43 us
    ppermute x1, starting transfers between devices, down(): lax.ppermute(block, 'grp', [(at + 1, at) for at in range(group_devices -...  3.84 us
  transfers between devices with their start and end apart: 8, of which 6 were waited for; matrix products, arithmetic and copies ran while one was open for 0% of the time, Pallas kernels for 17%

profile of v5, /device:TPU:385, one launch (start us, length us, event | category | flops | bytes accessed | tf_op | source)
XLA Modules:
  0.0 118.9 jit_solution(15073959250968806116)
XLA Ops:
  0.0 3.8 %collective-permute-start = (bf16[256,1536]{1,0:T(8,128)(2,1)}, bf16[256,1536]{1,0:T(8,128)(2,1)S(1)}, u32[]{:S(2)}, u32[]{:S(2)}) collective-permute-start(bf16[256,1536]{1,0:T(8,128)(2,1)} %whole_ref.1), channel_id=1, source_target_pairs={{32,0},{64,32},{96,64},{128,96},{160,128},{192,160},{224,192},{256... | collective-permute-start | bytes 2359304 | tf_op jit(solution)/shard_map/ppermute | solution.py:458
  3.8 2.4 %cut_first.1 = (bf16[32,4,32,128]{3,2,1,0:T(8,128)(2,1)}, bf16[32,2,32,128]{3,2,1,0:T(8,128)(2,1)}) custom-call(bf16[256,1536]{1,0:T(8,128)(2,1)} %k_ref.1, bf16[256,1536]{1,0:T(8,128)(2,1)} %v_ref.1), custom_call_target="tpu_custom_call" | custom-call | tf_op jit(solution)/shard_map/cut_first/pallas_call | solution.py:359
  6.3 0.0 copy-start.3
  6.3 0.0 copy-start.4
  6.3 1.9 %collective-permute-start.1 = (bf16[32,2,32,128]{3,2,1,0:T(8,128)(2,1)}, bf16[32,2,32,128]{3,2,1,0:T(8,128)(2,1)S(1)}, u32[]{:S(2)}, u32[]{:S(2)}) collective-permute-start(bf16[32,2,32,128]{3,2,1,0:T(8,128)(2,1)} %get-tuple-element.11.piece_ref), channel_id=1, source_target_pairs={{0,32},{32,64},{64,96},{96,128},{128,160},{160,192},{192,224},{224... | collective-permute-start | bytes 1572872 | tf_op jit(solution)/shard_map/ppermute | solution.py:455
  8.2 8.1 %all-to-all-start = ((bf16[32,4,32,128]{3,2,1,0:T(8,128)(2,1)}), bf16[32,4,32,128]{3,2,1,0:T(8,128)(2,1)}, u32[]{:S(2)}, u32[]{:S(2)}) async-start(bf16[32,4,32,128]{3,2,1,0:T(8,128)(2,1)} %get-tuple-element.12), calls=%async_computation | async-start | bytes 2097152 | tf_op jit(solution)/shard_map/all_to_all | solution.py:452
  16.4 0.0 copy-done.3
  16.4 0.1 copy.8.groups_ref
  16.5 0.0 copy-done.4
  16.5 0.1 copy.9.count_ref
  16.6 2.4 %flags.1.refs_2_.flags_ref = s32[4]{0:T(128)S(1)} custom-call(s32[16,8,2]{2,1,0:T(8,128)S(1)} %copy.8.groups_ref, s32[16,8]{1,0:T(8,128)S(1)} %copy.9.count_ref), custom_call_target="tpu_custom_call" | custom-call | tf_op jit(solution)/shard_map/flags/pallas_call | solution.py:52
  18.9 3.3 %collective-permute-done.1.piece_ref = bf16[32,2,32,128]{3,2,1,0:T(8,128)(2,1)S(1)} collective-permute-done((bf16[32,2,32,128]{3,2,1,0:T(8,128)(2,1)}, bf16[32,2,32,128]{3,2,1,0:T(8,128)(2,1)S(1)}, u32[]{:S(2)}, u32[]{:S(2)}) %collective-permute-start.1) | collective-permute-done | bytes 524320 | tf_op jit(solution)/shard_map/ppermute | solution.py:455
  22.2 0.0 collective-permute-done.whole_ref
  22.2 1.3 %cut.3.refs_0_ = bf16[32,5,32,128]{3,2,1,0:T(8,128)(2,1)} custom-call(bf16[256,1536]{1,0:T(8,128)(2,1)S(1)} %collective-permute-done.whole_ref, bf16[32,2,32,128]{3,2,1,0:T(8,128)(2,1)S(1)} %collective-permute-done.1.piece_ref), custom_call_target="tpu_custom_call" | custom-call | flops 99999997952 | bytes 2097152 | tf_op jit(solution)/shard_map/cut/pallas_call | solution.py:406
  23.5 9.8 %all-to-all-done.refs_1_.own_ref = bf16[32,4,32,128]{3,2,1,0:T(8,128)(2,1)} async-done(((bf16[32,4,32,128]{3,2,1,0:T(8,128)(2,1)}), bf16[32,4,32,128]{3,2,1,0:T(8,128)(2,1)}, u32[]{:S(2)}, u32[]{:S(2)}) %all-to-all-start) | async-done | bytes 1048608 | tf_op jit(solution)/shard_map/all_to_all | solution.py:452
  33.3 0.0 copy-start.1
  33.3 4.1 %all-to-all-start.1 = ((bf16[32,5,32,128]{3,2,1,0:T(8,128)(2,1)}), bf16[32,5,32,128]{3,2,1,0:T(8,128)(2,1)S(1)}, u32[]{:S(2)}, u32[]{:S(2)}) async-start(bf16[32,5,32,128]{3,2,1,0:T(8,128)(2,1)} %gate.2), calls=%async_computation.1 | async-start | bytes 2621440 | tf_op jit(solution)/shard_map/all_to_all | solution.py:452
  37.4 2.4 %collective-permute-start.2 = (bf16[32,4,32,128]{3,2,1,0:T(8,128)(2,1)}, bf16[32,4,32,128]{3,2,1,0:T(8,128)(2,1)}, u32[]{:S(2)}, u32[]{:S(2)}) collective-permute-start(bf16[32,4,32,128]{3,2,1,0:T(8,128)(2,1)} %all-to-all-done.refs_1_.own_ref), channel_id=1, source_target_pairs={{0,32},{32,64},{64,96},{96,128},{128,160},{160,192},{192,224},{224... | collective-permute-start | bytes 3145736 | tf_op jit(solution)/shard_map/ppermute | solution.py:455
  39.9 0.0 copy-done.1
  39.9 0.0 copy-start.2
  39.9 1.0 copy-done.2
  40.9 0.2 cut.2.refs_0_
  41.1 16.1 %all-to-all-done.1.refs_1_.up_ref.q_ref.kv_ref = bf16[32,5,32,128]{3,2,1,0:T(8,128)(2,1)S(1)} async-done(((bf16[32,5,32,128]{3,2,1,0:T(8,128)(2,1)}), bf16[32,5,32,128]{3,2,1,0:T(8,128)(2,1)S(1)}, u32[]{:S(2)}, u32[]{:S(2)}) %all-to-all-start.1) | async-done | bytes 1310752 | tf_op jit(solution)/shard_map/all_to_all | solution.py:452
  57.2 0.0 copy-start
  57.2 1.1 copy-done
  58.3 4.0 %all-to-all-start.2 = ((bf16[32,5,32,128]{3,2,1,0:T(8,128)(2,1)}), bf16[32,5,32,128]{3,2,1,0:T(8,128)(2,1)S(1)}, u32[]{:S(2)}, u32[]{:S(2)}) async-start(bf16[32,5,32,128]{3,2,1,0:T(8,128)(2,1)} %copy-done), calls=%async_computation.2 | async-start | bytes 2621440 | tf_op jit(solution)/shard_map/all_to_all | solution.py:452
  62.3 2.4 %ahead.2.rest_0_ = bf16[1,1056,128]{2,1,0:T(8,128)(2,1)S(1)} custom-call(s32[4]{0:T(128)S(1)} %flags.1.refs_2_.flags_ref, bf16[32,5,32,128]{3,2,1,0:T(8,128)(2,1)S(1)} %all-to-all-done.1.refs_1_.up_ref.q_ref.kv_ref, bf16[32,5,32,128]{3,2,1,0:T(8,128)(2,1)S(1)} %all-to-all-done.1.refs_1_.up_ref.q_ref.kv_ref), custom_call_target="tpu_custom_call" | custom-call | flops 536870912 | bytes 1048576 | tf_op jit(solution)/shard_map/ahead/pallas_call | solution.py:275
  64.7 1.2 %collective-permute-done.2.up_ref.kv_ref = bf16[32,4,32,128]{3,2,1,0:T(8,128)(2,1)} collective-permute-done((bf16[32,4,32,128]{3,2,1,0:T(8,128)(2,1)}, bf16[32,4,32,128]{3,2,1,0:T(8,128)(2,1)}, u32[]{:S(2)}, u32[]{:S(2)}) %collective-permute-start.2) | collective-permute-done | bytes 1048608 | tf_op jit(solution)/shard_map/ppermute | solution.py:455
  66.0 5.7 %ahead.3 = bf16[2,1056,128]{2,1,0:T(8,128)(2,1)} custom-call(s32[4]{0:T(128)S(1)} %flags.1.refs_2_.flags_ref, bf16[32,5,32,128]{3,2,1,0:T(8,128)(2,1)S(1)} %all-to-all-done.1.refs_1_.up_ref.q_ref.kv_ref, bf16[32,4,32,128]{3,2,1,0:T(8,128)(2,1)} %collective-permute-done.2.up_ref.kv_ref, bf16[1,1056,128]{2,1,0:T(8,128)(2,1)S(1)} %ahead.2.rest_0_), custom_call_target="tpu_custom_call" | custom-call | flops 1073741824 | bytes 2097152 | tf_op jit(solution)/shard_map/ahead/pallas_call | solution.py:275
  71.7 1.9 %collective-permute-start.3 = (bf16[2,1056,128]{2,1,0:T(8,128)(2,1)}, bf16[2,1056,128]{2,1,0:T(8,128)(2,1)S(1)}, u32[]{:S(2)}, u32[]{:S(2)}) collective-permute-start(bf16[2,1056,128]{2,1,0:T(8,128)(2,1)} %ahead.3), channel_id=1, source_target_pairs={{0,32},{32,64},{64,96},{96,128},{128,160},{160,192},{192,224},{224... | collective-permute-start | bytes 1622024 | tf_op jit(solution)/shard_map/ppermute | solution.py:455
  73.6 1.9 %collective-permute-start.4 = (bf16[1,1056,128]{2,1,0:T(8,128)(2,1)S(1)}, bf16[1,1056,128]{2,1,0:T(8,128)(2,1)}, u32[]{:S(2)}, u32[]{:S(2)}) collective-permute-start(bf16[1,1056,128]{2,1,0:T(8,128)(2,1)S(1)} %ahead.2.rest_0_), channel_id=1, source_target_pairs={{0,32},{32,64},{64,96},{96,128},{128,160},{160,192},{192,224},{224... | collective-permute-start | bytes 811016 | tf_op jit(solution)/shard_map/ppermute | solution.py:455
  75.5 6.6 %all-to-all-done.2.q_ref.own_ref = bf16[32,5,32,128]{3,2,1,0:T(8,128)(2,1)S(1)} async-done(((bf16[32,5,32,128]{3,2,1,0:T(8,128)(2,1)}), bf16[32,5,32,128]{3,2,1,0:T(8,128)(2,1)S(1)}, u32[]{:S(2)}, u32[]{:S(2)}) %all-to-all-start.2) | async-done | bytes 1310752 | tf_op jit(solution)/shard_map/all_to_all | solution.py:452
  82.2 1.9 %near.3 = (f32[1,1024,128]{2,1,0:T(8,128)S(1)}, f32[1,8,128]{2,1,0:T(8,128)S(1)}) custom-call(s32[4]{0:T(128)S(1)} %flags.1.refs_2_.flags_ref, bf16[32,5,32,128]{3,2,1,0:T(8,128)(2,1)S(1)} %all-to-all-done.2.q_ref.own_ref, bf16[32,5,32,128]{3,2,1,0:T(8,128)(2,1)S(1)} %all-to-all-done.2.q_ref.own_ref, ...), custom_call_target="tpu_custom_call" | custom-call | flops 858993472 | bytes 1835008 | tf_op jit(solution)/shard_map/near/pallas_call | solution.py:289
  84.1 4.5 %near.2 = (f32[2,1024,128]{2,1,0:T(8,128)S(1)}, f32[2,8,128]{2,1,0:T(8,128)S(1)}) custom-call(s32[4]{0:T(128)S(1)} %flags.1.refs_2_.flags_ref, bf16[32,5,32,128]{3,2,1,0:T(8,128)(2,1)S(1)} %all-to-all-done.2.q_ref.own_ref, bf16[32,4,32,128]{3,2,1,0:T(8,128)(2,1)} %all-to-all-done.refs_1_.own_ref, bf16[32,4,32,128]{3,2,1,0:T(8,128)(2,1)} %collective-permute-done.2.up_ref.kv_ref), custom_call_target="tpu_custom_call" | custom-call | flops 1717986944 | bytes 3670016 | tf_op jit(solution)/shard_map/near/pallas_call | solution.py:289
  88.6 5.3 %collective-permute-done.4.far_b = bf16[1,1056,128]{2,1,0:T(8,128)(2,1)} collective-permute-done((bf16[1,1056,128]{2,1,0:T(8,128)(2,1)S(1)}, bf16[1,1056,128]{2,1,0:T(8,128)(2,1)}, u32[]{:S(2)}, u32[]{:S(2)}) %collective-permute-start.4) | collective-permute-done | bytes 270368 | tf_op jit(solution)/shard_map/ppermute | solution.py:455
  94.0 0.0 collective-permute-done.3.far_a
  94.0 1.2 %merge.1 = bf16[32,3,32,128]{3,2,1,0:T(8,128)(2,1)S(1)} custom-call(s32[4]{0:T(128)S(1)} %flags.1.refs_2_.flags_ref, f32[2,1024,128]{2,1,0:T(8,128)S(1)} %get-tuple-element.13.near_a, f32[1,1024,128]{2,1,0:T(8,128)S(1)} %get-tuple-element.14.near_b, f32[2,8,128]{2,1,0:T(8,128)S(1)} %get-tuple-element.15.log_a, f32[1,8,128]{2,1,0:T(8,128)S(1)} %get-tuple-element.16.log_b, ...), custom_call_target="tpu_custom_call" | custom-call | bytes 3145728 | tf_op jit(solution)/shard_map/merge/pallas_call | solution.py:306
  95.2 22.5 %all_to_all.20.in_ref = bf16[32,3,32,128]{3,2,1,0:T(8,128)(2,1)S(1)} all-to-all(bf16[32,3,32,128]{3,2,1,0:T(8,128)(2,1)S(1)} %merge.1), channel_id=1, replica_groups=mesh['grp'=16,'ctx'=32] {'ctx'}, dimensions={0} | all-to-all | bytes 1572864 | tf_op jit(solution)/shard_map/all_to_all | solution.py:452
  117.8 1.0 paste.1
  (2 shorter events, 0.0 us)
Async XLA Ops:
  0.0 22.2 %collective-permute-start = (bf16[256,1536]{1,0:T(8,128)(2,1)}, bf16[256,1536]{1,0:T(8,128)(2,1)S(1)}, u32[]{:S(2)}, u32[]{:S(2)}) collective-permute-start(bf16[256,1536]{1,0:T(8,128)(2,1)} %whole_ref.1), channel_id=1, source_target_pairs={{32,0},{64,32},{96,64},{128,96},{160,128},{192,160},{224,192},{256... | collective-permute-start | bytes 2359304 | tf_op jit(solution)/shard_map/ppermute | solution.py:458
  6.3 10.1 %copy-start.3 = (s32[16,8,2]{0,2,1:T(2,128)S(1)}, s32[16,8,2]{0,2,1:T(2,128)}, u32[]{:S(2)}) copy-start(s32[16,8,2]{0,2,1:T(2,128)} %param.8) | copy-start | bytes 3076
  6.3 10.2 %copy-start.4 = (s32[16,8]{0,1:T(8,128)S(1)}, s32[16,8]{0,1:T(8,128)}, u32[]{:S(2)}) copy-start(s32[16,8]{0,1:T(8,128)} %param.9) | copy-start | bytes 1540
  6.3 15.9 %collective-permute-start.1 = (bf16[32,2,32,128]{3,2,1,0:T(8,128)(2,1)}, bf16[32,2,32,128]{3,2,1,0:T(8,128)(2,1)S(1)}, u32[]{:S(2)}, u32[]{:S(2)}) collective-permute-start(bf16[32,2,32,128]{3,2,1,0:T(8,128)(2,1)} %get-tuple-element.11.piece_ref), channel_id=1, source_target_pairs={{0,32},{32,64},{64,96},{96,128},{128,160},{160,192},{192,224},{224... | collective-permute-start | bytes 1572872 | tf_op jit(solution)/shard_map/ppermute | solution.py:455
  8.2 25.1 %all-to-all-start = ((bf16[32,4,32,128]{3,2,1,0:T(8,128)(2,1)}), bf16[32,4,32,128]{3,2,1,0:T(8,128)(2,1)}, u32[]{:S(2)}, u32[]{:S(2)}) async-start(bf16[32,4,32,128]{3,2,1,0:T(8,128)(2,1)} %get-tuple-element.12), calls=%async_computation | async-start | bytes 2097152 | tf_op jit(solution)/shard_map/all_to_all | solution.py:452
  33.3 6.5 %copy-start.1 = (bf16[256,1536]{1,0:T(8,128)(2,1)S(1)}, bf16[256,1536]{1,0:T(8,128)(2,1)}, u32[]{:S(2)}) copy-start(bf16[256,1536]{1,0:T(8,128)(2,1)} %whole_ref.1) | copy-start | bytes 2359300
  33.3 23.9 %all-to-all-start.1 = ((bf16[32,5,32,128]{3,2,1,0:T(8,128)(2,1)}), bf16[32,5,32,128]{3,2,1,0:T(8,128)(2,1)S(1)}, u32[]{:S(2)}, u32[]{:S(2)}) async-start(bf16[32,5,32,128]{3,2,1,0:T(8,128)(2,1)} %gate.2), calls=%async_computation.1 | async-start | bytes 2621440 | tf_op jit(solution)/shard_map/all_to_all | solution.py:452
  37.4 28.5 %collective-permute-start.2 = (bf16[32,4,32,128]{3,2,1,0:T(8,128)(2,1)}, bf16[32,4,32,128]{3,2,1,0:T(8,128)(2,1)}, u32[]{:S(2)}, u32[]{:S(2)}) collective-permute-start(bf16[32,4,32,128]{3,2,1,0:T(8,128)(2,1)} %all-to-all-done.refs_1_.own_ref), channel_id=1, source_target_pairs={{0,32},{32,64},{64,96},{96,128},{128,160},{160,192},{192,224},{224... | collective-permute-start | bytes 3145736 | tf_op jit(solution)/shard_map/ppermute | solution.py:455
  39.9 1.0 copy-start.2
  57.2 1.1 copy-start
  58.3 23.9 %all-to-all-start.2 = ((bf16[32,5,32,128]{3,2,1,0:T(8,128)(2,1)}), bf16[32,5,32,128]{3,2,1,0:T(8,128)(2,1)S(1)}, u32[]{:S(2)}, u32[]{:S(2)}) async-start(bf16[32,5,32,128]{3,2,1,0:T(8,128)(2,1)} %copy-done), calls=%async_computation.2 | async-start | bytes 2621440 | tf_op jit(solution)/shard_map/all_to_all | solution.py:452
  71.7 22.3 %collective-permute-start.3 = (bf16[2,1056,128]{2,1,0:T(8,128)(2,1)}, bf16[2,1056,128]{2,1,0:T(8,128)(2,1)S(1)}, u32[]{:S(2)}, u32[]{:S(2)}) collective-permute-start(bf16[2,1056,128]{2,1,0:T(8,128)(2,1)} %ahead.3), channel_id=1, source_target_pairs={{0,32},{32,64},{64,96},{96,128},{128,160},{160,192},{192,224},{224... | collective-permute-start | bytes 1622024 | tf_op jit(solution)/shard_map/ppermute | solution.py:455
  73.6 20.4 %collective-permute-start.4 = (bf16[1,1056,128]{2,1,0:T(8,128)(2,1)S(1)}, bf16[1,1056,128]{2,1,0:T(8,128)(2,1)}, u32[]{:S(2)}, u32[]{:S(2)}) collective-permute-start(bf16[1,1056,128]{2,1,0:T(8,128)(2,1)S(1)} %ahead.2.rest_0_), channel_id=1, source_target_pairs={{0,32},{32,64},{64,96},{96,128},{128,160},{160,192},{192,224},{224... | collective-permute-start | bytes 811016 | tf_op jit(solution)/shard_map/ppermute | solution.py:455

commit v6 on v4

--- a/solution.py
+++ b/solution.py
@@ -26,7 +26,7 @@
 ANY = pl.BlockSpec(memory_space=pl.ANY)
 HBM = pl.BlockSpec(memory_space=pltpu.HBM)
 SMALL = pltpu.CompilerParams(vmem_limit_bytes=2**20)
-PARAMS = pltpu.CompilerParams(vmem_limit_bytes=8 * 2**20)
+PARAMS = pltpu.CompilerParams(vmem_limit_bytes=10 * 2**20)
 
 
 def is_taken(groups_ref, count_ref, group, distance):
@@ -216,8 +216,9 @@
         run(False)
 
 
-def merge_kernel(flags_ref, near_a, near_b, log_a, log_b, far_a, far_b, out_ref):
-    rows = near_a.shape[1]
+def merge_kernel(flags_ref, near_ref, log_ref, far_ref, *rest):
+    out_ref = rest[-1]
+    heads, rows, _ = near_ref.shape
     blocks = rows // HD
     taken = flags_ref[1] > 0
 
@@ -226,29 +227,34 @@
         frames = pl.ds(block * count, count)
         out_ref[frames, head] = value.astype(jnp.bfloat16).reshape(count, POSITIONS, HD)
 
-    def each_head():
-        count = near_a.shape[0]
-        for head in range(PARTS):
-            refs = (near_a, log_a, far_a) if head < count else (near_b, log_b, far_b)
-            yield (head,) + tuple(ref.at[head if head < count else head - count] for ref in refs)
+    for other in rest[:-1]:
+        out_ref[:, heads:] = other[...]
 
     @pl.when(taken)
     def _():
-        for head, near_ref, log_ref, far_ref in each_head():
-            pieces = far_ref[pl.ds(rows, STAT_ROWS), :].astype(jnp.float32)
+        for head in range(heads):
+            pieces = far_ref[head, pl.ds(rows, STAT_ROWS), :].astype(jnp.float32)
             far_log = pieces[:blocks] + pieces[blocks : 2 * blocks] + pieces[2 * blocks : 3 * blocks]
-            shares = jnp.transpose(1.0 / (1.0 + jnp.exp2(log_ref[...] - far_log)))
+            shares = jnp.transpose(1.0 / (1.0 + jnp.exp2(log_ref[head] - far_log)))
             for block in range(blocks):
                 part = pl.ds(block * HD, HD)
-                near = near_ref[part, :]
-                far = far_ref[part, :].astype(jnp.float32)
+                near = near_ref[head, part, :]
+                far = far_ref[head, part, :].astype(jnp.float32)
                 put(head, block, near + (far - near) * shares[:, block : block + 1])
 
     @pl.when(jnp.logical_not(taken))
     def _():
-        for head, near_ref, _, _ in each_head():
+        for head in range(heads):
             for block in range(blocks):
-                put(head, block, near_ref[pl.ds(block * HD, HD), :])
+                put(head, block, near_ref[head, pl.ds(block * HD, HD), :])
+
+
+def near_merged_kernel(query_slab, own_slab, up_slab, flags_ref, q_ref, own_ref, up_ref, *rest):
+    far_ref, out_ref, near_ref, log_ref = rest
+    near_kernel(
+        query_slab, own_slab, up_slab, flags_ref, q_ref, own_ref, up_ref, near_ref, log_ref
+    )
+    merge_kernel(flags_ref, near_ref, log_ref, far_ref, out_ref)
 
 
 def cost(passes, rows, heads, moved):
@@ -259,7 +265,7 @@
     )
 
 
-def attend_ahead(flags, heads, query, query_slab, pair, pair_slab, *waited):
+def attend_ahead(flags, heads, passes, query, query_slab, pair, pair_slab, *waited):
     rows = pair.shape[0] * POSITIONS
     return pl.pallas_call(
         functools.partial(ahead_kernel, query_slab, pair_slab),
@@ -267,7 +273,7 @@
         out_specs=VMEM,
         out_shape=jax.ShapeDtypeStruct((heads, rows + STAT_ROWS, HD), jnp.bfloat16),
         compiler_params=PARAMS,
-        cost_estimate=cost(1, rows, heads, rows * heads * HD * 8),
+        cost_estimate=cost(passes, rows, heads, rows * heads * HD * 8),
         name="ahead",
     )(flags, query, pair, *waited)
 
@@ -283,22 +289,41 @@
             jax.ShapeDtypeStruct((heads, rows // HD, HD), jnp.float32),
         ],
         compiler_params=PARAMS,
-        cost_estimate=cost(1.6, rows, heads, rows * heads * HD * 14),
+        cost_estimate=cost(160, rows, heads, rows * heads * HD * 14),
         name="near",
     )(flags, query, own, up)
 
 
-def merge(flags, near, logs, far):
-    rows = near[0].shape[1]
+def attend_near_merged(flags, query, query_slab, own, own_slab, up, up_slab, far):
+    frames = query.shape[0]
+    rows = frames * POSITIONS
+    return pl.pallas_call(
+        functools.partial(near_merged_kernel, query_slab, own_slab, up_slab),
+        in_specs=[SMEM] + [VMEM] * 4,
+        out_specs=VMEM,
+        out_shape=jax.ShapeDtypeStruct((frames, 1, POSITIONS, HD), jnp.bfloat16),
+        scratch_shapes=[
+            pltpu.VMEM((1, rows, HD), jnp.float32),
+            pltpu.VMEM((1, rows // HD, HD), jnp.float32),
+        ],
+        compiler_params=PARAMS,
+        cost_estimate=cost(1.6, rows, 1, rows * HD * 14),
+        name="near_merged",
+    )(flags, query, own, up, far)
+
+
+def merge(flags, near, logs, far, *others):
+    heads, rows, _ = near.shape
+    slabs = heads + sum(other.shape[1] for other in others)
     return pl.pallas_call(
         merge_kernel,
-        in_specs=[SMEM] + [VMEM] * 6,
+        in_specs=[SMEM] + [VMEM] * (3 + len(others)),
         out_specs=VMEM,
-        out_shape=jax.ShapeDtypeStruct((rows // POSITIONS, PARTS, POSITIONS, HD), jnp.bfloat16),
+        out_shape=jax.ShapeDtypeStruct((rows // POSITIONS, slabs, POSITIONS, HD), jnp.bfloat16),
         compiler_params=PARAMS,
-        cost_estimate=cost(0, rows, PARTS, rows * PARTS * HD * 8),
+        cost_estimate=cost(0, rows, heads, rows * heads * HD * 8),
         name="merge",
-    )(flags, *near, *logs, *far)
+    )(flags, near, logs, far, *others)
 
 
 def cut_first_kernel(k_ref, v_ref, first_ref, last_ref, held_ref, first_piece, last_piece, *sems):
@@ -365,11 +390,11 @@
     del refs
 
 
-def gate(passed, *waited):
+def gate(space, passed, *waited):
     return pl.pallas_call(
         gate_kernel,
-        in_specs=[ANY] * (1 + len(waited)),
-        out_specs=ANY,
+        in_specs=[space] + [ANY] * len(waited),
+        out_specs=space,
         out_shape=jax.ShapeDtypeStruct(passed.shape, passed.dtype),
         input_output_aliases={0: 0},
         compiler_params=SMALL,
@@ -398,6 +423,27 @@
         compiler_params=PARAMS,
         cost_estimate=pl.CostEstimate(flops=flops, bytes_accessed=2**21, transcendentals=0),
         name="cut",
+    )(whole, piece)
+
+
+def cut_out_kernel(whole_ref, piece_ref, out_ref, held_ref, sem):
+    cut_kernel(whole_ref, piece_ref, held_ref)
+    copy = pltpu.make_async_copy(held_ref, out_ref, sem)
+    copy.start()
+    copy.wait()
+
+
+def cut_out(whole, piece):
+    shape = (NWIN * SPAN, PARTS + piece.shape[1], POSITIONS, HD)
+    return pl.pallas_call(
+        cut_out_kernel,
+        in_specs=[VMEM] * 2,
+        out_specs=HBM,
+        out_shape=jax.ShapeDtypeStruct(shape, jnp.bfloat16),
+        scratch_shapes=[pltpu.VMEM(shape, jnp.bfloat16), pltpu.SemaphoreType.DMA],
+        compiler_params=pltpu.CompilerParams(vmem_limit_bytes=60 * 2**20),
+        cost_estimate=pl.CostEstimate(flops=10**6, bytes_accessed=2**21, transcendentals=0),
+        name="cut_out",
     )(whole, piece)
 
 
@@ -450,15 +496,14 @@
     first = to_peers(first)
     first_up = up(first)
     flags = make_flags(chosen_groups, chosen_count)
-    second = to_peers(gate(cut(later_query, last_up, 10**11), first, flags))
-    third = to_peers(gate(cut(query_vectors, last, 10**6), second))
-    ahead_b = attend_ahead(flags, 1, second, 2, second, 3)
+    second = to_peers(gate(ANY, cut(later_query, last_up, 10**11), first, flags))
+    third = to_peers(gate(HBM, cut_out(query_vectors, last), second))
+    ahead_b = attend_ahead(flags, 1, 1, second, 2, second, 3)
     far_b = up(ahead_b)
-    far_a = up(attend_ahead(flags, 2, second, 0, first_up, 0, ahead_b))
-    near_b, log_b = attend_near(flags, 1, third, 2, third, 3, second, 3)
-    near_a, log_a = attend_near(flags, 2, third, 0, first, 0, first_up, 0)
-    merged = merge(flags, (near_a, near_b), (log_a, log_b), (far_a, far_b))
-    return paste(to_peers(merged))
+    far_a = up(attend_ahead(flags, 2, 4, second, 0, first_up, 0, ahead_b))
+    merged = attend_near_merged(flags, third, 2, third, 3, second, 3, far_b)
+    near, logs = attend_near(flags, 2, third, 0, first, 0, first_up, 0)
+    return paste(to_peers(merge(flags, near, logs, far_a, merged)))
 
 
 def solution(mesh):

time: 119 us -> 117 us (0.983)
  the two profiles are of different devices: /device:TPU:385 before, /device:TPU:65 now
where the time goes in v6:
time: 117 us
  waiting for transfers between devices  32.2 us (28%)
  starting transfers between devices  31.4 us (27%)
  Pallas kernels  30.1 us (26%)
  blocking collectives  19.9 us (17%)
  local copies, waits for them, and re-layouts  2.6 us (2%)
    all_to_all x3, waiting for transfers between devices, to_peers(): return lax.all_to_all(block, 'ctx', split_axis=0, concat_axis=0, tiled=True)  30 us
    all_to_all x1, blocking collectives, to_peers(): return lax.all_to_all(block, 'ctx', split_axis=0, concat_axis=0, tiled=True)  19.9 us
    all_to_all x3, starting transfers between devices, to_peers(): return lax.all_to_all(block, 'ctx', split_axis=0, concat_axis=0, tiled=True)  16.1 us
    ppermute x4, starting transfers between devices, up(): lax.ppermute(block, 'grp', [(at, at + 1) for at in range(group_devices -...  13.3 us
    pallas_call x2, Pallas kernels, attend_ahead(): pl.pallas_call(functools.partial(ahead_kernel, query_slab, pair_slab), in...  8.23 us
    pallas_call x1, Pallas kernels, attend_near(): pl.pallas_call(functools.partial(near_kernel, query_slab, own_slab, up_sl...  6.74 us
    pallas_call x1, Pallas kernels, attend_near_merged(): pl.pallas_call(functools.partial(near_merged_kernel, query_slab, own_slab...  4.1 us
    unnamed x10, local copies, waits for them, and re-layouts  2.6 us
  transfers between devices with their start and end apart: 8, of which 4 were waited for; matrix products, arithmetic and copies ran while one was open for 0% of the time, Pallas kernels for 24%

profile of v6, /device:TPU:65, one launch (start us, length us, event | category | flops | bytes accessed | tf_op | source)
XLA Modules:
  0.0 116.5 jit_solution(6659515024554338353)
XLA Ops:
  0.0 1.9 %collective-permute-start = (bf16[256,1536]{1,0:T(8,128)(2,1)}, bf16[256,1536]{1,0:T(8,128)(2,1)S(1)}, u32[]{:S(2)}, u32[]{:S(2)}) collective-permute-start(bf16[256,1536]{1,0:T(8,128)(2,1)} %whole_ref.1), channel_id=1, source_target_pairs={{32,0},{64,32},{96,64},{128,96},{160,128},{192,160},{224,192},{256... | collective-permute-start | bytes 2359304 | tf_op jit(solution)/shard_map/ppermute | solution.py:491
  1.9 2.4 %cut_first.1 = (bf16[32,4,32,128]{3,2,1,0:T(8,128)(2,1)}, bf16[32,2,32,128]{3,2,1,0:T(8,128)(2,1)}) custom-call(bf16[256,1536]{1,0:T(8,128)(2,1)} %k_ref.1, bf16[256,1536]{1,0:T(8,128)(2,1)} %v_ref.1), custom_call_target="tpu_custom_call" | custom-call | tf_op jit(solution)/shard_map/cut_first/pallas_call | solution.py:371
  4.4 0.0 copy-start.2
  4.4 0.0 copy-start.3
  4.4 3.5 %collective-permute-start.1 = (bf16[32,2,32,128]{3,2,1,0:T(8,128)(2,1)}, bf16[32,2,32,128]{3,2,1,0:T(8,128)(2,1)S(1)}, u32[]{:S(2)}, u32[]{:S(2)}) collective-permute-start(bf16[32,2,32,128]{3,2,1,0:T(8,128)(2,1)} %get-tuple-element.9.piece_ref), channel_id=1, source_target_pairs={{0,32},{32,64},{64,96},{96,128},{128,160},{160,192},{192,224},{224... | collective-permute-start | bytes 1572872 | tf_op jit(solution)/shard_map/ppermute | solution.py:488
  7.9 8.2 %all-to-all-start = ((bf16[32,4,32,128]{3,2,1,0:T(8,128)(2,1)}), bf16[32,4,32,128]{3,2,1,0:T(8,128)(2,1)}, u32[]{:S(2)}, u32[]{:S(2)}) async-start(bf16[32,4,32,128]{3,2,1,0:T(8,128)(2,1)} %get-tuple-element.10), calls=%async_computation | async-start | bytes 2097152 | tf_op jit(solution)/shard_map/all_to_all | solution.py:485
  16.2 0.0 copy-done.2
  16.2 0.1 copy.8.groups_ref
  16.3 0.0 copy-done.3
  16.3 0.1 copy.9.count_ref
  16.4 2.4 %flags.1.refs_2_.flags_ref = s32[4]{0:T(128)S(1)} custom-call(s32[16,8,2]{2,1,0:T(8,128)S(1)} %copy.8.groups_ref, s32[16,8]{1,0:T(8,128)S(1)} %copy.9.count_ref), custom_call_target="tpu_custom_call" | custom-call | tf_op jit(solution)/shard_map/flags/pallas_call | solution.py:52
  18.7 0.0 collective-permute-done.1.piece_ref
  18.8 2.2 %collective-permute-done.whole_ref = bf16[256,1536]{1,0:T(8,128)(2,1)S(1)} collective-permute-done((bf16[256,1536]{1,0:T(8,128)(2,1)}, bf16[256,1536]{1,0:T(8,128)(2,1)S(1)}, u32[]{:S(2)}, u32[]{:S(2)}) %collective-permute-start) | collective-permute-done | bytes 786464 | tf_op jit(solution)/shard_map/ppermute | solution.py:491
  21.0 1.2 %cut.1.refs_0_ = bf16[32,5,32,128]{3,2,1,0:T(8,128)(2,1)} custom-call(bf16[256,1536]{1,0:T(8,128)(2,1)S(1)} %collective-permute-done.whole_ref, bf16[32,2,32,128]{3,2,1,0:T(8,128)(2,1)S(1)} %collective-permute-done.1.piece_ref), custom_call_target="tpu_custom_call" | custom-call | flops 99999997952 | bytes 2097152 | tf_op jit(solution)/shard_map/cut/pallas_call | solution.py:418
  22.2 10.9 %all-to-all-done.refs_1_.own_ref = bf16[32,4,32,128]{3,2,1,0:T(8,128)(2,1)} async-done(((bf16[32,4,32,128]{3,2,1,0:T(8,128)(2,1)}), bf16[32,4,32,128]{3,2,1,0:T(8,128)(2,1)}, u32[]{:S(2)}, u32[]{:S(2)}) %all-to-all-start) | async-done | bytes 1048608 | tf_op jit(solution)/shard_map/all_to_all | solution.py:485
  33.1 4.0 %all-to-all-start.1 = ((bf16[32,5,32,128]{3,2,1,0:T(8,128)(2,1)}), bf16[32,5,32,128]{3,2,1,0:T(8,128)(2,1)S(1)}, u32[]{:S(2)}, u32[]{:S(2)}) async-start(bf16[32,5,32,128]{3,2,1,0:T(8,128)(2,1)} %gate.2), calls=%async_computation.1 | async-start | bytes 2621440 | tf_op jit(solution)/shard_map/all_to_all | solution.py:485
  37.1 4.8 %collective-permute-start.2 = (bf16[32,4,32,128]{3,2,1,0:T(8,128)(2,1)}, bf16[32,4,32,128]{3,2,1,0:T(8,128)(2,1)}, u32[]{:S(2)}, u32[]{:S(2)}) collective-permute-start(bf16[32,4,32,128]{3,2,1,0:T(8,128)(2,1)} %all-to-all-done.refs_1_.own_ref), channel_id=1, source_target_pairs={{0,32},{32,64},{64,96},{96,128},{128,160},{160,192},{192,224},{224... | collective-permute-start | bytes 3145736 | tf_op jit(solution)/shard_map/ppermute | solution.py:488
  41.8 2.5 %cut_out.1.refs_0_ = bf16[32,5,32,128]{3,2,1,0:T(8,128)(2,1)} custom-call(bf16[256,1536]{1,0:T(8,128)(2,1)} %whole_ref.1, bf16[32,2,32,128]{3,2,1,0:T(8,128)(2,1)} %get-tuple-element.9.piece_ref), custom_call_target="tpu_custom_call" | custom-call | flops 1000000 | bytes 2097152 | tf_op jit(solution)/shard_map/cut_out/pallas_call | solution.py:438
  44.4 12.5 %all-to-all-done.1.refs_1_.q_ref.kv_ref.up_ref = bf16[32,5,32,128]{3,2,1,0:T(8,128)(2,1)S(1)} async-done(((bf16[32,5,32,128]{3,2,1,0:T(8,128)(2,1)}), bf16[32,5,32,128]{3,2,1,0:T(8,128)(2,1)S(1)}, u32[]{:S(2)}, u32[]{:S(2)}) %all-to-all-start.1) | async-done | bytes 1310752 | tf_op jit(solution)/shard_map/all_to_all | solution.py:485
  56.9 0.0 copy-start
  56.9 1.3 %copy-done = bf16[32,5,32,128]{3,2,1,0:T(8,128)(2,1)S(1)} copy-done((bf16[32,5,32,128]{3,2,1,0:T(8,128)(2,1)S(1)}, bf16[32,5,32,128]{3,2,1,0:T(8,128)(2,1)}, u32[]{:S(2)}) %copy-start) | copy-done | bytes 1310744
  58.2 0.0 copy-start.1
  58.2 1.1 copy-done.1
  59.3 4.0 %all-to-all-start.2 = ((bf16[32,5,32,128]{3,2,1,0:T(8,128)(2,1)}), bf16[32,5,32,128]{3,2,1,0:T(8,128)(2,1)S(1)}, u32[]{:S(2)}, u32[]{:S(2)}) async-start(bf16[32,5,32,128]{3,2,1,0:T(8,128)(2,1)} %copy-done.1), calls=%async_computation.2 | async-start | bytes 2621440 | tf_op jit(solution)/shard_map/all_to_all | solution.py:485
  63.3 2.9 %ahead.2.rest_0_ = bf16[1,1056,128]{2,1,0:T(8,128)(2,1)} custom-call(s32[4]{0:T(128)S(1)} %flags.1.refs_2_.flags_ref, bf16[32,5,32,128]{3,2,1,0:T(8,128)(2,1)S(1)} %all-to-all-done.1.refs_1_.q_ref.kv_ref.up_ref, bf16[32,5,32,128]{3,2,1,0:T(8,128)(2,1)S(1)} %all-to-all-done.1.refs_1_.q_ref.kv_ref.up_ref), custom_call_target="tpu_custom_call" | custom-call | flops 536870912 | bytes 1048576 | tf_op jit(solution)/shard_map/ahead/pallas_call | solution.py:270
  66.2 3.1 %collective-permute-start.4 = (bf16[1,1056,128]{2,1,0:T(8,128)(2,1)}, bf16[1,1056,128]{2,1,0:T(8,128)(2,1)}, u32[]{:S(2)}, u32[]{:S(2)}) collective-permute-start(bf16[1,1056,128]{2,1,0:T(8,128)(2,1)} %ahead.2.rest_0_), channel_id=1, source_target_pairs={{0,32},{32,64},{64,96},{96,128},{128,160},{160,192},{192,224},{224... | collective-permute-start | bytes 811016 | tf_op jit(solution)/shard_map/ppermute | solution.py:488
  69.3 0.0 collective-permute-done.2.up_ref.kv_ref
  69.3 5.3 %ahead.3 = bf16[2,1056,128]{2,1,0:T(8,128)(2,1)} custom-call(s32[4]{0:T(128)S(1)} %flags.1.refs_2_.flags_ref, bf16[32,5,32,128]{3,2,1,0:T(8,128)(2,1)S(1)} %all-to-all-done.1.refs_1_.q_ref.kv_ref.up_ref, bf16[32,4,32,128]{3,2,1,0:T(8,128)(2,1)} %collective-permute-done.2.up_ref.kv_ref, bf16[1,1056,128]{2,1,0:T(8,128)(2,1)} %ahead.2.rest_0_), custom_call_target="tpu_custom_call" | custom-call | flops 4294967296 | bytes 2097152 | tf_op jit(solution)/shard_map/ahead/pallas_call | solution.py:270
  74.6 1.9 %collective-permute-start.3 = (bf16[2,1056,128]{2,1,0:T(8,128)(2,1)}, bf16[2,1056,128]{2,1,0:T(8,128)(2,1)}, u32[]{:S(2)}, u32[]{:S(2)}) collective-permute-start(bf16[2,1056,128]{2,1,0:T(8,128)(2,1)} %ahead.3), channel_id=1, source_target_pairs={{0,32},{32,64},{64,96},{96,128},{128,160},{160,192},{192,224},{224... | collective-permute-start | bytes 1622024 | tf_op jit(solution)/shard_map/ppermute | solution.py:488
  76.5 6.6 %all-to-all-done.2.q_ref.own_ref = bf16[32,5,32,128]{3,2,1,0:T(8,128)(2,1)S(1)} async-done(((bf16[32,5,32,128]{3,2,1,0:T(8,128)(2,1)}), bf16[32,5,32,128]{3,2,1,0:T(8,128)(2,1)S(1)}, u32[]{:S(2)}, u32[]{:S(2)}) %all-to-all-start.2) | async-done | bytes 1310752 | tf_op jit(solution)/shard_map/all_to_all | solution.py:485
  83.1 6.7 %near.1 = (f32[2,1024,128]{2,1,0:T(8,128)S(1)}, f32[2,8,128]{2,1,0:T(8,128)S(1)}) custom-call(s32[4]{0:T(128)S(1)} %flags.1.refs_2_.flags_ref, bf16[32,5,32,128]{3,2,1,0:T(8,128)(2,1)S(1)} %all-to-all-done.2.q_ref.own_ref, bf16[32,4,32,128]{3,2,1,0:T(8,128)(2,1)} %all-to-all-done.refs_1_.own_ref, bf16[32,4,32,128]{3,2,1,0:T(8,128)(2,1)} %collective-permute-done.2.up_ref.kv_ref), custom_call_target="tpu_custom_call" | custom-call | flops 171798691840 | bytes 3670016 | tf_op jit(solution)/shard_map/near/pallas_call | solution.py:283
  89.9 0.0 collective-permute-done.4.rest_0_
  89.9 4.1 %near_merged.1.rest_0_ = bf16[32,1,32,128]{3,2,1,0:T(8,128)(2,1)S(1)} custom-call(s32[4]{0:T(128)S(1)} %flags.1.refs_2_.flags_ref, bf16[32,5,32,128]{3,2,1,0:T(8,128)(2,1)S(1)} %all-to-all-done.2.q_ref.own_ref, bf16[32,5,32,128]{3,2,1,0:T(8,128)(2,1)S(1)} %all-to-all-done.2.q_ref.own_ref, ...), custom_call_target="tpu_custom_call" | custom-call | flops 858993472 | bytes 1835008 | tf_op jit(solution)/shard_map/near_merged/pallas_call | solution.py:300
  94.0 0.0 collective-permute-done.3.far_ref
  94.0 1.5 %merge.1 = bf16[32,3,32,128]{3,2,1,0:T(8,128)(2,1)S(1)} custom-call(s32[4]{0:T(128)S(1)} %flags.1.refs_2_.flags_ref, f32[2,1024,128]{2,1,0:T(8,128)S(1)} %get-tuple-element.11.near_ref, f32[2,8,128]{2,1,0:T(8,128)S(1)} %get-tuple-element.12.log_ref, bf16[2,1056,128]{2,1,0:T(8,128)(2,1)} %collective-permute-done.3.far_ref, ...), custom_call_target="tpu_custom_call" | custom-call | bytes 2097152 | tf_op jit(solution)/shard_map/merge/pallas_call | solution.py:318
  95.6 19.9 %all_to_all.20.in_ref = bf16[32,3,32,128]{3,2,1,0:T(8,128)(2,1)S(1)} all-to-all(bf16[32,3,32,128]{3,2,1,0:T(8,128)(2,1)S(1)} %merge.1), channel_id=1, replica_groups=mesh['grp'=16,'ctx'=32] {'ctx'}, dimensions={0} | all-to-all | bytes 1572864 | tf_op jit(solution)/shard_map/all_to_all | solution.py:485
  115.4 1.0 paste.1
  (2 shorter events, 0.0 us)
Async XLA Ops:
  0.0 21.0 %collective-permute-start = (bf16[256,1536]{1,0:T(8,128)(2,1)}, bf16[256,1536]{1,0:T(8,128)(2,1)S(1)}, u32[]{:S(2)}, u32[]{:S(2)}) collective-permute-start(bf16[256,1536]{1,0:T(8,128)(2,1)} %whole_ref.1), channel_id=1, source_target_pairs={{32,0},{64,32},{96,64},{128,96},{160,128},{192,160},{224,192},{256... | collective-permute-start | bytes 2359304 | tf_op jit(solution)/shard_map/ppermute | solution.py:491
  4.4 11.8 %copy-start.2 = (s32[16,8,2]{0,2,1:T(2,128)S(1)}, s32[16,8,2]{0,2,1:T(2,128)}, u32[]{:S(2)}) copy-start(s32[16,8,2]{0,2,1:T(2,128)} %param.8) | copy-start | bytes 3076
  4.4 11.9 %copy-start.3 = (s32[16,8]{0,1:T(8,128)S(1)}, s32[16,8]{0,1:T(8,128)}, u32[]{:S(2)}) copy-start(s32[16,8]{0,1:T(8,128)} %param.9) | copy-start | bytes 1540
  4.4 14.4 %collective-permute-start.1 = (bf16[32,2,32,128]{3,2,1,0:T(8,128)(2,1)}, bf16[32,2,32,128]{3,2,1,0:T(8,128)(2,1)S(1)}, u32[]{:S(2)}, u32[]{:S(2)}) collective-permute-start(bf16[32,2,32,128]{3,2,1,0:T(8,128)(2,1)} %get-tuple-element.9.piece_ref), channel_id=1, source_target_pairs={{0,32},{32,64},{64,96},{96,128},{128,160},{160,192},{192,224},{224... | collective-permute-start | bytes 1572872 | tf_op jit(solution)/shard_map/ppermute | solution.py:488
  7.9 25.2 %all-to-all-start = ((bf16[32,4,32,128]{3,2,1,0:T(8,128)(2,1)}), bf16[32,4,32,128]{3,2,1,0:T(8,128)(2,1)}, u32[]{:S(2)}, u32[]{:S(2)}) async-start(bf16[32,4,32,128]{3,2,1,0:T(8,128)(2,1)} %get-tuple-element.10), calls=%async_computation | async-start | bytes 2097152 | tf_op jit(solution)/shard_map/all_to_all | solution.py:485
  33.1 23.8 %all-to-all-start.1 = ((bf16[32,5,32,128]{3,2,1,0:T(8,128)(2,1)}), bf16[32,5,32,128]{3,2,1,0:T(8,128)(2,1)S(1)}, u32[]{:S(2)}, u32[]{:S(2)}) async-start(bf16[32,5,32,128]{3,2,1,0:T(8,128)(2,1)} %gate.2), calls=%async_computation.1 | async-start | bytes 2621440 | tf_op jit(solution)/shard_map/all_to_all | solution.py:485
  37.1 32.2 %collective-permute-start.2 = (bf16[32,4,32,128]{3,2,1,0:T(8,128)(2,1)}, bf16[32,4,32,128]{3,2,1,0:T(8,128)(2,1)}, u32[]{:S(2)}, u32[]{:S(2)}) collective-permute-start(bf16[32,4,32,128]{3,2,1,0:T(8,128)(2,1)} %all-to-all-done.refs_1_.own_ref), channel_id=1, source_target_pairs={{0,32},{32,64},{64,96},{96,128},{128,160},{160,192},{192,224},{224... | collective-permute-start | bytes 3145736 | tf_op jit(solution)/shard_map/ppermute | solution.py:488
  56.9 1.3 %copy-start = (bf16[32,5,32,128]{3,2,1,0:T(8,128)(2,1)S(1)}, bf16[32,5,32,128]{3,2,1,0:T(8,128)(2,1)}, u32[]{:S(2)}) copy-start(bf16[32,5,32,128]{3,2,1,0:T(8,128)(2,1)} %cut_out.1.refs_0_) | copy-start | bytes 3932164
  58.2 1.1 copy-start.1
  59.3 23.9 %all-to-all-start.2 = ((bf16[32,5,32,128]{3,2,1,0:T(8,128)(2,1)}), bf16[32,5,32,128]{3,2,1,0:T(8,128)(2,1)S(1)}, u32[]{:S(2)}, u32[]{:S(2)}) async-start(bf16[32,5,32,128]{3,2,1,0:T(8,128)(2,1)} %copy-done.1), calls=%async_computation.2 | async-start | bytes 2621440 | tf_op jit(solution)/shard_map/all_to_all | solution.py:485
  66.2 23.7 %collective-permute-start.4 = (bf16[1,1056,128]{2,1,0:T(8,128)(2,1)}, bf16[1,1056,128]{2,1,0:T(8,128)(2,1)}, u32[]{:S(2)}, u32[]{:S(2)}) collective-permute-start(bf16[1,1056,128]{2,1,0:T(8,128)(2,1)} %ahead.2.rest_0_), channel_id=1, source_target_pairs={{0,32},{32,64},{64,96},{96,128},{128,160},{160,192},{192,224},{224... | collective-permute-start | bytes 811016 | tf_op jit(solution)/shard_map/ppermute | solution.py:488
  74.6 19.4 %collective-permute-start.3 = (bf16[2,1056,128]{2,1,0:T(8,128)(2,1)}, bf16[2,1056,128]{2,1,0:T(8,128)(2,1)}, u32[]{:S(2)}, u32[]{:S(2)}) collective-permute-start(bf16[2,1056,128]{2,1,0:T(8,128)(2,1)} %ahead.3), channel_id=1, source_target_pairs={{0,32},{32,64},{64,96},{96,128},{128,160},{160,192},{192,224},{224... | collective-permute-start | bytes 1622024 | tf_op jit(solution)/shard_map/ppermute | solution.py:488

commit v7 on v6

--- a/solution.py
+++ b/solution.py
@@ -441,7 +441,7 @@
         out_specs=HBM,
         out_shape=jax.ShapeDtypeStruct(shape, jnp.bfloat16),
         scratch_shapes=[pltpu.VMEM(shape, jnp.bfloat16), pltpu.SemaphoreType.DMA],
-        compiler_params=pltpu.CompilerParams(vmem_limit_bytes=60 * 2**20),
+        compiler_params=PARAMS,
         cost_estimate=pl.CostEstimate(flops=10**6, bytes_accessed=2**21, transcendentals=0),
         name="cut_out",
     )(whole, piece)

time: 117 us -> 116 us (level)
  the two profiles are of different devices: /device:TPU:65 before, /device:TPU:129 now
where the time goes in v7:
time: 116 us; the launch traced here: 115 us
  waiting for transfers between devices  34.2 us (29%)
  starting transfers between devices  30.7 us (26%)
  Pallas kernels  27.1 us (23%)
  blocking collectives  20.6 us (18%)
  local copies, waits for them, and re-layouts  2.34 us (2%)
    all_to_all x3, waiting for transfers between devices, to_peers(): return lax.all_to_all(block, 'ctx', split_axis=0, concat_axis=0, tiled=True)  32 us
    all_to_all x1, blocking collectives, to_peers(): return lax.all_to_all(block, 'ctx', split_axis=0, concat_axis=0, tiled=True)  20.6 us
    all_to_all x3, starting transfers between devices, to_peers(): return lax.all_to_all(block, 'ctx', split_axis=0, concat_axis=0, tiled=True)  16.3 us
    ppermute x4, starting transfers between devices, up(): lax.ppermute(block, 'grp', [(at, at + 1) for at in range(group_devices -...  12.5 us
    pallas_call x2, Pallas kernels, attend_ahead(): pl.pallas_call(functools.partial(ahead_kernel, query_slab, pair_slab), in...  8.19 us
    pallas_call x1, Pallas kernels, attend_near(): pl.pallas_call(functools.partial(near_kernel, query_slab, own_slab, up_sl...  6.73 us
    pallas_call x1, Pallas kernels, attend_near_merged(): pl.pallas_call(functools.partial(near_merged_kernel, query_slab, own_slab...  3.78 us
    pallas_call x1, Pallas kernels, cut_first(): pl.pallas_call(cut_first_kernel, in_specs=[HBM] * 2, out_specs=[HBM] * 2,...  2.44 us
  transfers between devices with their start and end apart: 8, of which 5 were waited for; matrix products, arithmetic and copies ran while one was open for 0% of the time, Pallas kernels for 22%

profile of v7, /device:TPU:129, one launch (start us, length us, event | category | flops | bytes accessed | tf_op | source)
XLA Modules:
  0.0 115.3 jit_solution(18044439442115621303)
XLA Ops:
  0.0 1.9 %collective-permute-start = (bf16[256,1536]{1,0:T(8,128)(2,1)}, bf16[256,1536]{1,0:T(8,128)(2,1)S(1)}, u32[]{:S(2)}, u32[]{:S(2)}) collective-permute-start(bf16[256,1536]{1,0:T(8,128)(2,1)} %whole_ref.1), channel_id=1, source_target_pairs={{32,0},{64,32},{96,64},{128,96},{160,128},{192,160},{224,192},{256... | collective-permute-start | bytes 2359304 | tf_op jit(solution)/shard_map/ppermute | solution.py:491
  1.9 2.4 %cut_first.1 = (bf16[32,4,32,128]{3,2,1,0:T(8,128)(2,1)}, bf16[32,2,32,128]{3,2,1,0:T(8,128)(2,1)}) custom-call(bf16[256,1536]{1,0:T(8,128)(2,1)} %k_ref.1, bf16[256,1536]{1,0:T(8,128)(2,1)} %v_ref.1), custom_call_target="tpu_custom_call" | custom-call | tf_op jit(solution)/shard_map/cut_first/pallas_call | solution.py:371
  4.4 0.0 copy-start.3
  4.4 0.0 copy-start.4
  4.4 3.5 %collective-permute-start.1 = (bf16[32,2,32,128]{3,2,1,0:T(8,128)(2,1)}, bf16[32,2,32,128]{3,2,1,0:T(8,128)(2,1)S(1)}, u32[]{:S(2)}, u32[]{:S(2)}) collective-permute-start(bf16[32,2,32,128]{3,2,1,0:T(8,128)(2,1)} %get-tuple-element.9.piece_ref), channel_id=1, source_target_pairs={{0,32},{32,64},{64,96},{96,128},{128,160},{160,192},{192,224},{224... | collective-permute-start | bytes 1572872 | tf_op jit(solution)/shard_map/ppermute | solution.py:488
  7.9 8.2 %all-to-all-start = ((bf16[32,4,32,128]{3,2,1,0:T(8,128)(2,1)}), bf16[32,4,32,128]{3,2,1,0:T(8,128)(2,1)}, u32[]{:S(2)}, u32[]{:S(2)}) async-start(bf16[32,4,32,128]{3,2,1,0:T(8,128)(2,1)} %get-tuple-element.10), calls=%async_computation | async-start | bytes 2097152 | tf_op jit(solution)/shard_map/all_to_all | solution.py:485
  16.2 0.0 copy-done.3
  16.2 0.1 copy.8.groups_ref
  16.3 0.0 copy-done.4
  16.3 0.1 copy.9.count_ref
  16.4 2.4 %flags.1.refs_2_.flags_ref = s32[4]{0:T(128)S(1)} custom-call(s32[16,8,2]{2,1,0:T(8,128)S(1)} %copy.8.groups_ref, s32[16,8]{1,0:T(8,128)S(1)} %copy.9.count_ref), custom_call_target="tpu_custom_call" | custom-call | tf_op jit(solution)/shard_map/flags/pallas_call | solution.py:52
  18.7 1.7 %collective-permute-done.1.piece_ref = bf16[32,2,32,128]{3,2,1,0:T(8,128)(2,1)S(1)} collective-permute-done((bf16[32,2,32,128]{3,2,1,0:T(8,128)(2,1)}, bf16[32,2,32,128]{3,2,1,0:T(8,128)(2,1)S(1)}, u32[]{:S(2)}, u32[]{:S(2)}) %collective-permute-start.1) | collective-permute-done | bytes 524320 | tf_op jit(solution)/shard_map/ppermute | solution.py:488
  20.5 0.5 collective-permute-done.whole_ref
  21.0 1.2 %cut.1.refs_0_ = bf16[32,5,32,128]{3,2,1,0:T(8,128)(2,1)} custom-call(bf16[256,1536]{1,0:T(8,128)(2,1)S(1)} %collective-permute-done.whole_ref, bf16[32,2,32,128]{3,2,1,0:T(8,128)(2,1)S(1)} %collective-permute-done.1.piece_ref), custom_call_target="tpu_custom_call" | custom-call | flops 99999997952 | bytes 2097152 | tf_op jit(solution)/shard_map/cut/pallas_call | solution.py:418
  22.3 10.9 %all-to-all-done.refs_1_.own_ref = bf16[32,4,32,128]{3,2,1,0:T(8,128)(2,1)} async-done(((bf16[32,4,32,128]{3,2,1,0:T(8,128)(2,1)}), bf16[32,4,32,128]{3,2,1,0:T(8,128)(2,1)}, u32[]{:S(2)}, u32[]{:S(2)}) %all-to-all-start) | async-done | bytes 1048608 | tf_op jit(solution)/shard_map/all_to_all | solution.py:485
  33.1 0.0 copy-start.1
  33.1 4.1 %all-to-all-start.1 = ((bf16[32,5,32,128]{3,2,1,0:T(8,128)(2,1)}), bf16[32,5,32,128]{3,2,1,0:T(8,128)(2,1)S(1)}, u32[]{:S(2)}, u32[]{:S(2)}) async-start(bf16[32,5,32,128]{3,2,1,0:T(8,128)(2,1)} %gate.2), calls=%async_computation.1 | async-start | bytes 2621440 | tf_op jit(solution)/shard_map/all_to_all | solution.py:485
  37.2 3.5 %collective-permute-start.2 = (bf16[32,4,32,128]{3,2,1,0:T(8,128)(2,1)}, bf16[32,4,32,128]{3,2,1,0:T(8,128)(2,1)}, u32[]{:S(2)}, u32[]{:S(2)}) collective-permute-start(bf16[32,4,32,128]{3,2,1,0:T(8,128)(2,1)} %all-to-all-done.refs_1_.own_ref), channel_id=1, source_target_pairs={{0,32},{32,64},{64,96},{96,128},{128,160},{160,192},{192,224},{224... | collective-permute-start | bytes 3145736 | tf_op jit(solution)/shard_map/ppermute | solution.py:488
  40.8 0.0 copy-done.1
  40.8 0.0 copy-start.2
  40.8 1.0 copy-done.2
  41.8 0.3 cut_out.1.refs_0_
  42.1 14.9 %all-to-all-done.1.refs_1_.q_ref.kv_ref.up_ref = bf16[32,5,32,128]{3,2,1,0:T(8,128)(2,1)S(1)} async-done(((bf16[32,5,32,128]{3,2,1,0:T(8,128)(2,1)}), bf16[32,5,32,128]{3,2,1,0:T(8,128)(2,1)S(1)}, u32[]{:S(2)}, u32[]{:S(2)}) %all-to-all-start.1) | async-done | bytes 1310752 | tf_op jit(solution)/shard_map/all_to_all | solution.py:485
  57.0 0.0 copy-start
  57.0 1.1 copy-done
  58.1 4.0 %all-to-all-start.2 = ((bf16[32,5,32,128]{3,2,1,0:T(8,128)(2,1)}), bf16[32,5,32,128]{3,2,1,0:T(8,128)(2,1)S(1)}, u32[]{:S(2)}, u32[]{:S(2)}) async-start(bf16[32,5,32,128]{3,2,1,0:T(8,128)(2,1)} %copy-done), calls=%async_computation.2 | async-start | bytes 2621440 | tf_op jit(solution)/shard_map/all_to_all | solution.py:485
  62.1 2.9 %ahead.2.rest_0_ = bf16[1,1056,128]{2,1,0:T(8,128)(2,1)} custom-call(s32[4]{0:T(128)S(1)} %flags.1.refs_2_.flags_ref, bf16[32,5,32,128]{3,2,1,0:T(8,128)(2,1)S(1)} %all-to-all-done.1.refs_1_.q_ref.kv_ref.up_ref, bf16[32,5,32,128]{3,2,1,0:T(8,128)(2,1)S(1)} %all-to-all-done.1.refs_1_.q_ref.kv_ref.up_ref), custom_call_target="tpu_custom_call" | custom-call | flops 536870912 | bytes 1048576 | tf_op jit(solution)/shard_map/ahead/pallas_call | solution.py:270
  65.0 3.5 %collective-permute-start.4 = (bf16[1,1056,128]{2,1,0:T(8,128)(2,1)}, bf16[1,1056,128]{2,1,0:T(8,128)(2,1)}, u32[]{:S(2)}, u32[]{:S(2)}) collective-permute-start(bf16[1,1056,128]{2,1,0:T(8,128)(2,1)} %ahead.2.rest_0_), channel_id=1, source_target_pairs={{0,32},{32,64},{64,96},{96,128},{128,160},{160,192},{192,224},{224... | collective-permute-start | bytes 811016 | tf_op jit(solution)/shard_map/ppermute | solution.py:488
  68.5 0.0 collective-permute-done.2.up_ref.kv_ref
  68.5 5.3 %ahead.3 = bf16[2,1056,128]{2,1,0:T(8,128)(2,1)} custom-call(s32[4]{0:T(128)S(1)} %flags.1.refs_2_.flags_ref, bf16[32,5,32,128]{3,2,1,0:T(8,128)(2,1)S(1)} %all-to-all-done.1.refs_1_.q_ref.kv_ref.up_ref, bf16[32,4,32,128]{3,2,1,0:T(8,128)(2,1)} %collective-permute-done.2.up_ref.kv_ref, bf16[1,1056,128]{2,1,0:T(8,128)(2,1)} %ahead.2.rest_0_), custom_call_target="tpu_custom_call" | custom-call | flops 4294967296 | bytes 2097152 | tf_op jit(solution)/shard_map/ahead/pallas_call | solution.py:270
  73.8 1.9 %collective-permute-start.3 = (bf16[2,1056,128]{2,1,0:T(8,128)(2,1)}, bf16[2,1056,128]{2,1,0:T(8,128)(2,1)}, u32[]{:S(2)}, u32[]{:S(2)}) collective-permute-start(bf16[2,1056,128]{2,1,0:T(8,128)(2,1)} %ahead.3), channel_id=1, source_target_pairs={{0,32},{32,64},{64,96},{96,128},{128,160},{160,192},{192,224},{224... | collective-permute-start | bytes 1622024 | tf_op jit(solution)/shard_map/ppermute | solution.py:488
  75.8 6.2 %all-to-all-done.2.q_ref.own_ref = bf16[32,5,32,128]{3,2,1,0:T(8,128)(2,1)S(1)} async-done(((bf16[32,5,32,128]{3,2,1,0:T(8,128)(2,1)}), bf16[32,5,32,128]{3,2,1,0:T(8,128)(2,1)S(1)}, u32[]{:S(2)}, u32[]{:S(2)}) %all-to-all-start.2) | async-done | bytes 1310752 | tf_op jit(solution)/shard_map/all_to_all | solution.py:485
  82.0 6.7 %near.1 = (f32[2,1024,128]{2,1,0:T(8,128)S(1)}, f32[2,8,128]{2,1,0:T(8,128)S(1)}) custom-call(s32[4]{0:T(128)S(1)} %flags.1.refs_2_.flags_ref, bf16[32,5,32,128]{3,2,1,0:T(8,128)(2,1)S(1)} %all-to-all-done.2.q_ref.own_ref, bf16[32,4,32,128]{3,2,1,0:T(8,128)(2,1)} %all-to-all-done.refs_1_.own_ref, bf16[32,4,32,128]{3,2,1,0:T(8,128)(2,1)} %collective-permute-done.2.up_ref.kv_ref), custom_call_target="tpu_custom_call" | custom-call | flops 171798691840 | bytes 3670016 | tf_op jit(solution)/shard_map/near/pallas_call | solution.py:283
  88.7 0.0 collective-permute-done.4.rest_0_
  88.7 3.8 %near_merged.1.rest_0_ = bf16[32,1,32,128]{3,2,1,0:T(8,128)(2,1)S(1)} custom-call(s32[4]{0:T(128)S(1)} %flags.1.refs_2_.flags_ref, bf16[32,5,32,128]{3,2,1,0:T(8,128)(2,1)S(1)} %all-to-all-done.2.q_ref.own_ref, bf16[32,5,32,128]{3,2,1,0:T(8,128)(2,1)S(1)} %all-to-all-done.2.q_ref.own_ref, ...), custom_call_target="tpu_custom_call" | custom-call | flops 858993472 | bytes 1835008 | tf_op jit(solution)/shard_map/near_merged/pallas_call | solution.py:300
  92.5 0.0 collective-permute-done.3.far_ref
  92.5 1.1 merge.1
  93.7 20.6 %all_to_all.20.in_ref = bf16[32,3,32,128]{3,2,1,0:T(8,128)(2,1)S(1)} all-to-all(bf16[32,3,32,128]{3,2,1,0:T(8,128)(2,1)S(1)} %merge.1), channel_id=1, replica_groups=mesh['grp'=16,'ctx'=32] {'ctx'}, dimensions={0} | all-to-all | bytes 1572864 | tf_op jit(solution)/shard_map/all_to_all | solution.py:485
  114.2 1.0 paste.1
  (2 shorter events, 0.0 us)
Async XLA Ops:
  0.0 21.0 %collective-permute-start = (bf16[256,1536]{1,0:T(8,128)(2,1)}, bf16[256,1536]{1,0:T(8,128)(2,1)S(1)}, u32[]{:S(2)}, u32[]{:S(2)}) collective-permute-start(bf16[256,1536]{1,0:T(8,128)(2,1)} %whole_ref.1), channel_id=1, source_target_pairs={{32,0},{64,32},{96,64},{128,96},{160,128},{192,160},{224,192},{256... | collective-permute-start | bytes 2359304 | tf_op jit(solution)/shard_map/ppermute | solution.py:491
  4.4 11.8 %copy-start.3 = (s32[16,8,2]{0,2,1:T(2,128)S(1)}, s32[16,8,2]{0,2,1:T(2,128)}, u32[]{:S(2)}) copy-start(s32[16,8,2]{0,2,1:T(2,128)} %param.8) | copy-start | bytes 3076
  4.4 11.9 %copy-start.4 = (s32[16,8]{0,1:T(8,128)S(1)}, s32[16,8]{0,1:T(8,128)}, u32[]{:S(2)}) copy-start(s32[16,8]{0,1:T(8,128)} %param.9) | copy-start | bytes 1540
  4.4 16.1 %collective-permute-start.1 = (bf16[32,2,32,128]{3,2,1,0:T(8,128)(2,1)}, bf16[32,2,32,128]{3,2,1,0:T(8,128)(2,1)S(1)}, u32[]{:S(2)}, u32[]{:S(2)}) collective-permute-start(bf16[32,2,32,128]{3,2,1,0:T(8,128)(2,1)} %get-tuple-element.9.piece_ref), channel_id=1, source_target_pairs={{0,32},{32,64},{64,96},{96,128},{128,160},{160,192},{192,224},{224... | collective-permute-start | bytes 1572872 | tf_op jit(solution)/shard_map/ppermute | solution.py:488
  7.9 25.2 %all-to-all-start = ((bf16[32,4,32,128]{3,2,1,0:T(8,128)(2,1)}), bf16[32,4,32,128]{3,2,1,0:T(8,128)(2,1)}, u32[]{:S(2)}, u32[]{:S(2)}) async-start(bf16[32,4,32,128]{3,2,1,0:T(8,128)(2,1)} %get-tuple-element.10), calls=%async_computation | async-start | bytes 2097152 | tf_op jit(solution)/shard_map/all_to_all | solution.py:485
  33.1 7.7 %copy-start.1 = (bf16[256,1536]{1,0:T(8,128)(2,1)S(1)}, bf16[256,1536]{1,0:T(8,128)(2,1)}, u32[]{:S(2)}) copy-start(bf16[256,1536]{1,0:T(8,128)(2,1)} %whole_ref.1) | copy-start | bytes 2359300
  33.1 23.9 %all-to-all-start.1 = ((bf16[32,5,32,128]{3,2,1,0:T(8,128)(2,1)}), bf16[32,5,32,128]{3,2,1,0:T(8,128)(2,1)S(1)}, u32[]{:S(2)}, u32[]{:S(2)}) async-start(bf16[32,5,32,128]{3,2,1,0:T(8,128)(2,1)} %gate.2), calls=%async_computation.1 | async-start | bytes 2621440 | tf_op jit(solution)/shard_map/all_to_all | solution.py:485
  37.2 31.3 %collective-permute-start.2 = (bf16[32,4,32,128]{3,2,1,0:T(8,128)(2,1)}, bf16[32,4,32,128]{3,2,1,0:T(8,128)(2,1)}, u32[]{:S(2)}, u32[]{:S(2)}) collective-permute-start(bf16[32,4,32,128]{3,2,1,0:T(8,128)(2,1)} %all-to-all-done.refs_1_.own_ref), channel_id=1, source_target_pairs={{0,32},{32,64},{64,96},{96,128},{128,160},{160,192},{192,224},{224... | collective-permute-start | bytes 3145736 | tf_op jit(solution)/shard_map/ppermute | solution.py:488
  40.8 1.0 copy-start.2
  57.0 1.1 copy-start
  58.1 23.9 %all-to-all-start.2 = ((bf16[32,5,32,128]{3,2,1,0:T(8,128)(2,1)}), bf16[32,5,32,128]{3,2,1,0:T(8,128)(2,1)S(1)}, u32[]{:S(2)}, u32[]{:S(2)}) async-start(bf16[32,5,32,128]{3,2,1,0:T(8,128)(2,1)} %copy-done), calls=%async_computation.2 | async-start | bytes 2621440 | tf_op jit(solution)/shard_map/all_to_all | solution.py:485
  65.0 23.7 %collective-permute-start.4 = (bf16[1,1056,128]{2,1,0:T(8,128)(2,1)}, bf16[1,1056,128]{2,1,0:T(8,128)(2,1)}, u32[]{:S(2)}, u32[]{:S(2)}) collective-permute-start(bf16[1,1056,128]{2,1,0:T(8,128)(2,1)} %ahead.2.rest_0_), channel_id=1, source_target_pairs={{0,32},{32,64},{64,96},{96,128},{128,160},{160,192},{192,224},{224... | collective-permute-start | bytes 811016 | tf_op jit(solution)/shard_map/ppermute | solution.py:488
  73.8 18.7 %collective-permute-start.3 = (bf16[2,1056,128]{2,1,0:T(8,128)(2,1)}, bf16[2,1056,128]{2,1,0:T(8,128)(2,1)}, u32[]{:S(2)}, u32[]{:S(2)}) collective-permute-start(bf16[2,1056,128]{2,1,0:T(8,128)(2,1)} %ahead.3), channel_id=1, source_target_pairs={{0,32},{32,64},{64,96},{96,128},{128,160},{160,192},{192,224},{224... | collective-permute-start | bytes 1622024 | tf_op jit(solution)/shard_map/ppermute | solution.py:488

commit v8 on v7

--- a/solution.py
+++ b/solution.py
@@ -158,62 +158,71 @@
         out_ref[:, pl.ds(rows, STAT_ROWS), :] = jnp.zeros((heads, STAT_ROWS, HD), jnp.bfloat16)
 
 
-def near_kernel(query_slab, own_slab, up_slab, flags_ref, q_ref, own_ref, up_ref, out_ref, log_ref):
-    rows = q_ref.shape[0] * POSITIONS
-    heads = out_ref.shape[0]
+def near_kernel(flags_ref, third_ref, second_ref, first_hbm, up_hbm, far_ref, *rest):
+    out_ref, log_ref, last_ref, first_ref, up_ref, last_near, last_log, sems = rest
+    frames = third_ref.shape[0]
+    rows = frames * POSITIONS
     taken = flags_ref[0] > 0
-
-    def run(with_earlier):
-        @pl.loop(0, heads)
-        def _(head):
-            def own(start):
-                def begin():
-                    query = rows_of(q_ref, query_slab + head, start, QB)
-                    return score(query, rows_of(own_ref, own_slab + 2 * head, 0, start + QB))
-
-                def finish(scores):
-                    return soften(scores, rows_of(own_ref, own_slab + 2 * head + 1, 0, start + QB), True)
-
-                return begin, finish
-
-            def earlier(start):
-                def begin():
-                    query = rows_of(q_ref, query_slab + head, start, QB)
-                    return score(query, rows_of(up_ref, up_slab + 2 * head, 0, rows))
-
-                def finish(scores):
-                    return soften(scores, rows_of(up_ref, up_slab + 2 * head + 1, 0, rows))
-
-                return begin, finish
-
-            logs = []
-            held = []
-
-            def done(at, part):
-                if with_earlier:
-                    held.append(part)
-                    if at % 2 == 0:
-                        return
-                    part = join(held[-2], held[-1])
-                    at = at // 2
-                out_ref[head, pl.ds(at * QB, QB), :] = part[2] / part[1]
-                logs.extend(log_rows(part))
-
-            jobs = []
-            for start in range(0, rows, QB):
-                jobs.append(own(start))
-                if with_earlier:
-                    jobs.append(earlier(start))
-            in_turn(jobs, done)
-            log_ref[head] = jnp.concatenate(logs, axis=0)
-
-    @pl.when(taken)
-    def _():
-        run(True)
-
-    @pl.when(jnp.logical_not(taken))
-    def _():
-        run(False)
+    half = frames // 2
+    copies = [
+        pltpu.make_async_copy(
+            source.at[pl.ds(at * half, half)], held.at[pl.ds(at * half, half)], sems.at[which, at]
+        )
+        for which, (source, held) in enumerate(((first_hbm, first_ref), (up_hbm, up_ref)))
+        for at in range(2)
+    ]
+    for copy in copies:
+        copy.start()
+
+    def run(with_earlier, query_slab, own, up, near_ref, logs_ref, head):
+        def job(pair, slab, start, count, diagonal):
+            def begin():
+                query = rows_of(third_ref, query_slab, start, QB)
+                return score(query, rows_of(pair, slab, 0, count))
+
+            def finish(scores):
+                return soften(scores, rows_of(pair, slab + 1, 0, count), diagonal)
+
+            return begin, finish
+
+        logs = []
+        held = []
+
+        def done(at, part):
+            if with_earlier:
+                held.append(part)
+                if at % 2 == 0:
+                    return
+                part = join(held[-2], held[-1])
+                at = at // 2
+            near_ref[head, pl.ds(at * QB, QB), :] = part[2] / part[1]
+            logs.extend(log_rows(part))
+
+        jobs = []
+        for start in range(0, rows, QB):
+            jobs.append(job(own[0], own[1], start, start + QB, True))
+            if with_earlier:
+                jobs.append(job(up[0], up[1], start, rows, False))
+        in_turn(jobs, done)
+        logs_ref[head] = jnp.concatenate(logs, axis=0)
+
+    def run_as_taken(*where):
+        @pl.when(taken)
+        def _():
+            run(True, *where)
+
+        @pl.when(jnp.logical_not(taken))
+        def _():
+            run(False, *where)
+
+    run_as_taken(PARTS - 1, (third_ref, PARTS), (second_ref, PARTS), last_near, last_log, 0)
+    merge_kernel(flags_ref, last_near, last_log, far_ref, last_ref)
+    for copy in copies:
+        copy.wait()
+
+    @pl.loop(0, PARTS - 1)
+    def _(head):
+        run_as_taken(head, (first_ref, 2 * head), (up_ref, 2 * head), out_ref, log_ref, head)
 
 
 def merge_kernel(flags_ref, near_ref, log_ref, far_ref, *rest):
@@ -249,14 +258,6 @@
                 put(head, block, near_ref[head, pl.ds(block * HD, HD), :])
 
 
-def near_merged_kernel(query_slab, own_slab, up_slab, flags_ref, q_ref, own_ref, up_ref, *rest):
-    far_ref, out_ref, near_ref, log_ref = rest
-    near_kernel(
-        query_slab, own_slab, up_slab, flags_ref, q_ref, own_ref, up_ref, near_ref, log_ref
-    )
-    merge_kernel(flags_ref, near_ref, log_ref, far_ref, out_ref)
-
-
 def cost(passes, rows, heads, moved):
     return pl.CostEstimate(
         flops=int(4 * passes * rows * rows * heads * HD),
@@ -278,38 +279,29 @@
     )(flags, query, pair, *waited)
 
 
-def attend_near(flags, heads, query, query_slab, own, own_slab, up, up_slab):
-    rows = query.shape[0] * POSITIONS
-    return pl.pallas_call(
-        functools.partial(near_kernel, query_slab, own_slab, up_slab),
-        in_specs=[SMEM] + [VMEM] * 3,
-        out_specs=[VMEM] * 2,
+def attend_near(flags, third, second, first, first_up, far):
+    frames, heads = third.shape[0], PARTS - 1
+    rows = frames * POSITIONS
+    return pl.pallas_call(
+        near_kernel,
+        in_specs=[SMEM] + [VMEM] * 2 + [ANY] * 2 + [VMEM],
+        out_specs=[VMEM] * 3,
         out_shape=[
             jax.ShapeDtypeStruct((heads, rows, HD), jnp.float32),
             jax.ShapeDtypeStruct((heads, rows // HD, HD), jnp.float32),
+            jax.ShapeDtypeStruct((frames, 1, POSITIONS, HD), jnp.bfloat16),
         ],
-        compiler_params=PARAMS,
+        scratch_shapes=[
+            pltpu.VMEM(first.shape, first.dtype),
+            pltpu.VMEM(first_up.shape, first_up.dtype),
+            pltpu.VMEM((1, rows, HD), jnp.float32),
+            pltpu.VMEM((1, rows // HD, HD), jnp.float32),
+            pltpu.SemaphoreType.DMA((2, 2)),
+        ],
+        compiler_params=pltpu.CompilerParams(vmem_limit_bytes=14 * 2**20),
         cost_estimate=cost(160, rows, heads, rows * heads * HD * 14),
         name="near",
-    )(flags, query, own, up)
-
-
-def attend_near_merged(flags, query, query_slab, own, own_slab, up, up_slab, far):
-    frames = query.shape[0]
-    rows = frames * POSITIONS
-    return pl.pallas_call(
-        functools.partial(near_merged_kernel, query_slab, own_slab, up_slab),
-        in_specs=[SMEM] + [VMEM] * 4,
-        out_specs=VMEM,
-        out_shape=jax.ShapeDtypeStruct((frames, 1, POSITIONS, HD), jnp.bfloat16),
-        scratch_shapes=[
-            pltpu.VMEM((1, rows, HD), jnp.float32),
-            pltpu.VMEM((1, rows // HD, HD), jnp.float32),
-        ],
-        compiler_params=PARAMS,
-        cost_estimate=cost(1.6, rows, 1, rows * HD * 14),
-        name="near_merged",
-    )(flags, query, own, up, far)
+    )(flags, third, second, first, first_up, far)
 
 
 def merge(flags, near, logs, far, *others):
@@ -501,8 +493,7 @@
     ahead_b = attend_ahead(flags, 1, 1, second, 2, second, 3)
     far_b = up(ahead_b)
     far_a = up(attend_ahead(flags, 2, 4, second, 0, first_up, 0, ahead_b))
-    merged = attend_near_merged(flags, third, 2, third, 3, second, 3, far_b)
-    near, logs = attend_near(flags, 2, third, 0, first, 0, first_up, 0)
+    near, logs, merged = attend_near(flags, third, second, first, first_up, far_b)
     return paste(to_peers(merge(flags, near, logs, far_a, merged)))
 
 

time: 116 us -> 115 us (level)
  the two profiles are of different devices: /device:TPU:129 before, /device:TPU:225 now
where the time goes in v8:
time: 115 us; the launch traced here: 114 us
  starting transfers between devices  37.4 us (33%)
  waiting for transfers between devices  34 us (30%)
  blocking collectives  23.8 us (21%)
  Pallas kernels  17.4 us (15%)
  local copies, waits for them, and re-layouts  1.26 us (1%)
    all_to_all x3, waiting for transfers between devices, to_peers(): return lax.all_to_all(block, 'ctx', split_axis=0, concat_axis=0, tiled=True)  31.7 us
    all_to_all x1, blocking collectives, to_peers(): return lax.all_to_all(block, 'ctx', split_axis=0, concat_axis=0, tiled=True)  23.8 us
    ppermute x4, starting transfers between devices, up(): lax.ppermute(block, 'grp', [(at, at + 1) for at in range(group_devices -...  18.6 us
    all_to_all x3, starting transfers between devices, to_peers(): return lax.all_to_all(block, 'ctx', split_axis=0, concat_axis=0, tiled=True)  16.9 us
    pallas_call x1, Pallas kernels, attend_near(): pl.pallas_call(near_kernel, in_specs=[SMEM] + [VMEM] * 2 + [ANY] * 2 + [V...  5.39 us
    pallas_call x2, Pallas kernels, attend_ahead(): pl.pallas_call(functools.partial(ahead_kernel, query_slab, pair_slab), in...  2.6 us
    pallas_call x1, Pallas kernels, cut_first(): pl.pallas_call(cut_first_kernel, in_specs=[HBM] * 2, out_specs=[HBM] * 2,...  2.44 us
    pallas_call x1, Pallas kernels, make_flags(): pl.pallas_call(flags_kernel, in_specs=[SMEM] * 2, out_specs=SMEM, out_sha...  2.37 us
  transfers between devices with their start and end apart: 8, of which 4 were waited for; matrix products, arithmetic and copies ran while one was open for 0% of the time, Pallas kernels for 13%

profile of v8, /device:TPU:225, one launch (start us, length us, event | category | flops | bytes accessed | tf_op | source)
XLA Modules:
  0.0 114.1 jit_solution(992961358692448754)
XLA Ops:
  0.0 1.9 %collective-permute-start = (bf16[256,1536]{1,0:T(8,128)(2,1)}, bf16[256,1536]{1,0:T(8,128)(2,1)S(1)}, u32[]{:S(2)}, u32[]{:S(2)}) collective-permute-start(bf16[256,1536]{1,0:T(8,128)(2,1)} %whole_ref.1), channel_id=1, source_target_pairs={{32,0},{64,32},{96,64},{128,96},{160,128},{192,160},{224,192},{256... | collective-permute-start | bytes 2359304 | tf_op jit(solution)/shard_map/ppermute | solution.py:483
  1.9 2.4 %cut_first.1 = (bf16[32,4,32,128]{3,2,1,0:T(8,128)(2,1)}, bf16[32,2,32,128]{3,2,1,0:T(8,128)(2,1)}) custom-call(bf16[256,1536]{1,0:T(8,128)(2,1)} %k_ref.1, bf16[256,1536]{1,0:T(8,128)(2,1)} %v_ref.1), custom_call_target="tpu_custom_call" | custom-call | tf_op jit(solution)/shard_map/cut_first/pallas_call | solution.py:363
  4.4 0.0 copy-start.2
  4.4 0.0 copy-start.3
  4.4 4.8 %collective-permute-start.1 = (bf16[32,2,32,128]{3,2,1,0:T(8,128)(2,1)}, bf16[32,2,32,128]{3,2,1,0:T(8,128)(2,1)S(1)}, u32[]{:S(2)}, u32[]{:S(2)}) collective-permute-start(bf16[32,2,32,128]{3,2,1,0:T(8,128)(2,1)} %get-tuple-element.10.piece_ref), channel_id=1, source_target_pairs={{0,32},{32,64},{64,96},{96,128},{128,160},{160,192},{192,224},{224... | collective-permute-start | bytes 1572872 | tf_op jit(solution)/shard_map/ppermute | solution.py:480
  9.2 8.1 %all-to-all-start = ((bf16[32,4,32,128]{3,2,1,0:T(8,128)(2,1)}), bf16[32,4,32,128]{3,2,1,0:T(8,128)(2,1)S(1)}, u32[]{:S(2)}, u32[]{:S(2)}) async-start(bf16[32,4,32,128]{3,2,1,0:T(8,128)(2,1)} %get-tuple-element.11), calls=%async_computation | async-start | bytes 2097152 | tf_op jit(solution)/shard_map/all_to_all | solution.py:477
  17.3 0.0 copy-done.2
  17.3 0.1 copy.8.groups_ref
  17.4 0.0 copy-done.3
  17.5 0.1 copy.9.count_ref
  17.5 2.4 %flags.1.refs_2_.flags_ref = s32[4]{0:T(128)S(1)} custom-call(s32[16,8,2]{2,1,0:T(8,128)S(1)} %copy.8.groups_ref, s32[16,8]{1,0:T(8,128)S(1)} %copy.9.count_ref), custom_call_target="tpu_custom_call" | custom-call | tf_op jit(solution)/shard_map/flags/pallas_call | solution.py:52
  19.9 0.0 collective-permute-done.1.piece_ref
  19.9 2.2 %collective-permute-done.whole_ref = bf16[256,1536]{1,0:T(8,128)(2,1)S(1)} collective-permute-done((bf16[256,1536]{1,0:T(8,128)(2,1)}, bf16[256,1536]{1,0:T(8,128)(2,1)S(1)}, u32[]{:S(2)}, u32[]{:S(2)}) %collective-permute-start) | collective-permute-done | bytes 786464 | tf_op jit(solution)/shard_map/ppermute | solution.py:483
  22.1 1.2 %cut.1.refs_0_ = bf16[32,5,32,128]{3,2,1,0:T(8,128)(2,1)} custom-call(bf16[256,1536]{1,0:T(8,128)(2,1)S(1)} %collective-permute-done.whole_ref, bf16[32,2,32,128]{3,2,1,0:T(8,128)(2,1)S(1)} %collective-permute-done.1.piece_ref), custom_call_target="tpu_custom_call" | custom-call | flops 99999997952 | bytes 2097152 | tf_op jit(solution)/shard_map/cut/pallas_call | solution.py:410
  23.3 10.9 %all-to-all-done.refs_1_.first_hbm = bf16[32,4,32,128]{3,2,1,0:T(8,128)(2,1)S(1)} async-done(((bf16[32,4,32,128]{3,2,1,0:T(8,128)(2,1)}), bf16[32,4,32,128]{3,2,1,0:T(8,128)(2,1)S(1)}, u32[]{:S(2)}, u32[]{:S(2)}) %all-to-all-start) | async-done | bytes 1048608 | tf_op jit(solution)/shard_map/all_to_all | solution.py:477
  34.2 0.0 copy-start
  34.2 4.1 %all-to-all-start.1 = ((bf16[32,5,32,128]{3,2,1,0:T(8,128)(2,1)}), bf16[32,5,32,128]{3,2,1,0:T(8,128)(2,1)S(1)}, u32[]{:S(2)}, u32[]{:S(2)}) async-start(bf16[32,5,32,128]{3,2,1,0:T(8,128)(2,1)} %gate.2), calls=%async_computation.1 | async-start | bytes 2621440 | tf_op jit(solution)/shard_map/all_to_all | solution.py:477
  38.3 3.5 %collective-permute-start.2 = (bf16[32,4,32,128]{3,2,1,0:T(8,128)(2,1)S(1)}, bf16[32,4,32,128]{3,2,1,0:T(8,128)(2,1)}, u32[]{:S(2)}, u32[]{:S(2)}) collective-permute-start(bf16[32,4,32,128]{3,2,1,0:T(8,128)(2,1)S(1)} %all-to-all-done.refs_1_.first_hbm), channel_id=1, source_target_pairs={{0,32},{32,64},{64,96},{96,128},{128,160},{160,192},{192,224},{224... | collective-permute-start | bytes 3145736 | tf_op jit(solution)/shard_map/ppermute | solution.py:480
  41.9 0.0 copy-done
  41.9 0.0 copy-start.1
  41.9 1.0 copy-done.1
  42.9 1.3 %cut_out.1.refs_0_ = bf16[32,5,32,128]{3,2,1,0:T(8,128)(2,1)} custom-call(bf16[256,1536]{1,0:T(8,128)(2,1)S(1)} %copy-done, bf16[32,2,32,128]{3,2,1,0:T(8,128)(2,1)S(1)} %copy-done.1), custom_call_target="tpu_custom_call" | custom-call | flops 1000000 | bytes 2097152 | tf_op jit(solution)/shard_map/cut_out/pallas_call | solution.py:430
  44.2 13.9 %all-to-all-done.1.refs_1_.q_ref.kv_ref.second_ref = bf16[32,5,32,128]{3,2,1,0:T(8,128)(2,1)S(1)} async-done(((bf16[32,5,32,128]{3,2,1,0:T(8,128)(2,1)}), bf16[32,5,32,128]{3,2,1,0:T(8,128)(2,1)S(1)}, u32[]{:S(2)}, u32[]{:S(2)}) %all-to-all-start.1) | async-done | bytes 1310752 | tf_op jit(solution)/shard_map/all_to_all | solution.py:477
  58.1 4.7 %all-to-all-start.2 = ((bf16[32,5,32,128]{3,2,1,0:T(8,128)(2,1)}), bf16[32,5,32,128]{3,2,1,0:T(8,128)(2,1)}, u32[]{:S(2)}, u32[]{:S(2)}) async-start(bf16[32,5,32,128]{3,2,1,0:T(8,128)(2,1)} %gate.3), calls=%async_computation.2 | async-start | bytes 2621440 | tf_op jit(solution)/shard_map/all_to_all | solution.py:477
  62.8 0.6 ahead.2.rest_0_
  63.3 5.2 %collective-permute-start.3 = (bf16[1,1056,128]{2,1,0:T(8,128)(2,1)S(1)}, bf16[1,1056,128]{2,1,0:T(8,128)(2,1)S(1)}, u32[]{:S(2)}, u32[]{:S(2)}) collective-permute-start(bf16[1,1056,128]{2,1,0:T(8,128)(2,1)S(1)} %ahead.2.rest_0_), channel_id=1, source_target_pairs={{0,32},{32,64},{64,96},{96,128},{128,160},{160,192},{192,224},{224... | collective-permute-start | bytes 811016 | tf_op jit(solution)/shard_map/ppermute | solution.py:480
  68.5 0.0 collective-permute-done.2.up_hbm.kv_ref
  68.5 2.0 %ahead.3 = bf16[2,1056,128]{2,1,0:T(8,128)(2,1)} custom-call(s32[4]{0:T(128)S(1)} %flags.1.refs_2_.flags_ref, bf16[32,5,32,128]{3,2,1,0:T(8,128)(2,1)S(1)} %all-to-all-done.1.refs_1_.q_ref.kv_ref.second_ref, bf16[32,4,32,128]{3,2,1,0:T(8,128)(2,1)} %collective-permute-done.2.up_hbm.kv_ref, bf16[1,1056,128]{2,1,0:T(8,128)(2,1)S(1)} %ahead.2.rest_0_), custom_call_target="tpu_custom_call" | custom-call | flops 4294967296 | bytes 2097152 | tf_op jit(solution)/shard_map/ahead/pallas_call | solution.py:271
  70.6 5.2 %collective-permute-start.4 = (bf16[2,1056,128]{2,1,0:T(8,128)(2,1)}, bf16[2,1056,128]{2,1,0:T(8,128)(2,1)}, u32[]{:S(2)}, u32[]{:S(2)}) collective-permute-start(bf16[2,1056,128]{2,1,0:T(8,128)(2,1)} %ahead.3), channel_id=1, source_target_pairs={{0,32},{32,64},{64,96},{96,128},{128,160},{160,192},{192,224},{224... | collective-permute-start | bytes 1622024 | tf_op jit(solution)/shard_map/ppermute | solution.py:480
  75.7 0.0 collective-permute-done.3.far_ref
  75.8 7.0 %all-to-all-done.2.third_ref = bf16[32,5,32,128]{3,2,1,0:T(8,128)(2,1)} async-done(((bf16[32,5,32,128]{3,2,1,0:T(8,128)(2,1)}), bf16[32,5,32,128]{3,2,1,0:T(8,128)(2,1)}, u32[]{:S(2)}, u32[]{:S(2)}) %all-to-all-start.2) | async-done | bytes 1310752 | tf_op jit(solution)/shard_map/all_to_all | solution.py:477
  82.7 5.4 %near.1 = (f32[2,1024,128]{2,1,0:T(8,128)S(1)}, f32[2,8,128]{2,1,0:T(8,128)S(1)}, bf16[32,1,32,128]{3,2,1,0:T(8,128)(2,1)S(1)}) custom-call(s32[4]{0:T(128)S(1)} %flags.1.refs_2_.flags_ref, bf16[32,5,32,128]{3,2,1,0:T(8,128)(2,1)} %all-to-all-done.2.third_ref, bf16[32,5,32,128]{3,2,1,0:T(8,128)(2,1)S(1)} %all-to-all-done.1.refs_1_.q_ref.kv_ref.second_ref, ...), custom_call_target="tpu_custom_call" | custom-call | flops 171798691840 | bytes 3670016 | tf_op jit(solution)/shard_map/near/pallas_call | solution.py:285
  88.1 0.0 collective-permute-done.4.far_ref
  88.1 1.1 merge.1
  89.3 23.8 %all_to_all.20.in_ref = bf16[32,3,32,128]{3,2,1,0:T(8,128)(2,1)S(1)} all-to-all(bf16[32,3,32,128]{3,2,1,0:T(8,128)(2,1)S(1)} %merge.1), channel_id=1, replica_groups=mesh['grp'=16,'ctx'=32] {'ctx'}, dimensions={0} | all-to-all | bytes 1572864 | tf_op jit(solution)/shard_map/all_to_all | solution.py:477
  113.0 1.0 paste.1
  (2 shorter events, 0.0 us)
Async XLA Ops:
  0.0 22.1 %collective-permute-start = (bf16[256,1536]{1,0:T(8,128)(2,1)}, bf16[256,1536]{1,0:T(8,128)(2,1)S(1)}, u32[]{:S(2)}, u32[]{:S(2)}) collective-permute-start(bf16[256,1536]{1,0:T(8,128)(2,1)} %whole_ref.1), channel_id=1, source_target_pairs={{32,0},{64,32},{96,64},{128,96},{160,128},{192,160},{224,192},{256... | collective-permute-start | bytes 2359304 | tf_op jit(solution)/shard_map/ppermute | solution.py:483
  4.4 12.9 %copy-start.2 = (s32[16,8,2]{0,2,1:T(2,128)S(1)}, s32[16,8,2]{0,2,1:T(2,128)}, u32[]{:S(2)}) copy-start(s32[16,8,2]{0,2,1:T(2,128)} %param.8) | copy-start | bytes 3076
  4.4 13.1 %copy-start.3 = (s32[16,8]{0,1:T(8,128)S(1)}, s32[16,8]{0,1:T(8,128)}, u32[]{:S(2)}) copy-start(s32[16,8]{0,1:T(8,128)} %param.9) | copy-start | bytes 1540
  4.4 15.5 %collective-permute-start.1 = (bf16[32,2,32,128]{3,2,1,0:T(8,128)(2,1)}, bf16[32,2,32,128]{3,2,1,0:T(8,128)(2,1)S(1)}, u32[]{:S(2)}, u32[]{:S(2)}) collective-permute-start(bf16[32,2,32,128]{3,2,1,0:T(8,128)(2,1)} %get-tuple-element.10.piece_ref), channel_id=1, source_target_pairs={{0,32},{32,64},{64,96},{96,128},{128,160},{160,192},{192,224},{224... | collective-permute-start | bytes 1572872 | tf_op jit(solution)/shard_map/ppermute | solution.py:480
  9.2 25.1 %all-to-all-start = ((bf16[32,4,32,128]{3,2,1,0:T(8,128)(2,1)}), bf16[32,4,32,128]{3,2,1,0:T(8,128)(2,1)S(1)}, u32[]{:S(2)}, u32[]{:S(2)}) async-start(bf16[32,4,32,128]{3,2,1,0:T(8,128)(2,1)} %get-tuple-element.11), calls=%async_computation | async-start | bytes 2097152 | tf_op jit(solution)/shard_map/all_to_all | solution.py:477
  34.2 7.7 %copy-start = (bf16[256,1536]{1,0:T(8,128)(2,1)S(1)}, bf16[256,1536]{1,0:T(8,128)(2,1)}, u32[]{:S(2)}) copy-start(bf16[256,1536]{1,0:T(8,128)(2,1)} %whole_ref.1) | copy-start | bytes 2359300
  34.2 23.9 %all-to-all-start.1 = ((bf16[32,5,32,128]{3,2,1,0:T(8,128)(2,1)}), bf16[32,5,32,128]{3,2,1,0:T(8,128)(2,1)S(1)}, u32[]{:S(2)}, u32[]{:S(2)}) async-start(bf16[32,5,32,128]{3,2,1,0:T(8,128)(2,1)} %gate.2), calls=%async_computation.1 | async-start | bytes 2621440 | tf_op jit(solution)/shard_map/all_to_all | solution.py:477
  38.3 30.2 %collective-permute-start.2 = (bf16[32,4,32,128]{3,2,1,0:T(8,128)(2,1)S(1)}, bf16[32,4,32,128]{3,2,1,0:T(8,128)(2,1)}, u32[]{:S(2)}, u32[]{:S(2)}) collective-permute-start(bf16[32,4,32,128]{3,2,1,0:T(8,128)(2,1)S(1)} %all-to-all-done.refs_1_.first_hbm), channel_id=1, source_target_pairs={{0,32},{32,64},{64,96},{96,128},{128,160},{160,192},{192,224},{224... | collective-permute-start | bytes 3145736 | tf_op jit(solution)/shard_map/ppermute | solution.py:480
  41.9 1.0 copy-start.1
  58.1 24.6 %all-to-all-start.2 = ((bf16[32,5,32,128]{3,2,1,0:T(8,128)(2,1)}), bf16[32,5,32,128]{3,2,1,0:T(8,128)(2,1)}, u32[]{:S(2)}, u32[]{:S(2)}) async-start(bf16[32,5,32,128]{3,2,1,0:T(8,128)(2,1)} %gate.3), calls=%async_computation.2 | async-start | bytes 2621440 | tf_op jit(solution)/shard_map/all_to_all | solution.py:477
  63.3 12.4 %collective-permute-start.3 = (bf16[1,1056,128]{2,1,0:T(8,128)(2,1)S(1)}, bf16[1,1056,128]{2,1,0:T(8,128)(2,1)S(1)}, u32[]{:S(2)}, u32[]{:S(2)}) collective-permute-start(bf16[1,1056,128]{2,1,0:T(8,128)(2,1)S(1)} %ahead.2.rest_0_), channel_id=1, source_target_pairs={{0,32},{32,64},{64,96},{96,128},{128,160},{160,192},{192,224},{224... | collective-permute-start | bytes 811016 | tf_op jit(solution)/shard_map/ppermute | solution.py:480
  70.6 17.5 %collective-permute-start.4 = (bf16[2,1056,128]{2,1,0:T(8,128)(2,1)}, bf16[2,1056,128]{2,1,0:T(8,128)(2,1)}, u32[]{:S(2)}, u32[]{:S(2)}) collective-permute-start(bf16[2,1056,128]{2,1,0:T(8,128)(2,1)} %ahead.3), channel_id=1, source_target_pairs={{0,32},{32,64},{64,96},{96,128},{128,160},{160,192},{192,224},{224... | collective-permute-start | bytes 1622024 | tf_op jit(solution)/shard_map/ppermute | solution.py:480

commit v9 on v8

--- a/solution.py
+++ b/solution.py
@@ -14,7 +14,7 @@
 SPAN = 4
 NWIN = 8
 LOOK = 2
-QB = 256
+QB = 512
 PARTS = HEADS // SPAN
 POSITIONS = POS // NWIN
 STAT_ROWS = 32
@@ -26,7 +26,7 @@
 ANY = pl.BlockSpec(memory_space=pl.ANY)
 HBM = pl.BlockSpec(memory_space=pltpu.HBM)
 SMALL = pltpu.CompilerParams(vmem_limit_bytes=2**20)
-PARAMS = pltpu.CompilerParams(vmem_limit_bytes=10 * 2**20)
+PARAMS = pltpu.CompilerParams(vmem_limit_bytes=16 * 2**20)
 
 
 def is_taken(groups_ref, count_ref, group, distance):
@@ -298,7 +298,7 @@
             pltpu.VMEM((1, rows // HD, HD), jnp.float32),
             pltpu.SemaphoreType.DMA((2, 2)),
         ],
-        compiler_params=pltpu.CompilerParams(vmem_limit_bytes=14 * 2**20),
+        compiler_params=pltpu.CompilerParams(vmem_limit_bytes=20 * 2**20),
         cost_estimate=cost(160, rows, heads, rows * heads * HD * 14),
         name="near",
     )(flags, third, second, first, first_up, far)

time: 115 us -> 115 us (level)
  the two profiles are of different devices: /device:TPU:225 before, /device:TPU:65 now
where the time goes in v9:
time: 115 us; the launch traced here: 114 us
  starting transfers between devices  35.4 us (31%)
  waiting for transfers between devices  31.3 us (27%)
  Pallas kernels  23.5 us (20%)
  blocking collectives  22.5 us (20%)
  local copies, waits for them, and re-layouts  1.26 us (1%)
    all_to_all x3, waiting for transfers between devices, to_peers(): return lax.all_to_all(block, 'ctx', split_axis=0, concat_axis=0, tiled=True)  27.8 us
    all_to_all x1, blocking collectives, to_peers(): return lax.all_to_all(block, 'ctx', split_axis=0, concat_axis=0, tiled=True)  22.5 us
    all_to_all x3, starting transfers between devices, to_peers(): return lax.all_to_all(block, 'ctx', split_axis=0, concat_axis=0, tiled=True)  16.9 us
    ppermute x4, starting transfers between devices, up(): lax.ppermute(block, 'grp', [(at, at + 1) for at in range(group_devices -...  16.6 us
    pallas_call x2, Pallas kernels, attend_ahead(): pl.pallas_call(functools.partial(ahead_kernel, query_slab, pair_slab), in...  7.38 us
    pallas_call x1, Pallas kernels, attend_near(): pl.pallas_call(near_kernel, in_specs=[SMEM] + [VMEM] * 2 + [ANY] * 2 + [V...  6.29 us
    pallas_call x1, Pallas kernels, cut_first(): pl.pallas_call(cut_first_kernel, in_specs=[HBM] * 2, out_specs=[HBM] * 2,...  2.44 us
    pallas_call x1, Pallas kernels, make_flags(): pl.pallas_call(flags_kernel, in_specs=[SMEM] * 2, out_specs=SMEM, out_sha...  2.37 us
  transfers between devices with their start and end apart: 8, of which 5 were waited for; matrix products, arithmetic and copies ran while one was open for 0% of the time, Pallas kernels for 18%

profile of v9, /device:TPU:65, one launch (start us, length us, event | category | flops | bytes accessed | tf_op | source)
XLA Modules:
  0.0 114.2 jit_solution(18435363963599988043)
XLA Ops:
  0.0 1.9 %collective-permute-start = (bf16[256,1536]{1,0:T(8,128)(2,1)}, bf16[256,1536]{1,0:T(8,128)(2,1)S(1)}, u32[]{:S(2)}, u32[]{:S(2)}) collective-permute-start(bf16[256,1536]{1,0:T(8,128)(2,1)} %whole_ref.1), channel_id=1, source_target_pairs={{32,0},{64,32},{96,64},{128,96},{160,128},{192,160},{224,192},{256... | collective-permute-start | bytes 2359304 | tf_op jit(solution)/shard_map/ppermute | solution.py:483
  1.9 2.4 %cut_first.1 = (bf16[32,4,32,128]{3,2,1,0:T(8,128)(2,1)}, bf16[32,2,32,128]{3,2,1,0:T(8,128)(2,1)}) custom-call(bf16[256,1536]{1,0:T(8,128)(2,1)} %k_ref.1, bf16[256,1536]{1,0:T(8,128)(2,1)} %v_ref.1), custom_call_target="tpu_custom_call" | custom-call | tf_op jit(solution)/shard_map/cut_first/pallas_call | solution.py:363
  4.4 0.0 copy-start.2
  4.4 0.0 copy-start.3
  4.4 3.5 %collective-permute-start.1 = (bf16[32,2,32,128]{3,2,1,0:T(8,128)(2,1)}, bf16[32,2,32,128]{3,2,1,0:T(8,128)(2,1)S(1)}, u32[]{:S(2)}, u32[]{:S(2)}) collective-permute-start(bf16[32,2,32,128]{3,2,1,0:T(8,128)(2,1)} %get-tuple-element.10.piece_ref), channel_id=1, source_target_pairs={{0,32},{32,64},{64,96},{96,128},{128,160},{160,192},{192,224},{224... | collective-permute-start | bytes 1572872 | tf_op jit(solution)/shard_map/ppermute | solution.py:480
  7.9 8.1 %all-to-all-start = ((bf16[32,4,32,128]{3,2,1,0:T(8,128)(2,1)}), bf16[32,4,32,128]{3,2,1,0:T(8,128)(2,1)S(1)}, u32[]{:S(2)}, u32[]{:S(2)}) async-start(bf16[32,4,32,128]{3,2,1,0:T(8,128)(2,1)} %get-tuple-element.11), calls=%async_computation | async-start | bytes 2097152 | tf_op jit(solution)/shard_map/all_to_all | solution.py:477
  16.1 0.0 copy-done.2
  16.1 0.1 copy.8.groups_ref
  16.2 0.0 copy-done.3
  16.2 0.1 copy.9.count_ref
  16.3 2.4 %flags.1.refs_2_.flags_ref = s32[4]{0:T(128)S(1)} custom-call(s32[16,8,2]{2,1,0:T(8,128)S(1)} %copy.8.groups_ref, s32[16,8]{1,0:T(8,128)S(1)} %copy.9.count_ref), custom_call_target="tpu_custom_call" | custom-call | tf_op jit(solution)/shard_map/flags/pallas_call | solution.py:52
  18.7 0.0 collective-permute-done.1.piece_ref
  18.7 2.2 %collective-permute-done.whole_ref = bf16[256,1536]{1,0:T(8,128)(2,1)S(1)} collective-permute-done((bf16[256,1536]{1,0:T(8,128)(2,1)}, bf16[256,1536]{1,0:T(8,128)(2,1)S(1)}, u32[]{:S(2)}, u32[]{:S(2)}) %collective-permute-start) | collective-permute-done | bytes 786464 | tf_op jit(solution)/shard_map/ppermute | solution.py:483
  20.9 1.2 %cut.1.refs_0_ = bf16[32,5,32,128]{3,2,1,0:T(8,128)(2,1)} custom-call(bf16[256,1536]{1,0:T(8,128)(2,1)S(1)} %collective-permute-done.whole_ref, bf16[32,2,32,128]{3,2,1,0:T(8,128)(2,1)S(1)} %collective-permute-done.1.piece_ref), custom_call_target="tpu_custom_call" | custom-call | flops 99999997952 | bytes 2097152 | tf_op jit(solution)/shard_map/cut/pallas_call | solution.py:410
  22.1 10.9 %all-to-all-done.refs_1_.first_hbm = bf16[32,4,32,128]{3,2,1,0:T(8,128)(2,1)S(1)} async-done(((bf16[32,4,32,128]{3,2,1,0:T(8,128)(2,1)}), bf16[32,4,32,128]{3,2,1,0:T(8,128)(2,1)S(1)}, u32[]{:S(2)}, u32[]{:S(2)}) %all-to-all-start) | async-done | bytes 1048608 | tf_op jit(solution)/shard_map/all_to_all | solution.py:477
  33.0 0.0 copy-start
  33.0 4.1 %all-to-all-start.1 = ((bf16[32,5,32,128]{3,2,1,0:T(8,128)(2,1)}), bf16[32,5,32,128]{3,2,1,0:T(8,128)(2,1)S(1)}, u32[]{:S(2)}, u32[]{:S(2)}) async-start(bf16[32,5,32,128]{3,2,1,0:T(8,128)(2,1)} %gate.2), calls=%async_computation.1 | async-start | bytes 2621440 | tf_op jit(solution)/shard_map/all_to_all | solution.py:477
  37.1 4.8 %collective-permute-start.2 = (bf16[32,4,32,128]{3,2,1,0:T(8,128)(2,1)S(1)}, bf16[32,4,32,128]{3,2,1,0:T(8,128)(2,1)}, u32[]{:S(2)}, u32[]{:S(2)}) collective-permute-start(bf16[32,4,32,128]{3,2,1,0:T(8,128)(2,1)S(1)} %all-to-all-done.refs_1_.first_hbm), channel_id=1, source_target_pairs={{0,32},{32,64},{64,96},{96,128},{128,160},{160,192},{192,224},{224... | collective-permute-start | bytes 3145736 | tf_op jit(solution)/shard_map/ppermute | solution.py:480
  41.9 0.0 copy-done
  41.9 0.0 copy-start.1
  41.9 1.0 copy-done.1
  42.9 1.3 %cut_out.1.refs_0_ = bf16[32,5,32,128]{3,2,1,0:T(8,128)(2,1)} custom-call(bf16[256,1536]{1,0:T(8,128)(2,1)S(1)} %copy-done, bf16[32,2,32,128]{3,2,1,0:T(8,128)(2,1)S(1)} %copy-done.1), custom_call_target="tpu_custom_call" | custom-call | flops 1000000 | bytes 2097152 | tf_op jit(solution)/shard_map/cut_out/pallas_call | solution.py:430
  44.2 12.7 %all-to-all-done.1.refs_1_.q_ref.kv_ref.second_ref = bf16[32,5,32,128]{3,2,1,0:T(8,128)(2,1)S(1)} async-done(((bf16[32,5,32,128]{3,2,1,0:T(8,128)(2,1)}), bf16[32,5,32,128]{3,2,1,0:T(8,128)(2,1)S(1)}, u32[]{:S(2)}, u32[]{:S(2)}) %all-to-all-start.1) | async-done | bytes 1310752 | tf_op jit(solution)/shard_map/all_to_all | solution.py:477
  56.9 4.7 %all-to-all-start.2 = ((bf16[32,5,32,128]{3,2,1,0:T(8,128)(2,1)}), bf16[32,5,32,128]{3,2,1,0:T(8,128)(2,1)}, u32[]{:S(2)}, u32[]{:S(2)}) async-start(bf16[32,5,32,128]{3,2,1,0:T(8,128)(2,1)} %gate.3), calls=%async_computation.2 | async-start | bytes 2621440 | tf_op jit(solution)/shard_map/all_to_all | solution.py:477
  61.6 2.1 %ahead.2.rest_0_ = bf16[1,1056,128]{2,1,0:T(8,128)(2,1)S(1)} custom-call(s32[4]{0:T(128)S(1)} %flags.1.refs_2_.flags_ref, bf16[32,5,32,128]{3,2,1,0:T(8,128)(2,1)S(1)} %all-to-all-done.1.refs_1_.q_ref.kv_ref.second_ref, bf16[32,5,32,128]{3,2,1,0:T(8,128)(2,1)S(1)} %all-to-all-done.1.refs_1_.q_ref.kv_ref.second_ref), custom_call_target="tpu_custom_call" | custom-call | flops 536870912 | bytes 1048576 | tf_op jit(solution)/shard_map/ahead/pallas_call | solution.py:271
  63.7 4.8 %collective-permute-start.3 = (bf16[1,1056,128]{2,1,0:T(8,128)(2,1)S(1)}, bf16[1,1056,128]{2,1,0:T(8,128)(2,1)S(1)}, u32[]{:S(2)}, u32[]{:S(2)}) collective-permute-start(bf16[1,1056,128]{2,1,0:T(8,128)(2,1)S(1)} %ahead.2.rest_0_), channel_id=1, source_target_pairs={{0,32},{32,64},{64,96},{96,128},{128,160},{160,192},{192,224},{224... | collective-permute-start | bytes 811016 | tf_op jit(solution)/shard_map/ppermute | solution.py:480
  68.5 0.0 collective-permute-done.2.up_hbm.kv_ref
  68.5 5.2 %ahead.3 = bf16[2,1056,128]{2,1,0:T(8,128)(2,1)} custom-call(s32[4]{0:T(128)S(1)} %flags.1.refs_2_.flags_ref, bf16[32,5,32,128]{3,2,1,0:T(8,128)(2,1)S(1)} %all-to-all-done.1.refs_1_.q_ref.kv_ref.second_ref, bf16[32,4,32,128]{3,2,1,0:T(8,128)(2,1)} %collective-permute-done.2.up_hbm.kv_ref, bf16[1,1056,128]{2,1,0:T(8,128)(2,1)S(1)} %ahead.2.rest_0_), custom_call_target="tpu_custom_call" | custom-call | flops 4294967296 | bytes 2097152 | tf_op jit(solution)/shard_map/ahead/pallas_call | solution.py:271
  73.7 3.5 %collective-permute-start.4 = (bf16[2,1056,128]{2,1,0:T(8,128)(2,1)}, bf16[2,1056,128]{2,1,0:T(8,128)(2,1)}, u32[]{:S(2)}, u32[]{:S(2)}) collective-permute-start(bf16[2,1056,128]{2,1,0:T(8,128)(2,1)} %ahead.3), channel_id=1, source_target_pairs={{0,32},{32,64},{64,96},{96,128},{128,160},{160,192},{192,224},{224... | collective-permute-start | bytes 1622024 | tf_op jit(solution)/shard_map/ppermute | solution.py:480
  77.3 0.0 collective-permute-done.3.far_ref
  77.3 4.2 %all-to-all-done.2.third_ref = bf16[32,5,32,128]{3,2,1,0:T(8,128)(2,1)} async-done(((bf16[32,5,32,128]{3,2,1,0:T(8,128)(2,1)}), bf16[32,5,32,128]{3,2,1,0:T(8,128)(2,1)}, u32[]{:S(2)}, u32[]{:S(2)}) %all-to-all-start.2) | async-done | bytes 1310752 | tf_op jit(solution)/shard_map/all_to_all | solution.py:477
  81.5 6.3 %near.1 = (f32[2,1024,128]{2,1,0:T(8,128)S(1)}, f32[2,8,128]{2,1,0:T(8,128)S(1)}, bf16[32,1,32,128]{3,2,1,0:T(8,128)(2,1)S(1)}) custom-call(s32[4]{0:T(128)S(1)} %flags.1.refs_2_.flags_ref, bf16[32,5,32,128]{3,2,1,0:T(8,128)(2,1)} %all-to-all-done.2.third_ref, bf16[32,5,32,128]{3,2,1,0:T(8,128)(2,1)S(1)} %all-to-all-done.1.refs_1_.q_ref.kv_ref.second_ref, ...), custom_call_target="tpu_custom_call" | custom-call | flops 171798691840 | bytes 3670016 | tf_op jit(solution)/shard_map/near/pallas_call | solution.py:285
  87.8 1.2 %collective-permute-done.4.far_ref = bf16[2,1056,128]{2,1,0:T(8,128)(2,1)} collective-permute-done((bf16[2,1056,128]{2,1,0:T(8,128)(2,1)}, bf16[2,1056,128]{2,1,0:T(8,128)(2,1)}, u32[]{:S(2)}, u32[]{:S(2)}) %collective-permute-start.4) | collective-permute-done | bytes 540704 | tf_op jit(solution)/shard_map/ppermute | solution.py:480
  89.0 1.5 %merge.1 = bf16[32,3,32,128]{3,2,1,0:T(8,128)(2,1)S(1)} custom-call(s32[4]{0:T(128)S(1)} %flags.1.refs_2_.flags_ref, f32[2,1024,128]{2,1,0:T(8,128)S(1)} %get-tuple-element.12.near_ref, f32[2,8,128]{2,1,0:T(8,128)S(1)} %get-tuple-element.13.log_ref, bf16[2,1056,128]{2,1,0:T(8,128)(2,1)} %collective-permute-done.4.far_ref, ...), custom_call_target="tpu_custom_call" | custom-call | bytes 2097152 | tf_op jit(solution)/shard_map/merge/pallas_call | solution.py:310
  90.6 22.5 %all_to_all.20.in_ref = bf16[32,3,32,128]{3,2,1,0:T(8,128)(2,1)S(1)} all-to-all(bf16[32,3,32,128]{3,2,1,0:T(8,128)(2,1)S(1)} %merge.1), channel_id=1, replica_groups=mesh['grp'=16,'ctx'=32] {'ctx'}, dimensions={0} | all-to-all | bytes 1572864 | tf_op jit(solution)/shard_map/all_to_all | solution.py:477
  113.1 1.0 paste.1
  (2 shorter events, 0.0 us)
Async XLA Ops:
  0.0 20.9 %collective-permute-start = (bf16[256,1536]{1,0:T(8,128)(2,1)}, bf16[256,1536]{1,0:T(8,128)(2,1)S(1)}, u32[]{:S(2)}, u32[]{:S(2)}) collective-permute-start(bf16[256,1536]{1,0:T(8,128)(2,1)} %whole_ref.1), channel_id=1, source_target_pairs={{32,0},{64,32},{96,64},{128,96},{160,128},{192,160},{224,192},{256... | collective-permute-start | bytes 2359304 | tf_op jit(solution)/shard_map/ppermute | solution.py:483
  4.4 11.7 %copy-start.2 = (s32[16,8,2]{0,2,1:T(2,128)S(1)}, s32[16,8,2]{0,2,1:T(2,128)}, u32[]{:S(2)}) copy-start(s32[16,8,2]{0,2,1:T(2,128)} %param.8) | copy-start | bytes 3076
  4.4 11.9 %copy-start.3 = (s32[16,8]{0,1:T(8,128)S(1)}, s32[16,8]{0,1:T(8,128)}, u32[]{:S(2)}) copy-start(s32[16,8]{0,1:T(8,128)} %param.9) | copy-start | bytes 1540
  4.4 14.3 %collective-permute-start.1 = (bf16[32,2,32,128]{3,2,1,0:T(8,128)(2,1)}, bf16[32,2,32,128]{3,2,1,0:T(8,128)(2,1)S(1)}, u32[]{:S(2)}, u32[]{:S(2)}) collective-permute-start(bf16[32,2,32,128]{3,2,1,0:T(8,128)(2,1)} %get-tuple-element.10.piece_ref), channel_id=1, source_target_pairs={{0,32},{32,64},{64,96},{96,128},{128,160},{160,192},{192,224},{224... | collective-permute-start | bytes 1572872 | tf_op jit(solution)/shard_map/ppermute | solution.py:480
  7.9 25.1 %all-to-all-start = ((bf16[32,4,32,128]{3,2,1,0:T(8,128)(2,1)}), bf16[32,4,32,128]{3,2,1,0:T(8,128)(2,1)S(1)}, u32[]{:S(2)}, u32[]{:S(2)}) async-start(bf16[32,4,32,128]{3,2,1,0:T(8,128)(2,1)} %get-tuple-element.11), calls=%async_computation | async-start | bytes 2097152 | tf_op jit(solution)/shard_map/all_to_all | solution.py:477
  33.0 8.9 %copy-start = (bf16[256,1536]{1,0:T(8,128)(2,1)S(1)}, bf16[256,1536]{1,0:T(8,128)(2,1)}, u32[]{:S(2)}) copy-start(bf16[256,1536]{1,0:T(8,128)(2,1)} %whole_ref.1) | copy-start | bytes 2359300
  33.0 23.9 %all-to-all-start.1 = ((bf16[32,5,32,128]{3,2,1,0:T(8,128)(2,1)}), bf16[32,5,32,128]{3,2,1,0:T(8,128)(2,1)S(1)}, u32[]{:S(2)}, u32[]{:S(2)}) async-start(bf16[32,5,32,128]{3,2,1,0:T(8,128)(2,1)} %gate.2), calls=%async_computation.1 | async-start | bytes 2621440 | tf_op jit(solution)/shard_map/all_to_all | solution.py:477
  37.1 31.4 %collective-permute-start.2 = (bf16[32,4,32,128]{3,2,1,0:T(8,128)(2,1)S(1)}, bf16[32,4,32,128]{3,2,1,0:T(8,128)(2,1)}, u32[]{:S(2)}, u32[]{:S(2)}) collective-permute-start(bf16[32,4,32,128]{3,2,1,0:T(8,128)(2,1)S(1)} %all-to-all-done.refs_1_.first_hbm), channel_id=1, source_target_pairs={{0,32},{32,64},{64,96},{96,128},{128,160},{160,192},{192,224},{224... | collective-permute-start | bytes 3145736 | tf_op jit(solution)/shard_map/ppermute | solution.py:480
  41.9 1.0 copy-start.1
  56.9 24.6 %all-to-all-start.2 = ((bf16[32,5,32,128]{3,2,1,0:T(8,128)(2,1)}), bf16[32,5,32,128]{3,2,1,0:T(8,128)(2,1)}, u32[]{:S(2)}, u32[]{:S(2)}) async-start(bf16[32,5,32,128]{3,2,1,0:T(8,128)(2,1)} %gate.3), calls=%async_computation.2 | async-start | bytes 2621440 | tf_op jit(solution)/shard_map/all_to_all | solution.py:477
  63.7 13.6 %collective-permute-start.3 = (bf16[1,1056,128]{2,1,0:T(8,128)(2,1)S(1)}, bf16[1,1056,128]{2,1,0:T(8,128)(2,1)S(1)}, u32[]{:S(2)}, u32[]{:S(2)}) collective-permute-start(bf16[1,1056,128]{2,1,0:T(8,128)(2,1)S(1)} %ahead.2.rest_0_), channel_id=1, source_target_pairs={{0,32},{32,64},{64,96},{96,128},{128,160},{160,192},{192,224},{224... | collective-permute-start | bytes 811016 | tf_op jit(solution)/shard_map/ppermute | solution.py:480
  73.7 15.3 %collective-permute-start.4 = (bf16[2,1056,128]{2,1,0:T(8,128)(2,1)}, bf16[2,1056,128]{2,1,0:T(8,128)(2,1)}, u32[]{:S(2)}, u32[]{:S(2)}) collective-permute-start(bf16[2,1056,128]{2,1,0:T(8,128)(2,1)} %ahead.3), channel_id=1, source_target_pairs={{0,32},{32,64},{64,96},{96,128},{128,160},{160,192},{192,224},{224... | collective-permute-start | bytes 1622024 | tf_op jit(solution)/shard_map/ppermute | solution.py:480

commit v10 on v8

--- a/solution.py
+++ b/solution.py
@@ -15,6 +15,7 @@
 NWIN = 8
 LOOK = 2
 QB = 256
+AHEAD_QB = 512
 PARTS = HEADS // SPAN
 POSITIONS = POS // NWIN
 STAT_ROWS = 32
@@ -26,7 +27,7 @@
 ANY = pl.BlockSpec(memory_space=pl.ANY)
 HBM = pl.BlockSpec(memory_space=pltpu.HBM)
 SMALL = pltpu.CompilerParams(vmem_limit_bytes=2**20)
-PARAMS = pltpu.CompilerParams(vmem_limit_bytes=10 * 2**20)
+PARAMS = pltpu.CompilerParams(vmem_limit_bytes=16 * 2**20)
 
 
 def is_taken(groups_ref, count_ref, group, distance):
@@ -133,17 +134,17 @@
 
             def job(start):
                 return (
-                    lambda: score(rows_of(q_ref, query_slab + head, start, QB), keys),
+                    lambda: score(rows_of(q_ref, query_slab + head, start, AHEAD_QB), keys),
                     lambda scores: soften(scores, values),
                 )
 
             logs = []
 
             def done(at, part):
-                out_ref[head, pl.ds(at * QB, QB), :] = (part[2] / part[1]).astype(jnp.bfloat16)
+                out_ref[head, pl.ds(at * AHEAD_QB, AHEAD_QB), :] = (part[2] / part[1]).astype(jnp.bfloat16)
                 logs.extend(log_rows(part))
 
-            in_turn([job(start) for start in range(0, rows, QB)], done)
+            in_turn([job(start) for start in range(0, rows, AHEAD_QB)], done)
             left = jnp.concatenate(logs, axis=0)
             pieces = []
             for _ in range(3):

time: 115 us -> 115 us (level)
  the two profiles are of different devices: /device:TPU:225 before, /device:TPU:65 now
where the time goes in v10:
time: 115 us; the launch traced here: 114 us
  waiting for transfers between devices  33.5 us (29%)
  starting transfers between devices  32.2 us (28%)
  blocking collectives  24.3 us (21%)
  Pallas kernels  22.9 us (20%)
  local copies, waits for them, and re-layouts  1.26 us (1%)
    all_to_all x3, waiting for transfers between devices, to_peers(): return lax.all_to_all(block, 'ctx', split_axis=0, concat_axis=0, tiled=True)  31 us
    all_to_all x1, blocking collectives, to_peers(): return lax.all_to_all(block, 'ctx', split_axis=0, concat_axis=0, tiled=True)  24.3 us
    all_to_all x3, starting transfers between devices, to_peers(): return lax.all_to_all(block, 'ctx', split_axis=0, concat_axis=0, tiled=True)  16.9 us
    ppermute x4, starting transfers between devices, up(): lax.ppermute(block, 'grp', [(at, at + 1) for at in range(group_devices -...  13.4 us
    pallas_call x2, Pallas kernels, attend_ahead(): pl.pallas_call(functools.partial(ahead_kernel, query_slab, pair_slab), in...  7.38 us
    pallas_call x1, Pallas kernels, attend_near(): pl.pallas_call(near_kernel, in_specs=[SMEM] + [VMEM] * 2 + [ANY] * 2 + [V...  5.71 us
    pallas_call x1, Pallas kernels, cut_first(): pl.pallas_call(cut_first_kernel, in_specs=[HBM] * 2, out_specs=[HBM] * 2,...  2.44 us
    pallas_call x1, Pallas kernels, make_flags(): pl.pallas_call(flags_kernel, in_specs=[SMEM] * 2, out_specs=SMEM, out_sha...  2.37 us
  transfers between devices with their start and end apart: 8, of which 5 were waited for; matrix products, arithmetic and copies ran while one was open for 0% of the time, Pallas kernels for 18%

profile of v10, /device:TPU:65, one launch (start us, length us, event | category | flops | bytes accessed | tf_op | source)
XLA Modules:
  0.0 114.4 jit_solution(14882901437658371777)
XLA Ops:
  0.0 1.9 %collective-permute-start = (bf16[256,1536]{1,0:T(8,128)(2,1)}, bf16[256,1536]{1,0:T(8,128)(2,1)S(1)}, u32[]{:S(2)}, u32[]{:S(2)}) collective-permute-start(bf16[256,1536]{1,0:T(8,128)(2,1)} %whole_ref.1), channel_id=1, source_target_pairs={{32,0},{64,32},{96,64},{128,96},{160,128},{192,160},{224,192},{256... | collective-permute-start | bytes 2359304 | tf_op jit(solution)/shard_map/ppermute | solution.py:484
  1.9 2.4 %cut_first.1 = (bf16[32,4,32,128]{3,2,1,0:T(8,128)(2,1)}, bf16[32,2,32,128]{3,2,1,0:T(8,128)(2,1)}) custom-call(bf16[256,1536]{1,0:T(8,128)(2,1)} %k_ref.1, bf16[256,1536]{1,0:T(8,128)(2,1)} %v_ref.1), custom_call_target="tpu_custom_call" | custom-call | tf_op jit(solution)/shard_map/cut_first/pallas_call | solution.py:364
  4.4 0.0 copy-start.2
  4.4 0.0 copy-start.3
  4.4 3.5 %collective-permute-start.1 = (bf16[32,2,32,128]{3,2,1,0:T(8,128)(2,1)}, bf16[32,2,32,128]{3,2,1,0:T(8,128)(2,1)S(1)}, u32[]{:S(2)}, u32[]{:S(2)}) collective-permute-start(bf16[32,2,32,128]{3,2,1,0:T(8,128)(2,1)} %get-tuple-element.10.piece_ref), channel_id=1, source_target_pairs={{0,32},{32,64},{64,96},{96,128},{128,160},{160,192},{192,224},{224... | collective-permute-start | bytes 1572872 | tf_op jit(solution)/shard_map/ppermute | solution.py:481
  7.9 8.1 %all-to-all-start = ((bf16[32,4,32,128]{3,2,1,0:T(8,128)(2,1)}), bf16[32,4,32,128]{3,2,1,0:T(8,128)(2,1)S(1)}, u32[]{:S(2)}, u32[]{:S(2)}) async-start(bf16[32,4,32,128]{3,2,1,0:T(8,128)(2,1)} %get-tuple-element.11), calls=%async_computation | async-start | bytes 2097152 | tf_op jit(solution)/shard_map/all_to_all | solution.py:478
  16.1 0.0 copy-done.2
  16.1 0.1 copy.8.groups_ref
  16.2 0.0 copy-done.3
  16.2 0.1 copy.9.count_ref
  16.3 2.4 %flags.1.refs_2_.flags_ref = s32[4]{0:T(128)S(1)} custom-call(s32[16,8,2]{2,1,0:T(8,128)S(1)} %copy.8.groups_ref, s32[16,8]{1,0:T(8,128)S(1)} %copy.9.count_ref), custom_call_target="tpu_custom_call" | custom-call | tf_op jit(solution)/shard_map/flags/pallas_call | solution.py:53
  18.7 0.0 collective-permute-done.1.piece_ref
  18.7 2.2 %collective-permute-done.whole_ref = bf16[256,1536]{1,0:T(8,128)(2,1)S(1)} collective-permute-done((bf16[256,1536]{1,0:T(8,128)(2,1)}, bf16[256,1536]{1,0:T(8,128)(2,1)S(1)}, u32[]{:S(2)}, u32[]{:S(2)}) %collective-permute-start) | collective-permute-done | bytes 786464 | tf_op jit(solution)/shard_map/ppermute | solution.py:484
  20.9 1.2 %cut.1.refs_0_ = bf16[32,5,32,128]{3,2,1,0:T(8,128)(2,1)} custom-call(bf16[256,1536]{1,0:T(8,128)(2,1)S(1)} %collective-permute-done.whole_ref, bf16[32,2,32,128]{3,2,1,0:T(8,128)(2,1)S(1)} %collective-permute-done.1.piece_ref), custom_call_target="tpu_custom_call" | custom-call | flops 99999997952 | bytes 2097152 | tf_op jit(solution)/shard_map/cut/pallas_call | solution.py:411
  22.1 10.9 %all-to-all-done.refs_1_.first_hbm = bf16[32,4,32,128]{3,2,1,0:T(8,128)(2,1)S(1)} async-done(((bf16[32,4,32,128]{3,2,1,0:T(8,128)(2,1)}), bf16[32,4,32,128]{3,2,1,0:T(8,128)(2,1)S(1)}, u32[]{:S(2)}, u32[]{:S(2)}) %all-to-all-start) | async-done | bytes 1048608 | tf_op jit(solution)/shard_map/all_to_all | solution.py:478
  33.0 0.0 copy-start
  33.0 4.1 %all-to-all-start.1 = ((bf16[32,5,32,128]{3,2,1,0:T(8,128)(2,1)}), bf16[32,5,32,128]{3,2,1,0:T(8,128)(2,1)S(1)}, u32[]{:S(2)}, u32[]{:S(2)}) async-start(bf16[32,5,32,128]{3,2,1,0:T(8,128)(2,1)} %gate.2), calls=%async_computation.1 | async-start | bytes 2621440 | tf_op jit(solution)/shard_map/all_to_all | solution.py:478
  37.1 4.8 %collective-permute-start.2 = (bf16[32,4,32,128]{3,2,1,0:T(8,128)(2,1)S(1)}, bf16[32,4,32,128]{3,2,1,0:T(8,128)(2,1)}, u32[]{:S(2)}, u32[]{:S(2)}) collective-permute-start(bf16[32,4,32,128]{3,2,1,0:T(8,128)(2,1)S(1)} %all-to-all-done.refs_1_.first_hbm), channel_id=1, source_target_pairs={{0,32},{32,64},{64,96},{96,128},{128,160},{160,192},{192,224},{224... | collective-permute-start | bytes 3145736 | tf_op jit(solution)/shard_map/ppermute | solution.py:481
  41.9 0.0 copy-done
  41.9 0.0 copy-start.1
  41.9 1.0 copy-done.1
  42.9 1.3 %cut_out.1.refs_0_ = bf16[32,5,32,128]{3,2,1,0:T(8,128)(2,1)} custom-call(bf16[256,1536]{1,0:T(8,128)(2,1)S(1)} %copy-done, bf16[32,2,32,128]{3,2,1,0:T(8,128)(2,1)S(1)} %copy-done.1), custom_call_target="tpu_custom_call" | custom-call | flops 1000000 | bytes 2097152 | tf_op jit(solution)/shard_map/cut_out/pallas_call | solution.py:431
  44.2 12.7 %all-to-all-done.1.refs_1_.q_ref.kv_ref.second_ref = bf16[32,5,32,128]{3,2,1,0:T(8,128)(2,1)S(1)} async-done(((bf16[32,5,32,128]{3,2,1,0:T(8,128)(2,1)}), bf16[32,5,32,128]{3,2,1,0:T(8,128)(2,1)S(1)}, u32[]{:S(2)}, u32[]{:S(2)}) %all-to-all-start.1) | async-done | bytes 1310752 | tf_op jit(solution)/shard_map/all_to_all | solution.py:478
  56.9 4.7 %all-to-all-start.2 = ((bf16[32,5,32,128]{3,2,1,0:T(8,128)(2,1)}), bf16[32,5,32,128]{3,2,1,0:T(8,128)(2,1)}, u32[]{:S(2)}, u32[]{:S(2)}) async-start(bf16[32,5,32,128]{3,2,1,0:T(8,128)(2,1)} %gate.3), calls=%async_computation.2 | async-start | bytes 2621440 | tf_op jit(solution)/shard_map/all_to_all | solution.py:478
  61.6 2.1 %ahead.2.rest_0_ = bf16[1,1056,128]{2,1,0:T(8,128)(2,1)S(1)} custom-call(s32[4]{0:T(128)S(1)} %flags.1.refs_2_.flags_ref, bf16[32,5,32,128]{3,2,1,0:T(8,128)(2,1)S(1)} %all-to-all-done.1.refs_1_.q_ref.kv_ref.second_ref, bf16[32,5,32,128]{3,2,1,0:T(8,128)(2,1)S(1)} %all-to-all-done.1.refs_1_.q_ref.kv_ref.second_ref), custom_call_target="tpu_custom_call" | custom-call | flops 536870912 | bytes 1048576 | tf_op jit(solution)/shard_map/ahead/pallas_call | solution.py:272
  63.7 3.2 %collective-permute-start.3 = (bf16[1,1056,128]{2,1,0:T(8,128)(2,1)S(1)}, bf16[1,1056,128]{2,1,0:T(8,128)(2,1)S(1)}, u32[]{:S(2)}, u32[]{:S(2)}) collective-permute-start(bf16[1,1056,128]{2,1,0:T(8,128)(2,1)S(1)} %ahead.2.rest_0_), channel_id=1, source_target_pairs={{0,32},{32,64},{64,96},{96,128},{128,160},{160,192},{192,224},{224... | collective-permute-start | bytes 811016 | tf_op jit(solution)/shard_map/ppermute | solution.py:481
  66.9 0.0 collective-permute-done.2.up_hbm.kv_ref
  66.9 5.2 %ahead.3 = bf16[2,1056,128]{2,1,0:T(8,128)(2,1)} custom-call(s32[4]{0:T(128)S(1)} %flags.1.refs_2_.flags_ref, bf16[32,5,32,128]{3,2,1,0:T(8,128)(2,1)S(1)} %all-to-all-done.1.refs_1_.q_ref.kv_ref.second_ref, bf16[32,4,32,128]{3,2,1,0:T(8,128)(2,1)} %collective-permute-done.2.up_hbm.kv_ref, bf16[1,1056,128]{2,1,0:T(8,128)(2,1)S(1)} %ahead.2.rest_0_), custom_call_target="tpu_custom_call" | custom-call | flops 4294967296 | bytes 2097152 | tf_op jit(solution)/shard_map/ahead/pallas_call | solution.py:272
  72.1 1.9 %collective-permute-start.4 = (bf16[2,1056,128]{2,1,0:T(8,128)(2,1)}, bf16[2,1056,128]{2,1,0:T(8,128)(2,1)}, u32[]{:S(2)}, u32[]{:S(2)}) collective-permute-start(bf16[2,1056,128]{2,1,0:T(8,128)(2,1)} %ahead.3), channel_id=1, source_target_pairs={{0,32},{32,64},{64,96},{96,128},{128,160},{160,192},{192,224},{224... | collective-permute-start | bytes 1622024 | tf_op jit(solution)/shard_map/ppermute | solution.py:481
  74.1 0.0 collective-permute-done.3.far_ref
  74.1 7.4 %all-to-all-done.2.third_ref = bf16[32,5,32,128]{3,2,1,0:T(8,128)(2,1)} async-done(((bf16[32,5,32,128]{3,2,1,0:T(8,128)(2,1)}), bf16[32,5,32,128]{3,2,1,0:T(8,128)(2,1)}, u32[]{:S(2)}, u32[]{:S(2)}) %all-to-all-start.2) | async-done | bytes 1310752 | tf_op jit(solution)/shard_map/all_to_all | solution.py:478
  81.5 5.7 %near.1 = (f32[2,1024,128]{2,1,0:T(8,128)S(1)}, f32[2,8,128]{2,1,0:T(8,128)S(1)}, bf16[32,1,32,128]{3,2,1,0:T(8,128)(2,1)S(1)}) custom-call(s32[4]{0:T(128)S(1)} %flags.1.refs_2_.flags_ref, bf16[32,5,32,128]{3,2,1,0:T(8,128)(2,1)} %all-to-all-done.2.third_ref, bf16[32,5,32,128]{3,2,1,0:T(8,128)(2,1)S(1)} %all-to-all-done.1.refs_1_.q_ref.kv_ref.second_ref, ...), custom_call_target="tpu_custom_call" | custom-call | flops 171798691840 | bytes 3670016 | tf_op jit(solution)/shard_map/near/pallas_call | solution.py:286
  87.2 0.2 collective-permute-done.4.far_ref
  87.5 1.5 %merge.1 = bf16[32,3,32,128]{3,2,1,0:T(8,128)(2,1)S(1)} custom-call(s32[4]{0:T(128)S(1)} %flags.1.refs_2_.flags_ref, f32[2,1024,128]{2,1,0:T(8,128)S(1)} %get-tuple-element.12.near_ref, f32[2,8,128]{2,1,0:T(8,128)S(1)} %get-tuple-element.13.log_ref, bf16[2,1056,128]{2,1,0:T(8,128)(2,1)} %collective-permute-done.4.far_ref, ...), custom_call_target="tpu_custom_call" | custom-call | bytes 2097152 | tf_op jit(solution)/shard_map/merge/pallas_call | solution.py:311
  89.0 24.3 %all_to_all.20.in_ref = bf16[32,3,32,128]{3,2,1,0:T(8,128)(2,1)S(1)} all-to-all(bf16[32,3,32,128]{3,2,1,0:T(8,128)(2,1)S(1)} %merge.1), channel_id=1, replica_groups=mesh['grp'=16,'ctx'=32] {'ctx'}, dimensions={0} | all-to-all | bytes 1572864 | tf_op jit(solution)/shard_map/all_to_all | solution.py:478
  113.3 1.0 paste.1
  (2 shorter events, 0.0 us)
Async XLA Ops:
  0.0 20.9 %collective-permute-start = (bf16[256,1536]{1,0:T(8,128)(2,1)}, bf16[256,1536]{1,0:T(8,128)(2,1)S(1)}, u32[]{:S(2)}, u32[]{:S(2)}) collective-permute-start(bf16[256,1536]{1,0:T(8,128)(2,1)} %whole_ref.1), channel_id=1, source_target_pairs={{32,0},{64,32},{96,64},{128,96},{160,128},{192,160},{224,192},{256... | collective-permute-start | bytes 2359304 | tf_op jit(solution)/shard_map/ppermute | solution.py:484
  4.4 11.7 %copy-start.2 = (s32[16,8,2]{0,2,1:T(2,128)S(1)}, s32[16,8,2]{0,2,1:T(2,128)}, u32[]{:S(2)}) copy-start(s32[16,8,2]{0,2,1:T(2,128)} %param.8) | copy-start | bytes 3076
  4.4 11.9 %copy-start.3 = (s32[16,8]{0,1:T(8,128)S(1)}, s32[16,8]{0,1:T(8,128)}, u32[]{:S(2)}) copy-start(s32[16,8]{0,1:T(8,128)} %param.9) | copy-start | bytes 1540
  4.4 14.3 %collective-permute-start.1 = (bf16[32,2,32,128]{3,2,1,0:T(8,128)(2,1)}, bf16[32,2,32,128]{3,2,1,0:T(8,128)(2,1)S(1)}, u32[]{:S(2)}, u32[]{:S(2)}) collective-permute-start(bf16[32,2,32,128]{3,2,1,0:T(8,128)(2,1)} %get-tuple-element.10.piece_ref), channel_id=1, source_target_pairs={{0,32},{32,64},{64,96},{96,128},{128,160},{160,192},{192,224},{224... | collective-permute-start | bytes 1572872 | tf_op jit(solution)/shard_map/ppermute | solution.py:481
  7.9 25.1 %all-to-all-start = ((bf16[32,4,32,128]{3,2,1,0:T(8,128)(2,1)}), bf16[32,4,32,128]{3,2,1,0:T(8,128)(2,1)S(1)}, u32[]{:S(2)}, u32[]{:S(2)}) async-start(bf16[32,4,32,128]{3,2,1,0:T(8,128)(2,1)} %get-tuple-element.11), calls=%async_computation | async-start | bytes 2097152 | tf_op jit(solution)/shard_map/all_to_all | solution.py:478
  33.0 8.9 %copy-start = (bf16[256,1536]{1,0:T(8,128)(2,1)S(1)}, bf16[256,1536]{1,0:T(8,128)(2,1)}, u32[]{:S(2)}) copy-start(bf16[256,1536]{1,0:T(8,128)(2,1)} %whole_ref.1) | copy-start | bytes 2359300
  33.0 23.9 %all-to-all-start.1 = ((bf16[32,5,32,128]{3,2,1,0:T(8,128)(2,1)}), bf16[32,5,32,128]{3,2,1,0:T(8,128)(2,1)S(1)}, u32[]{:S(2)}, u32[]{:S(2)}) async-start(bf16[32,5,32,128]{3,2,1,0:T(8,128)(2,1)} %gate.2), calls=%async_computation.1 | async-start | bytes 2621440 | tf_op jit(solution)/shard_map/all_to_all | solution.py:478
  37.1 29.8 %collective-permute-start.2 = (bf16[32,4,32,128]{3,2,1,0:T(8,128)(2,1)S(1)}, bf16[32,4,32,128]{3,2,1,0:T(8,128)(2,1)}, u32[]{:S(2)}, u32[]{:S(2)}) collective-permute-start(bf16[32,4,32,128]{3,2,1,0:T(8,128)(2,1)S(1)} %all-to-all-done.refs_1_.first_hbm), channel_id=1, source_target_pairs={{0,32},{32,64},{64,96},{96,128},{128,160},{160,192},{192,224},{224... | collective-permute-start | bytes 3145736 | tf_op jit(solution)/shard_map/ppermute | solution.py:481
  41.9 1.0 copy-start.1
  56.9 24.6 %all-to-all-start.2 = ((bf16[32,5,32,128]{3,2,1,0:T(8,128)(2,1)}), bf16[32,5,32,128]{3,2,1,0:T(8,128)(2,1)}, u32[]{:S(2)}, u32[]{:S(2)}) async-start(bf16[32,5,32,128]{3,2,1,0:T(8,128)(2,1)} %gate.3), calls=%async_computation.2 | async-start | bytes 2621440 | tf_op jit(solution)/shard_map/all_to_all | solution.py:478
  63.7 10.3 %collective-permute-start.3 = (bf16[1,1056,128]{2,1,0:T(8,128)(2,1)S(1)}, bf16[1,1056,128]{2,1,0:T(8,128)(2,1)S(1)}, u32[]{:S(2)}, u32[]{:S(2)}) collective-permute-start(bf16[1,1056,128]{2,1,0:T(8,128)(2,1)S(1)} %ahead.2.rest_0_), channel_id=1, source_target_pairs={{0,32},{32,64},{64,96},{96,128},{128,160},{160,192},{192,224},{224... | collective-permute-start | bytes 811016 | tf_op jit(solution)/shard_map/ppermute | solution.py:481
  72.1 15.3 %collective-permute-start.4 = (bf16[2,1056,128]{2,1,0:T(8,128)(2,1)}, bf16[2,1056,128]{2,1,0:T(8,128)(2,1)}, u32[]{:S(2)}, u32[]{:S(2)}) collective-permute-start(bf16[2,1056,128]{2,1,0:T(8,128)(2,1)} %ahead.3), channel_id=1, source_target_pairs={{0,32},{32,64},{64,96},{96,128},{128,160},{160,192},{192,224},{224... | collective-permute-start | bytes 1622024 | tf_op jit(solution)/shard_map/ppermute | solution.py:481
